TPU v7x, 32 devices: a whole 2x2x4 slice. The times are simulated.
32 devices in a mesh: dp: 8 (over z, x), tensor: 4 (over y, core).
Axes of the slice: x: 2, y: 2, z: 4, core: 2. Of those that a mesh axis runs over, the one named last changes fastest.
Arguments:
- tokens: bfloat16 [16384, 1024], P(('dp', 'tensor')), may hold values from -6 to 6
- norm_gain: bfloat16 [1024], P('dp'), may hold values from 0.5 to 1.5
- query_weight: bfloat16 [1024, 512], P('dp', 'tensor'), may hold values from -0.1875 to 0.1875
- key_weight: bfloat16 [1024, 512], P('dp', 'tensor'), may hold values from -0.1875 to 0.1875
- value_weight: bfloat16 [1024, 1024], P('dp', 'tensor'), may hold values from -0.1875 to 0.1875
- gate_weight: bfloat16 [1024, 1024], P('dp', 'tensor'), may hold values from -0.1875 to 0.1875
- low_down: bfloat16 [1024, 16], P('dp'), may hold values from -0.1875 to 0.1875
- low_up: bfloat16 [4, 16, 128], P('tensor', None, 'dp'), may hold values from -1.5 to 1.5
- rank_bias: bfloat16 [4, 128], P('tensor', 'dp'), may hold values from -1 to 7
- head_gain: bfloat16 [256], P('dp'), may hold values from 0.5 to 1.5
- out_weight: bfloat16 [1024, 1024], P('tensor', 'dp'), may hold values from -0.375 to 0.375
- mlp_gain: bfloat16 [1024], P('dp'), may hold values from 0.5 to 1.5
- mlp_gate: bfloat16 [1024, 2816], P('dp', 'tensor'), may hold values from -0.1875 to 0.1875
- mlp_up: bfloat16 [1024, 2816], P('dp', 'tensor'), may hold values from -0.1875 to 0.1875
- mlp_down: bfloat16 [2816, 1024], P('tensor', 'dp'), may hold values from -0.15625 to 0.15625
- cotangent: bfloat16 [16384, 1024], P(('dp', 'tensor')), may hold values from -6 to 6
Outputs:
- block_out: bfloat16 [16384, 1024], P(('dp', 'tensor'))
- grad_tokens: float32 [16384, 1024], P(('dp', 'tensor'))
- grad_norm_gain: float32 [1024], P(('dp', 'tensor'))
- grad_query: float32 [1024, 512], P('dp', 'tensor')
- grad_key: float32 [1024, 512], P('dp', 'tensor')
- grad_value: float32 [1024, 1024], P('dp', 'tensor')
- grad_gate: float32 [1024, 1024], P('dp', 'tensor')
- grad_low_down: float32 [1024, 16], P(('dp', 'tensor'))
- grad_low_up: float32 [4, 16, 128], P('tensor', None, 'dp')
- grad_rank_bias: float32 [4, 128], P('tensor', 'dp')
- grad_head_gain: float32 [256], P(('dp', 'tensor'))
- grad_out_weight: float32 [1024, 1024], P('tensor', 'dp')
- grad_mlp_gain: float32 [1024], P(('dp', 'tensor'))
- grad_mlp_gate: float32 [1024, 2816], P('dp', 'tensor')
- grad_mlp_up: float32 [1024, 2816], P('dp', 'tensor')
- grad_mlp_down: float32 [2816, 1024], P('tensor', 'dp')
All inputs are finite; a program needn't handle non-finite values.
Results may differ from a plain program's by a relative error of at most 0.024.
Values may be sent and summed in bfloat16 or wider, within the bound.
No kernel may reach another device: no remote copies, remote signals or barrier semaphores. Data moves between devices by JAX's collectives and lax.ppermute only.
A program may use at most 192 MiB of HBM per device.

v0:
```python
import jax
import jax.numpy as jnp
from jax import lax
from jax.sharding import PartitionSpec as P

HEAD_K = 128
HEAD_V = 256
BLOCK = 64


TOP_PRECISION = lax.Precision.HIGHEST
NORM_EPS = 1e-06
HEAD_EPS = 1e-05
NORMALIZER = 16.0


def split_up(array, dim, length):
    dims = array.shape
    tiles = array.reshape(*dims[:dim], length, dims[dim] // length, *dims[dim + 1 :])
    return jnp.moveaxis(tiles, dim, 0)


def summed_on_arrival(array, axis, dim):
    tiles = split_up(array, dim, lax.axis_size(axis))
    arrived = lax.all_to_all(tiles, axis, split_axis=0, concat_axis=0, tiled=True)
    return arrived.astype(jnp.float32).sum(axis=0)


def side_by_side(arrays, axis, dim, along):
    widths = [a.shape[along] for a in arrays]
    both = jnp.concatenate(arrays, axis=along)
    result = summed_on_arrival(both, axis, dim)
    return tuple(jnp.split(result, [sum(widths[:k]) for k in range(1, len(widths))], axis=along))


def contract_rows(former, latter):
    return lax.dot_general(
        former, latter, (((0,), (0,)), ((), ())), preferred_element_type=jnp.float32
    )


def contract_last(former, latter):
    return lax.dot_general(
        former, latter, (((1,), (1,)), ((), ())), preferred_element_type=jnp.float32
    )


def project(former, latter):
    return jnp.dot(former, latter, preferred_element_type=jnp.float32)


def block_step(running_memory, block_data):
    query_block, key_block, value_tile_block, decay_block = block_data
    positions = query_block.shape[0]
    row_index = lax.broadcasted_iota(jnp.int32, (positions, positions), 0)
    col_index = lax.broadcasted_iota(jnp.int32, (positions, positions), 1)
    triangle = (row_index >= col_index).astype(jnp.float32)
    cumulative = jnp.einsum("ij,jhk->ihk", triangle, decay_block, precision=TOP_PRECISION)
    closing = cumulative[-1]
    query_decay = query_block * jnp.exp(cumulative)
    key_dec = key_block * jnp.exp(-cumulative)
    key_stop_index = key_block * jnp.exp(closing[None] - cumulative)
    scores = jnp.einsum("ihk,jhk->hij", query_decay, key_dec, precision=TOP_PRECISION) * triangle
    final_result = jnp.einsum("hij,jhv->ihv", scores, value_tile_block, precision=TOP_PRECISION)
    final_result = final_result + jnp.einsum(
        "bqg,qgp->bqp", query_decay, running_memory, precision=TOP_PRECISION
    )
    running_memory = jnp.exp(closing)[:, :, None] * running_memory + jnp.einsum(
        "fid,fin->idn", key_stop_index, value_tile_block, precision=TOP_PRECISION
    )
    return (running_memory, final_result)


def mixer(queries, key_rows, values, gate_in, low_rank, up_rank, bias_rank, gain_head):
    length = queries.shape[0]
    head_count = up_rank.shape[0]
    logits = jnp.einsum("lr,hrk->lhk", low_rank, up_rank, precision=TOP_PRECISION) + bias_rank
    decays = jax.nn.log_sigmoid(logits) / NORMALIZER

    def blocked(source, columns):
        return source.reshape(length // BLOCK, BLOCK, head_count, columns)

    initial = jnp.zeros((head_count, HEAD_K, HEAD_V), jnp.float32)
    _, mixed_heads = lax.scan(
        jax.checkpoint(block_step),
        initial,
        (
            blocked(queries, HEAD_K),
            blocked(key_rows, HEAD_K),
            blocked(values, HEAD_V),
            blocked(decays, HEAD_K),
        ),
    )
    mixed_heads = mixed_heads.reshape(length, head_count, HEAD_V) * HEAD_K ** (-0.5)
    scaled = mixed_heads * lax.rsqrt(
        jnp.mean(mixed_heads * mixed_heads, axis=-1, keepdims=True) + HEAD_EPS
    )
    scaled = scaled * gain_head * jax.nn.silu(gate_in.reshape(length, head_count, HEAD_V))
    return scaled.reshape(length, head_count * HEAD_V)


def norm_back(grad_out, normal, scale, gain):
    scaled_grad = grad_out * gain
    return scale * (scaled_grad - normal * jnp.mean(scaled_grad * normal, axis=-1, keepdims=True))


def local(
    tokens,
    norm_gain,
    query_weight,
    key_weight,
    value_weight,
    gate_weight,
    low_down,
    low_up,
    rank_bias,
    head_gain,
    out_weight,
    mlp_gain,
    mlp_gate,
    mlp_up,
    mlp_down,
    cotangent,
):
    (
        gain_one,
        w_query,
        w_key,
        w_value,
        w_gate,
        w_down_rank,
        w_up_rank,
        bias_rank,
        gain_head,
        w_out,
        gain_two,
        w_mlp_gate,
        w_mlp_up,
        w_mlp_down,
    ) = (
        lax.all_gather(norm_gain, "dp", axis=0, tiled=True),
        lax.all_gather(query_weight, "dp", axis=0, tiled=True),
        lax.all_gather(key_weight, "dp", axis=0, tiled=True),
        lax.all_gather(value_weight, "dp", axis=0, tiled=True),
        lax.all_gather(gate_weight, "dp", axis=0, tiled=True),
        lax.all_gather(low_down, "dp", axis=0, tiled=True),
        lax.all_gather(low_up, "dp", axis=2, tiled=True),
        lax.all_gather(rank_bias, "dp", axis=1, tiled=True),
        lax.all_gather(head_gain, "dp", axis=0, tiled=True),
        lax.all_gather(out_weight, "dp", axis=1, tiled=True),
        lax.all_gather(mlp_gain, "dp", axis=0, tiled=True),
        lax.all_gather(mlp_gate, "dp", axis=0, tiled=True),
        lax.all_gather(mlp_up, "dp", axis=0, tiled=True),
        lax.all_gather(mlp_down, "dp", axis=1, tiled=True),
    )
    inputs = tokens.astype(jnp.float32)
    scale_one = lax.rsqrt(jnp.mean(inputs * inputs, axis=-1, keepdims=True) + NORM_EPS)
    normal_one = inputs * scale_one
    normed_rows = lax.all_gather(
        (normal_one * gain_one.astype(jnp.float32)).astype(jnp.bfloat16),
        "tensor",
        axis=0,
        tiled=True,
    )
    queries = project(normed_rows, w_query).astype(jnp.bfloat16)
    key_rows = project(normed_rows, w_key).astype(jnp.bfloat16)
    values = project(normed_rows, w_value).astype(jnp.bfloat16)
    gate_in = project(normed_rows, w_gate)
    low_rank = project(normed_rows, w_down_rank)
    gated_out, mixer_pull = jax.vjp(
        mixer,
        queries.astype(jnp.float32),
        key_rows.astype(jnp.float32),
        values.astype(jnp.float32),
        gate_in,
        low_rank,
        w_up_rank.astype(jnp.float32),
        bias_rank.astype(jnp.float32),
        gain_head.astype(jnp.float32),
    )
    gated_low = gated_out.astype(jnp.bfloat16)
    middle = inputs + lax.psum_scatter(
        project(gated_low, w_out).astype(jnp.bfloat16), "tensor", scatter_dimension=0, tiled=True
    ).astype(jnp.float32)
    scale_two = lax.rsqrt(jnp.mean(middle * middle, axis=-1, keepdims=True) + NORM_EPS)
    normal_two = middle * scale_two
    mlp_rows = lax.all_gather(
        (normal_two * gain_two.astype(jnp.float32)).astype(jnp.bfloat16),
        "tensor",
        axis=0,
        tiled=True,
    )
    gate_pre = project(mlp_rows, w_mlp_gate)
    up_pre = project(mlp_rows, w_mlp_up)
    sigmoid_gate = jax.nn.sigmoid(gate_pre)
    hidden = (gate_pre * sigmoid_gate * up_pre).astype(jnp.bfloat16)
    outputs = middle + lax.psum_scatter(
        project(hidden, w_mlp_down).astype(jnp.bfloat16), "tensor", scatter_dimension=0, tiled=True
    ).astype(jnp.float32)
    block_out = outputs.astype(jnp.bfloat16)
    (
        gain_one,
        w_query,
        w_key,
        w_value,
        w_gate,
        w_down_rank,
        w_out,
        gain_two,
        w_mlp_gate,
        w_mlp_up,
        w_mlp_down,
    ) = (
        lax.all_gather(norm_gain, "dp", axis=0, tiled=True),
        lax.all_gather(query_weight, "dp", axis=0, tiled=True),
        lax.all_gather(key_weight, "dp", axis=0, tiled=True),
        lax.all_gather(value_weight, "dp", axis=0, tiled=True),
        lax.all_gather(gate_weight, "dp", axis=0, tiled=True),
        lax.all_gather(low_down, "dp", axis=0, tiled=True),
        lax.all_gather(out_weight, "dp", axis=1, tiled=True),
        lax.all_gather(mlp_gain, "dp", axis=0, tiled=True),
        lax.all_gather(mlp_gate, "dp", axis=0, tiled=True),
        lax.all_gather(mlp_up, "dp", axis=0, tiled=True),
        lax.all_gather(mlp_down, "dp", axis=1, tiled=True),
    )
    cot_rows = lax.all_gather(cotangent, "tensor", axis=0, tiled=True)
    grad_hidden = contract_last(cot_rows, w_mlp_down)
    grad_mlp_down = contract_rows(hidden, cot_rows)
    grad_up_pre = (grad_hidden * gate_pre * sigmoid_gate).astype(jnp.bfloat16)
    grad_gate_pre = (
        grad_hidden * up_pre * sigmoid_gate * (1.0 + gate_pre * (1.0 - sigmoid_gate))
    ).astype(jnp.bfloat16)
    grad_mlp_gate = contract_rows(mlp_rows, grad_gate_pre)
    grad_mlp_up = contract_rows(mlp_rows, grad_up_pre)
    grad_second = lax.psum_scatter(
        (contract_last(grad_gate_pre, w_mlp_gate) + contract_last(grad_up_pre, w_mlp_up)).astype(
            jnp.bfloat16
        ),
        "tensor",
        scatter_dimension=0,
        tiled=True,
    ).astype(jnp.float32)
    grad_mlp_gate, grad_mlp_up, grad_mlp_down = (
        lax.psum_scatter(grad_mlp_gate, "dp", scatter_dimension=0, tiled=True),
        lax.psum_scatter(grad_mlp_up, "dp", scatter_dimension=0, tiled=True),
        lax.psum_scatter(grad_mlp_down, "dp", scatter_dimension=1, tiled=True),
    )
    grad_mlp_gain = jnp.sum(grad_second * normal_two, axis=0)
    grad_middle = cotangent.astype(jnp.float32) + norm_back(
        grad_second, normal_two, scale_two, gain_two.astype(jnp.float32)
    )
    mixer_cot = lax.all_gather(grad_middle.astype(jnp.bfloat16), "tensor", axis=0, tiled=True)
    grad_gated = contract_last(mixer_cot, w_out)
    grad_out_weight = contract_rows(gated_low, mixer_cot)
    (
        grad_queries,
        grad_keys,
        grad_values,
        grad_gate_in,
        grad_low_rank,
        grad_up_rank,
        grad_bias_rank,
        grad_gain_head,
    ) = mixer_pull(grad_gated)
    grad_queries = grad_queries.astype(jnp.bfloat16)
    grad_keys = grad_keys.astype(jnp.bfloat16)
    grad_values = grad_values.astype(jnp.bfloat16)
    grad_gate_in = grad_gate_in.astype(jnp.bfloat16)
    grad_low_rank = grad_low_rank.astype(jnp.bfloat16)
    grad_query = contract_rows(normed_rows, grad_queries)
    grad_key = contract_rows(normed_rows, grad_keys)
    grad_value = contract_rows(normed_rows, grad_values)
    grad_gate = contract_rows(normed_rows, grad_gate_in)
    grad_down_rank = contract_rows(normed_rows, grad_low_rank)

    def partial_term(grad_rows, weight):
        return contract_last(grad_rows, weight)

    total_term = partial_term(grad_queries, w_query) + partial_term(grad_keys, w_key)
    total_term = (
        total_term + partial_term(grad_values, w_value) + partial_term(grad_gate_in, w_gate)
    )
    grad_normed = lax.psum_scatter(
        (total_term + partial_term(grad_low_rank, w_down_rank)).astype(jnp.bfloat16),
        "tensor",
        scatter_dimension=0,
        tiled=True,
    ).astype(jnp.float32)
    grad_norm_gain = jnp.sum(grad_normed * normal_one, axis=0)
    grad_inputs = grad_middle + norm_back(
        grad_normed, normal_one, scale_one, gain_one.astype(jnp.float32)
    )
    grad_query, grad_key, grad_value, grad_gate, grad_up_rank, grad_bias_rank, grad_out_weight = (
        *side_by_side(
            (
                grad_query.astype(jnp.bfloat16),
                grad_key.astype(jnp.bfloat16),
                grad_value.astype(jnp.bfloat16),
                grad_gate.astype(jnp.bfloat16),
            ),
            "dp",
            0,
            1,
        ),
        summed_on_arrival(grad_up_rank.astype(jnp.bfloat16), "dp", 2),
        summed_on_arrival(grad_bias_rank.astype(jnp.bfloat16), "dp", 1),
        summed_on_arrival(grad_out_weight.astype(jnp.bfloat16), "dp", 1),
    )
    grad_norm_gain, grad_down_rank, grad_gain_head, grad_mlp_gain = (
        lax.psum_scatter(grad_norm_gain, ("dp", "tensor"), scatter_dimension=0, tiled=True),
        lax.psum_scatter(grad_down_rank, ("dp", "tensor"), scatter_dimension=0, tiled=True),
        lax.psum_scatter(grad_gain_head, ("dp", "tensor"), scatter_dimension=0, tiled=True),
        lax.psum_scatter(grad_mlp_gain, ("dp", "tensor"), scatter_dimension=0, tiled=True),
    )
    return (
        block_out,
        grad_inputs,
        grad_norm_gain,
        grad_query,
        grad_key,
        grad_value,
        grad_gate,
        grad_down_rank,
        grad_up_rank,
        grad_bias_rank,
        grad_gain_head,
        grad_out_weight,
        grad_mlp_gain,
        grad_mlp_gate,
        grad_mlp_up,
        grad_mlp_down,
    )


def solution(mesh):
    return jax.shard_map(
        local,
        mesh=mesh,
        in_specs=(
            P(("dp", "tensor"), None),
            P("dp"),
            P("dp", "tensor"),
            P("dp", "tensor"),
            P("dp", "tensor"),
            P("dp", "tensor"),
            P("dp", None),
            P("tensor", None, "dp"),
            P("tensor", "dp"),
            P("dp"),
            P("tensor", "dp"),
            P("dp"),
            P("dp", "tensor"),
            P("dp", "tensor"),
            P("tensor", "dp"),
            P(("dp", "tensor"), None),
        ),
        out_specs=(
            P(("dp", "tensor"), None),
            P(("dp", "tensor"), None),
            P(("dp", "tensor")),
            P("dp", "tensor"),
            P("dp", "tensor"),
            P("dp", "tensor"),
            P("dp", "tensor"),
            P(("dp", "tensor"), None),
            P("tensor", None, "dp"),
            P("tensor", "dp"),
            P(("dp", "tensor")),
            P("tensor", "dp"),
            P(("dp", "tensor")),
            P("dp", "tensor"),
            P("dp", "tensor"),
            P("tensor", "dp"),
        ),
        check_vma=False,
    )
```

profile of v0, /device:TPU:0, one launch (start us, length us, event | category | flops | bytes accessed | tf_op | source)
XLA Modules:
  0.0 1526.3 jit_solution(12973732531450991664)
XLA Ops:
  9.7 22.3 %all-gather = bf16[8,1,128]{2,1,0:T(2,128)(2,1)S(1)} all-gather(bf16[1,1,128]{2,1,0:T(2,128)(2,1)} %bitcast.580), channel_id=1, replica_groups=mesh['dp'=8,'tensor'=4] {'dp'}, dimensions={0}, use_global_device_ids=true | all-gather | bytes 2304 | tf_op jit(solution)/shard_map/all_gather | solution.py:141
  37.1 17.1 %all-reduce.7 = (bf16[128]{0:T(256)(128)(2,1)S(1)}, bf16[256]{0:T(256)(128)(2,1)S(1)}) all-reduce(bf16[128]{0:T(256)(128)(2,1)S(1)} %dynamic-update-slice, bf16[256]{0:T(256)(128)(2,1)S(1)} %dynamic-update-slice.1), channel_id=1, replica_groups=mesh['dp'=8,'tensor'=4] {'dp'}, use_global_device_ids=true, to_apply=%add.1 | all-reduce | flops 384 | bytes 1536
  54.4 30.5 %all_gather.68 = bf16[1,16,128]{1,0,2:T(2,128)(2,1)S(1)} all-gather(bf16[1,16,16]{1,0,2:T(2,128)(2,1)S(1)} %copy.65), channel_id=1, replica_groups=mesh['dp'=8,'tensor'=4] {'dp'}, dimensions={2}, use_global_device_ids=true | all-gather | bytes 4608 | tf_op jit(solution)/shard_map/all_gather | solution.py:147
  84.9 26.0 %all_gather.67 = bf16[1024,16]{0,1:T(8,128)(2,1)S(1)} all-gather(bf16[128,16]{0,1:T(8,128)(2,1)S(1)} %copy-done.53), channel_id=1, replica_groups=mesh['dp'=8,'tensor'=4] {'dp'}, dimensions={0}, use_global_device_ids=true | all-gather | bytes 36864 | tf_op jit(solution)/shard_map/all_gather | solution.py:146
  111.0 30.9 %all_gather.72 = bf16[1024,128]{1,0:T(8,128)(2,1)S(1)} all-gather(bf16[128,128]{1,0:T(8,128)(2,1)S(1)} %copy-done.43), channel_id=1, replica_groups=mesh['dp'=8,'tensor'=4] {'dp'}, dimensions={0}, use_global_device_ids=true | all-gather | bytes 294912 | tf_op jit(solution)/shard_map/all_gather | solution.py:142
  141.8 30.8 %all_gather.70 = bf16[1024,128]{1,0:T(8,128)(2,1)S(1)} all-gather(bf16[128,128]{1,0:T(8,128)(2,1)S(1)} %copy-done.44), channel_id=1, replica_groups=mesh['dp'=8,'tensor'=4] {'dp'}, dimensions={0}, use_global_device_ids=true | all-gather | bytes 294912 | tf_op jit(solution)/shard_map/all_gather | solution.py:143
  172.7 31.5 %all_gather.71 = bf16[1024,256]{1,0:T(8,128)(2,1)S(1)} all-gather(bf16[128,256]{1,0:T(8,128)(2,1)S(1)} %copy-done.40), channel_id=1, replica_groups=mesh['dp'=8,'tensor'=4] {'dp'}, dimensions={0}, use_global_device_ids=true | all-gather | bytes 589824 | tf_op jit(solution)/shard_map/all_gather | solution.py:144
  204.2 33.3 %all_gather.74 = bf16[1024,256]{1,0:T(8,128)(2,1)} all-gather(bf16[128,256]{1,0:T(8,128)(2,1)S(1)} %copy-done.41), channel_id=1, replica_groups=mesh['dp'=8,'tensor'=4] {'dp'}, dimensions={0}, use_global_device_ids=true | all-gather | bytes 589824 | tf_op jit(solution)/shard_map/all_gather | solution.py:145
  237.5 28.3 %all_gather.75 = bf16[256,1024]{1,0:T(8,128)(2,1)} all-gather(bf16[256,128]{1,0:T(8,128)(2,1)S(1)} %copy-done.42), channel_id=1, replica_groups=mesh['dp'=8,'tensor'=4] {'dp'}, dimensions={1}, use_global_device_ids=true | all-gather | bytes 589824 | tf_op jit(solution)/shard_map/all_gather | solution.py:150
  265.8 3.6 convolution_convert_fusion.3
  281.1 185.0 %while.40 = (s32[]{:T(128)}, f32[1,128,256]{2,1,0:T(8,128)S(1)}, f32[32,64,1,256]{3,1,2,0:T(8,128)S(1)}, f32[32,1,128,256]{3,2,1,0:T(8,128)}, f32[32,64,1,128]{3...) while((s32[]{:T(128)}, f32[1,128,256]{2,1,0:T(8,128)S(1)}, ...), condition=%wide.region_2.3_spmd.clone.clone, body=%wide.region_1.2_spmd.clone.sunk.clone | while | flops 75747328 | bytes 1545336 | solution.py:84
  467.4 5.2 multiply_convert_fusion.4
  476.5 16.5 %all-gather.1 = bf16[8,1,128]{2,1,0:T(2,128)(2,1)S(1)} all-gather(bf16[1,1,128]{2,1,0:T(2,128)(2,1)S(1)} %bitcast.581), channel_id=1, replica_groups=mesh['dp'=8,'tensor'=4] {'dp'}, dimensions={0}, use_global_device_ids=true | all-gather | bytes 2304 | tf_op jit(solution)/shard_map/all_gather | solution.py:151
  493.0 25.4 %reduce-scatter.11.cloned.1.call-done = bf16[512,1024]{1,0:T(8,128)(2,1)} async-done(((bf16[2048,1024]{1,0:T(8,128)(2,1)}), bf16[512,1024]{1,0:T(8,128)(2,1)}) %reduce-scatter.11.cloned.1.call-update) | async-done | bytes 1048592 | tf_op jit(solution)/shard_map/reduce_scatter | solution.py:182
  523.7 32.3 %all-gather.12.cloned.1.call-done = bf16[2048,1024]{1,0:T(8,128)(2,1)} async-done(((bf16[512,1024]{1,0:T(8,128)(2,1)}), bf16[2048,1024]{1,0:T(8,128)(2,1)}) %all-gather.12.cloned.1.call-update) | async-done | bytes 4194320 | tf_op jit(solution)/shard_map/all_gather | solution.py:187
  556.0 8.3 fusion.125
  564.3 37.0 %all-gather.14.cloned.1.call-done = bf16[1024,704]{0,1:T(8,128)(2,1)} async-done(((bf16[128,704]{0,1:T(8,128)(2,1)}), bf16[1024,704]{0,1:T(8,128)(2,1)}) %all-gather.14.cloned.1.call-update) | async-done | bytes 1441808 | tf_op jit(solution)/shard_map/all_gather | solution.py:152
  601.3 8.3 fusion.124
  609.6 35.3 %all-gather.18.cloned.1.call-done = bf16[704,1024]{1,0:T(8,128)(2,1)} async-done(((bf16[704,128]{1,0:T(8,128)(2,1)}), bf16[704,1024]{1,0:T(8,128)(2,1)}) %all-gather.18.cloned.1.call-update) | async-done | bytes 1441808 | tf_op jit(solution)/shard_map/all_gather | solution.py:154
  644.9 34.2 %all-gather.20.cloned.1.call-done = bf16[2048,1024]{1,0:T(8,128)(2,1)} async-done(((bf16[512,1024]{1,0:T(8,128)(2,1)}), bf16[2048,1024]{1,0:T(8,128)(2,1)}) %all-gather.20.cloned.1.call-update) | async-done | bytes 4194320 | tf_op jit(solution)/shard_map/all_gather | solution.py:226
  679.1 12.1 multiply_convert_fusion
  694.7 5.0 add_convert_fusion.1
  699.9 44.6 %reduce-scatter.15.cloned.1.call-done = bf16[512,1024]{1,0:T(8,128)(2,1)} async-done(((bf16[2048,1024]{1,0:T(8,128)(2,1)}), bf16[512,1024]{1,0:T(8,128)(2,1)}) %reduce-scatter.15.cloned.1.call-update) | async-done | bytes 1048592 | tf_op jit(solution)/shard_map/reduce_scatter | solution.py:235
  752.4 31.1 %all-gather.22.cloned.1.call-done = bf16[2048,1024]{1,0:T(8,128)(2,1)} async-done(((bf16[512,1024]{1,0:T(8,128)(2,1)}), bf16[2048,1024]{1,0:T(8,128)(2,1)}) %all-gather.22.cloned.1.call-update) | async-done | bytes 4194320 | tf_op jit(solution)/shard_map/all_gather | solution.py:252
  783.6 7.2 multiply_reduce_fusion.1
  793.0 264.2 %while.41 = (s32[]{:T(128)}, f32[1,128,256]{1,2,0:T(8,128)S(1)}, bf16[32,64,1,128]{3,1,2,0:T(8,128)(2,1)}, bf16[32,64,1,128]{3,1,2,0:T(8,128)(2,1)}, bf16[32,64,...) while((s32[]{:T(128)}, f32[1,128,256]{1,2,0:T(8,128)S(1)}, ...), condition=%wide.region_13.14_spmd.clone.clone, body=%wide.region_10.13_spmd.clone.sunk.clone | while | flops 157761536 | bytes 4054707 | solution.py:84
  1063.8 4.6 fusion.130
  1068.4 4.6 fusion.129
  1074.3 4.6 fusion.127
  1078.9 11.7 add_convert_fusion
  1091.9 6.9 convolution_convert_fusion
  1098.9 7.8 fusion.131
  1106.7 7.8 fusion.133
  1114.8 7.9 fusion.134
  1123.4 5.6 all-to-all-start.2
  1129.0 3.6 fusion.106
  1136.3 6.0 all-to-all-start.1
  1158.7 7.5 all-to-all-done.3
  1166.2 3.6 all-to-all-start
  1171.1 28.3 %reduce-scatter.25.cloned.1.call-done = f32[32,16]{1,0:T(8,128)} async-done(((f32[1024,16]{1,0:T(8,128)}), f32[32,16]{1,0:T(8,128)}) %reduce-scatter.25.cloned.1.call-update) | async-done | bytes 2064
  1201.5 4.6 all-to-all-done
  1214.4 28.0 %reduce-scatter.17.cloned.1.call-done = bf16[512,1024]{1,0:T(8,128)(2,1)} async-done(((bf16[2048,1024]{1,0:T(8,128)(2,1)}), bf16[512,1024]{1,0:T(8,128)(2,1)}) %reduce-scatter.17.cloned.1.call-update) | async-done | bytes 1048592 | tf_op jit(solution)/shard_map/reduce_scatter | solution.py:283
  1244.4 39.9 %all-reduce.6 = (f32[1024]{0:T(1024)S(1)}, f32[256]{0:T(256)S(1)}, f32[1024]{0:T(1024)S(1)}) all-reduce(f32[1024]{0:T(1024)S(1)} %get-tuple-element.494, f32[256]{0:T(256)} %get-tuple-element.490, f32[1024]{0:T(1024)} %get-tuple-element.492), channel_id=6, replica_groups=mesh['dp'=8,'tensor'=4] {'dp','tensor'}, use_global_device_ids=true, to_apply=%region_17.18.clone | all-reduce | flops 2304 | bytes 18432
  1286.1 3.9 reduce-scatter.13.cloned.1.call-done
  1290.0 4.2 fusion.88
  1294.2 72.7 %reduce-scatter.23.cloned.1.call-done = f32[704,128]{1,0:T(8,128)} async-done(((f32[704,1024]{1,0:T(8,128)}), f32[704,128]{1,0:T(8,128)}) %reduce-scatter.23.cloned.1.call-update) | async-done | bytes 360464 | tf_op jit(solution)/shard_map/reduce_scatter | solution.py:246
  1366.9 76.0 %reduce-scatter.19.cloned.1.call-done = f32[128,704]{0,1:T(8,128)} async-done(((f32[1024,704]{0,1:T(8,128)}), f32[128,704]{0,1:T(8,128)}) %reduce-scatter.19.cloned.1.call-update) | async-done | bytes 360464 | tf_op jit(solution)/shard_map/reduce_scatter | solution.py:244
  1442.9 76.0 %reduce-scatter.21.cloned.1.call-done = f32[128,704]{0,1:T(8,128)} async-done(((f32[1024,704]{0,1:T(8,128)}), f32[128,704]{0,1:T(8,128)}) %reduce-scatter.21.cloned.1.call-update) | async-done | bytes 360464 | tf_op jit(solution)/shard_map/reduce_scatter | solution.py:245
  (1234 shorter events, 531.4 us)
Async XLA Ops:
  8.0 257.8 %all-gather.10.cloned.1.call-start = ((), (), s32[]{:S(2)}) async-start(), calls=%async_computation.12 | async-start | bytes 5242880 | tf_op jit(solution)/shard_map/all_gather | solution.py:159
  8.1 26.7 %copy-start.62 = (u32[32]{0:T(128)S(1)}, u32[32]{0:T(128)}, u32[]{:S(2)}) copy-start(u32[32]{0:T(128)} %constant.121) | copy-start | bytes 388
  8.1 28.5 %copy-start.60 = (bf16[32]{0:T(256)(128)(2,1)S(1)}, bf16[32]{0:T(256)(128)(2,1)}, u32[]{:S(2)}) copy-start(bf16[32]{0:T(256)(128)(2,1)} %param.29) | copy-start | bytes 196
  8.1 28.8 %copy-start.61 = (bf16[1,16]{1,0:T(2,128)(2,1)S(1)}, bf16[1,16]{1,0:T(2,128)(2,1)}, u32[]{:S(2)}) copy-start(bf16[1,16]{1,0:T(2,128)(2,1)} %param.28) | copy-start | bytes 100
  8.1 46.2 %copy-start.52 = (bf16[1,16,16]{2,1,0:T(8,128)(2,1)S(1)}, bf16[1,16,16]{2,1,0:T(8,128)(2,1)}, u32[]{:S(2)}) copy-start(bf16[1,16,16]{2,1,0:T(8,128)(2,1)} %param.27) | copy-start | bytes 1540
  8.1 76.8 %copy-start.53 = (bf16[128,16]{0,1:T(8,128)(2,1)S(1)}, bf16[128,16]{0,1:T(8,128)(2,1)}, u32[]{:S(2)}) copy-start(bf16[128,16]{0,1:T(8,128)(2,1)} %param.26) | copy-start | bytes 12292
  8.1 102.8 %copy-start.43 = (bf16[128,128]{1,0:T(8,128)(2,1)S(1)}, bf16[128,128]{1,0:T(8,128)(2,1)}, u32[]{:S(2)}) copy-start(bf16[128,128]{1,0:T(8,128)(2,1)} %param.22) | copy-start | bytes 98308
  9.7 132.2 %copy-start.44 = (bf16[128,128]{1,0:T(8,128)(2,1)S(1)}, bf16[128,128]{1,0:T(8,128)(2,1)}, u32[]{:S(2)}) copy-start(bf16[128,128]{1,0:T(8,128)(2,1)} %param.23) | copy-start | bytes 98308
  9.7 163.0 %copy-start.40 = (bf16[128,256]{1,0:T(8,128)(2,1)S(1)}, bf16[128,256]{1,0:T(8,128)(2,1)}, u32[]{:S(2)}) copy-start(bf16[128,256]{1,0:T(8,128)(2,1)} %param.24) | copy-start | bytes 196612
  9.7 25.0 %copy-start.45 = (f32[512]{0:T(512)}, f32[512]{0:T(512)S(1)}, u32[]{:S(2)}) copy-start(f32[512]{0:T(512)S(1)} %add_rsqrt_fusion.1) | copy-start | bytes 6148
  32.0 172.2 %copy-start.41 = (bf16[128,256]{1,0:T(8,128)(2,1)S(1)}, bf16[128,256]{1,0:T(8,128)(2,1)}, u32[]{:S(2)}) copy-start(bf16[128,256]{1,0:T(8,128)(2,1)} %param.25) | copy-start | bytes 196612
  32.0 205.5 %copy-start.42 = (bf16[256,128]{1,0:T(8,128)(2,1)S(1)}, bf16[256,128]{1,0:T(8,128)(2,1)}, u32[]{:S(2)}) copy-start(bf16[256,128]{1,0:T(8,128)(2,1)} %param.30) | copy-start | bytes 196612
  34.6 483.8 %reduce-scatter.11.cloned.1.call-start = ((), (), s32[]{:S(2)}) async-start(), calls=%async_computation.13 | async-start | bytes 5242880 | tf_op jit(solution)/shard_map/reduce_scatter | solution.py:182
  54.3 413.1 %copy-start.54 = (f32[256]{0:T(256)}, f32[256]{0:T(256)S(1)}, u32[]{:S(2)}) copy-start(f32[256]{0:T(256)S(1)} %convert_element_type.175) | copy-start | bytes 3076
  84.9 193.4 %copy-start.49 = (bf16[1,16,128]{2,1,0:T(8,128)(2,1)}, bf16[1,16,128]{2,1,0:T(8,128)(2,1)S(1)}, u32[]{:S(2)}) copy-start(bf16[1,16,128]{2,1,0:T(8,128)(2,1)S(1)} %copy.66) | copy-start | bytes 12292
  110.9 166.2 %copy-start.36 = (bf16[1024,16]{0,1:T(8,128)(2,1)}, bf16[1024,16]{0,1:T(8,128)(2,1)S(1)}, u32[]{:S(2)}) copy-start(bf16[1024,16]{0,1:T(8,128)(2,1)S(1)} %all_gather.67) | copy-start | bytes 98308
  172.7 97.8 %copy-start.30 = (bf16[1024,128]{1,0:T(8,128)(2,1)}, bf16[1024,128]{1,0:T(8,128)(2,1)S(1)}, u32[]{:S(2)}) copy-start(bf16[1024,128]{1,0:T(8,128)(2,1)S(1)} %all_gather.70) | copy-start | bytes 786436
  204.2 68.7 %copy-start.24 = (bf16[1024,256]{1,0:T(8,128)(2,1)}, bf16[1024,256]{1,0:T(8,128)(2,1)S(1)}, u32[]{:S(2)}) copy-start(bf16[1024,256]{1,0:T(8,128)(2,1)S(1)} %all_gather.71) | copy-start | bytes 1572868
  475.8 42.6 %copy-start = (bf16[512,1024]{1,0:T(8,128)(2,1)S(1)}, bf16[512,1024]{1,0:T(8,128)(2,1)}, u32[]{:S(2)}) copy-start(bf16[512,1024]{1,0:T(8,128)(2,1)} %param.20) | copy-start | bytes 3145732
  475.9 47.8 %all-gather.16.cloned.1.call-start = ((), (), s32[]{:S(2)}) async-start(), calls=%async_computation.16 | async-start | bytes 1622016 | tf_op jit(solution)/shard_map/all_gather | solution.py:153
  476.5 79.6 %all-gather.12.cloned.1.call-start = ((), (), s32[]{:S(2)}) async-start(), calls=%async_computation.14 | async-start | bytes 5242880 | tf_op jit(solution)/shard_map/all_gather | solution.py:187
  521.6 79.7 %all-gather.14.cloned.1.call-start = ((), (), s32[]{:S(2)}) async-start(), calls=%async_computation.15 | async-start | bytes 1622016 | tf_op jit(solution)/shard_map/all_gather | solution.py:152
  522.2 122.7 %all-gather.18.cloned.1.call-start = ((), (), s32[]{:S(2)}) async-start(), calls=%async_computation.17 | async-start | bytes 1622016 | tf_op jit(solution)/shard_map/all_gather | solution.py:154
  522.9 156.2 %all-gather.20.cloned.1.call-start = ((), (), s32[]{:S(2)}) async-start(), calls=%async_computation.19 | async-start | bytes 5242880 | tf_op jit(solution)/shard_map/all_gather | solution.py:226
  523.6 220.8 %reduce-scatter.15.cloned.1.call-start = ((), (), s32[]{:S(2)}) async-start(), calls=%async_computation.20 | async-start | bytes 5242880 | tf_op jit(solution)/shard_map/reduce_scatter | solution.py:235
  679.1 12.1 copy-start.59
  699.8 47.5 %copy-start.7 = (bf16[512,1024]{1,0:T(8,128)(2,1)S(1)}, bf16[512,1024]{1,0:T(8,128)(2,1)}, u32[]{:S(2)}) copy-start(bf16[512,1024]{1,0:T(8,128)(2,1)} %param.35) | copy-start | bytes 3145732
  699.8 83.8 %all-gather.22.cloned.1.call-start = ((), (), s32[]{:S(2)}) async-start(), calls=%async_computation.21 | async-start | bytes 5242880 | tf_op jit(solution)/shard_map/all_gather | solution.py:252
  749.1 34.5 %copy-start.13 = (f32[32,64,1,256]{3,1,2,0:T(8,128)S(1)}, f32[32,64,1,256]{3,1,2,0:T(8,128)}, u32[]{:S(2)}) copy-start(f32[32,64,1,256]{3,1,2,0:T(8,128)} %copy-done.12) | copy-start | bytes 6291460
  749.1 450.2 %reduce-scatter.25.cloned.1.call-start = ((), (), s32[]{:S(2)}) async-start(), calls=%async_computation.26 | async-start | bytes 540672
  783.6 7.2 copy-start.23
  783.6 7.2 copy-start.47
  783.6 7.2 copy-start.55
  1063.6 178.8 %reduce-scatter.17.cloned.1.call-start = ((), (), s32[]{:S(2)}) async-start(), calls=%async_computation.22 | async-start | bytes 5242880 | tf_op jit(solution)/shard_map/reduce_scatter | solution.py:283
  1090.5 199.5 %reduce-scatter.13.cloned.1.call-start = ((), (), s32[]{:S(2)}) async-start(), calls=%async_computation.18 | async-start | bytes 5242880 | tf_op jit(solution)/shard_map/reduce_scatter | solution.py:197
  1098.8 268.1 %reduce-scatter.23.cloned.1.call-start = ((), (), s32[]{:S(2)}) async-start(), calls=%async_computation.25 | async-start | bytes 3244032 | tf_op jit(solution)/shard_map/reduce_scatter | solution.py:246
  1106.7 336.2 %reduce-scatter.19.cloned.1.call-start = ((), (), s32[]{:S(2)}) async-start(), calls=%async_computation.23 | async-start | bytes 3244032 | tf_op jit(solution)/shard_map/reduce_scatter | solution.py:244
  1114.5 404.4 %reduce-scatter.21.cloned.1.call-start = ((), (), s32[]{:S(2)}) async-start(), calls=%async_computation.24 | async-start | bytes 3244032 | tf_op jit(solution)/shard_map/reduce_scatter | solution.py:245
  1123.4 12.9 all-to-all-start.2
  1132.7 9.6 copy-start.16
  1136.3 12.4 all-to-all-start.1
  1145.3 6.9 copy-start.20
  1148.7 17.5 %all-to-all-start.3 = ((bf16[8,256,128]{2,1,0:T(8,128)(2,1)}), bf16[8,256,128]{2,1,0:T(8,128)(2,1)S(1)}, u32[]{:S(2)}, u32[]{:S(2)}) async-start(bf16[8,256,128]{2,1,0:T(8,128)(2,1)} %bitcast.358), calls=%async_computation.7 | async-start | bytes 1048576 | tf_op jit(solution)/shard_map/all_to_all | solution.py:25
  1166.2 39.8 %all-to-all-start = ((bf16[8,128,768]{1,2,0:T(8,128)(2,1)}), bf16[8,128,768]{1,2,0:T(8,128)(2,1)S(1)}, u32[]{:S(2)}, u32[]{:S(2)}) async-start(bf16[8,128,768]{1,2,0:T(8,128)(2,1)} %copy_bitcast_fusion.1), calls=%async_computation.4 | async-start | bytes 3145728 | tf_op jit(solution)/shard_map/all_to_all | solution.py:25
  1200.7 41.6 %copy-start.39 = (f32[8,1,128]{2,1,0:T(1,128)S(1)}, f32[8,1,128]{2,1,0:T(1,128)}, u32[]{:S(2)}) copy-start(f32[8,1,128]{2,1,0:T(1,128)} %copy-done.38) | copy-start | bytes 12292
  1200.7 41.6 %copy-start.46 = (f32[512]{0:T(512)S(1)}, f32[512]{0:T(512)}, u32[]{:S(2)}) copy-start(f32[512]{0:T(512)} %copy-done.45) | copy-start | bytes 6148
  1206.3 83.7 %copy-start.2 = (bf16[512,1024]{1,0:T(8,128)(2,1)S(1)}, bf16[512,1024]{1,0:T(8,128)(2,1)}, u32[]{:S(2)}) copy-start(bf16[512,1024]{1,0:T(8,128)(2,1)} %reduce-scatter.11.cloned.1.call-done) | copy-start | bytes 3145732
  1206.3 83.7 %copy-start.8 = (bf16[512,1024]{1,0:T(8,128)(2,1)S(1)}, bf16[512,1024]{1,0:T(8,128)(2,1)}, u32[]{:S(2)}) copy-start(bf16[512,1024]{1,0:T(8,128)(2,1)} %param.35) | copy-start | bytes 3145732
  (36 other events, 114.0 us)
Sparse Core Ops, SparseCore 0:
  34.7 31.8 all-gather.9
  476.0 42.3 reduce-scatter.10
  699.9 44.5 reduce-scatter.14
  1063.7 135.6 reduce-scatter.24
  1201.9 40.4 reduce-scatter.16
  1244.8 45.1 reduce-scatter.12
  1294.6 72.3 reduce-scatter.22
  1371.5 71.3 reduce-scatter.18
  1447.5 71.4 reduce-scatter.20
Sparse Core Ops, SparseCore 1:
  478.6 40.9 all-gather.15
  521.7 34.3 all-gather.11
  558.1 43.1 all-gather.13
  603.5 41.3 all-gather.17
  646.6 32.5 all-gather.19
  749.2 34.3 all-gather.21
where the time goes:
time: 1550 us; the launch traced here: 1530 us
  waiting for transfers between devices  542 us (35%)
  matrix products  347 us (22%)
  blocking collectives  307 us (20%)
  local copies, waits for them, and re-layouts  214 us (14%)
  other arithmetic  73.4 us (5%)
  starting transfers between devices  20.2 us (1%)
  between operations  17.6 us (1%)
    dynamic_slice x192, local copies, waits for them, and re-layouts, mixer(): lax.scan(jax.checkpoint(block_step), initial, (blocked(queries, HEAD_K),...  135 us
    reduce_scatter x1, waiting for transfers between devices, local(): lax.psum_scatter(grad_mlp_up, 'dp', scatter_dimension=0, tiled=True)  76 us
    reduce_scatter x1, waiting for transfers between devices, local(): lax.psum_scatter(grad_mlp_gate, 'dp', scatter_dimension=0, tiled=True)  76 us
    reduce_scatter x1, waiting for transfers between devices, local(): lax.psum_scatter(grad_mlp_down, 'dp', scatter_dimension=1, tiled=True)  72.7 us
    unnamed x2, blocking collectives  57 us
    dot_general x9, matrix products, contract_last(): lax.dot_general(former, latter, (((1,), (1,)), ((), ())), preferred_eleme...  54.4 us
    squeeze x64, local copies, waits for them, and re-layouts, mixer(): lax.scan(jax.checkpoint(block_step), initial, (blocked(queries, HEAD_K),...  54.2 us
    dot_general x96, matrix products, block_step(): jnp.einsum('fid,fin->idn', key_stop_index, value_tile_block, precision=TO...  52 us
  transfers between devices with their start and end apart: 19, of which 16 were waited for; matrix products, arithmetic and copies ran while one was open for 8% of the time, Pallas kernels for 0%

commit v1 on v0

v1 whole, which is shorter than its diff:
```python
import jax
import jax.numpy as jnp
from jax import lax
from jax.experimental import pallas as pl
from jax.experimental.pallas import tpu as pltpu
from jax.sharding import PartitionSpec as P

HEAD_K = 128
HEAD_V = 256
CHUNK = 128
FF_ROWS = 256
LANES = 128
SAFE_RANGE = 60.0

TOP_PRECISION = lax.Precision.HIGHEST
NORM_EPS = 1e-06
HEAD_EPS = 1e-05
NORMALIZER = 16.0
CORE = 1
PAIR = 2
BF = jnp.bfloat16
F32 = jnp.float32


def swap(array, axis, mask):
    size = lax.axis_size(axis)
    return lax.ppermute(array, axis, [(i, i ^ mask) for i in range(size)])


def radices(count):
    result = []
    while count > 1:
        radix = 4 if count % 4 == 0 else 2
        result.append(radix)
        count //= radix
    return result


def gather(part):
    span, held = 2, part
    for radix in radices(lax.axis_size("dp") // 2):
        held = jnp.concatenate([held] + [swap(held, "dp", d * span) for d in range(1, radix)], axis=0)
        span *= radix
    half = held.shape[0] // 2
    beside = swap(held, "dp", 1)
    pair = swap(held, "tensor", PAIR)
    pair_low = swap(pair[:half], "dp", 1)
    pair_high = swap(beside[half:], "tensor", PAIR)
    return (held, beside), (pair, pair_low, pair_high)


def scatter(own, pair):
    count = own.shape[0] // 2
    half = count // 2
    pair_low = swap(pair[count : count + half], "dp", 1)
    own_high = swap(pair[count + half :], "tensor", PAIR)
    total = own[:count].astype(F32)
    beside_low = swap(own[count : count + half], "dp", 1)
    pair_rest = swap(pair[half:count], "tensor", PAIR)
    beside_high = swap(
        (own[count + half :].astype(F32) + own_high.astype(F32)).astype(BF), "dp", 1
    )
    pair_sum = swap((pair[:half].astype(F32) + pair_low.astype(F32)).astype(BF), "tensor", PAIR)
    total = total + jnp.concatenate([beside_low, beside_high], axis=0).astype(F32)
    total = total + jnp.concatenate([pair_sum, pair_rest], axis=0).astype(F32)
    spans, span = [], 2
    for radix in radices(lax.axis_size("dp") // 2):
        spans.append((radix, span))
        span *= radix
    for radix, span in reversed(spans):
        rows = total.shape[0] // radix
        low = total.astype(BF)
        arrived = [swap(low[d * rows : (d + 1) * rows], "dp", d * span) for d in range(1, radix)]
        total = total[:rows] + sum(a.astype(F32) for a in arrived)
    return total


def place_matrix(width):
    count = lax.axis_size("dp")
    block = width // count
    feature = lax.broadcasted_iota(jnp.int32, (width, width), 0)
    place = lax.broadcasted_iota(jnp.int32, (width, width), 1)
    slot = place // block
    owner = (slot % (count // 2) * 2 + slot // (count // 2)) ^ lax.axis_index("dp")
    return (feature == owner * block + place % block).astype(BF)


def block_matrix():
    count = lax.axis_size("dp")
    owner = lax.broadcasted_iota(jnp.int32, (count, count), 0)
    slot = lax.broadcasted_iota(jnp.int32, (count, count), 1)
    return (owner == ((slot % (count // 2) * 2 + slot // (count // 2)) ^ lax.axis_index("dp"))).astype(F32)


def contract_rows(former, latter):
    return lax.dot_general(former, latter, (((0,), (0,)), ((), ())), preferred_element_type=F32)


def contract_last(former, latter):
    return lax.dot_general(former, latter, (((1,), (1,)), ((), ())), preferred_element_type=F32)


def project(former, latter):
    return jnp.dot(former, latter, preferred_element_type=F32)


def exact(former, latter):
    return jnp.dot(former, latter, preferred_element_type=F32, precision=TOP_PRECISION)


def positions():
    row = lax.broadcasted_iota(jnp.int32, (CHUNK, CHUNK), 0)
    col = lax.broadcasted_iota(jnp.int32, (CHUNK, CHUNK), 1)
    return row, col


def level_terms(cum, size):
    row, col = positions()
    boundary = row // (2 * size) * (2 * size) + size - 1
    at_boundary = exact((col == boundary).astype(F32), cum)
    fade = jnp.exp(-jnp.abs(cum - at_boundary))
    same = row // (2 * size) == col // (2 * size)
    mask = same & (row % (2 * size) >= size) & (col % (2 * size) < size)
    return fade, mask


def state_kernel(shift, k_own, v_own, k_pair, v_pair, low, up, bias, logits, cums, starts, end, memory):
    n = pl.program_id(0)

    @pl.when(n == 0)
    def _():
        memory[...] = jnp.zeros_like(memory)

    row, col = positions()
    triangle = (row >= col).astype(F32)
    for h, (k_ref, v_ref) in enumerate(((k_own, v_own), (k_pair, v_pair))):
        columns = slice(h * HEAD_K, (h + 1) * HEAD_K)
        logit = exact(low[...], up[h]) + bias[h]
        decay = (jnp.minimum(logit, 0.0) - jnp.log1p(jnp.exp(-jnp.abs(logit)))) / NORMALIZER
        cum = exact(triangle, decay)
        closing = cum[CHUNK - 1 :, :]
        logits[:, columns] = logit
        cums[:, columns] = cum
        starts[0, h] = memory[h]
        faded = (k_ref[...].astype(BF).astype(F32) * jnp.exp(closing - cum)).astype(BF)
        memory[h] = jnp.exp(closing) * memory[h] + contract_rows(v_ref[...].astype(BF), faded)

    @pl.when(n == pl.num_programs(0) - 1)
    def _():
        end[...] = memory[...]


def mix_kernel(
    shift, q_own, k_own, v_own, g_own, q_pair, k_pair, v_pair, g_pair, cums, starts, arrived, gain,
    gated_own, gated_pair, mixed_out, full, scores, passed,
):
    n = pl.program_id(0)

    @pl.when(n == 0)
    def _():
        passed[...] = jnp.zeros_like(passed)

    row, col = positions()
    heads = ((q_own, k_own, v_own, g_own, gated_own), (q_pair, k_pair, v_pair, g_pair, gated_pair))
    lowest = jnp.min(cums[CHUNK - 1 :, :])

    @pl.when(lowest > -SAFE_RANGE)
    def _():
        for h, (q_ref, k_ref, _, _, _) in enumerate(heads):
            cum = cums[:, h * HEAD_K : (h + 1) * HEAD_K]
            middle = cum[CHUNK // 2 : CHUNK // 2 + 1, :]
            q = q_ref[...].astype(BF).astype(F32)
            k = k_ref[...].astype(BF).astype(F32)
            both = contract_last((q * jnp.exp(cum - middle)).astype(BF), (k * jnp.exp(middle - cum)).astype(BF))
            scores[h] = jnp.where(row >= col, both, 0.0)

    @pl.when(lowest <= -SAFE_RANGE)
    def _():
        for h, (q_ref, k_ref, _, _, _) in enumerate(heads):
            cum = cums[:, h * HEAD_K : (h + 1) * HEAD_K]
            q = q_ref[...].astype(BF).astype(F32)
            k = k_ref[...].astype(BF).astype(F32)
            scores[h] = jnp.where(row == col, jnp.sum(q * k, axis=1, keepdims=True), 0.0)

            def level(step, carry):
                fade, mask = level_terms(cum, jnp.int32(1) << step)
                both = contract_last((q * fade).astype(BF), (k * fade).astype(BF))
                scores[h] = scores[h] + jnp.where(mask, both, 0.0)
                return carry

            lax.fori_loop(0, CHUNK.bit_length() - 1, level, 0)

    for h, (q_ref, _, v_ref, g_ref, out) in enumerate(heads):
        cum = cums[:, h * HEAD_K : (h + 1) * HEAD_K]
        state = (starts[0, h] + jnp.exp(passed[h]) * arrived[h]).astype(BF)
        full[0, h] = state
        passed[h] = passed[h] + cum[CHUNK - 1 :, :]
        q = q_ref[...].astype(BF).astype(F32)
        mixed = project(scores[h].astype(BF), v_ref[...].astype(BF))
        mixed = mixed + contract_last((q * jnp.exp(cum)).astype(BF), state)
        mixed = mixed * HEAD_K**-0.5
        mixed_out[:, h * HEAD_V : (h + 1) * HEAD_V] = mixed
        scale = lax.rsqrt(jnp.mean(mixed * mixed, axis=-1, keepdims=True) + HEAD_EPS)
        g = g_ref[...]
        out[...] = (mixed * scale * gain[...] * g * jax.nn.sigmoid(g)).astype(BF)


def gate_back_kernel(
    shift, q_own, g_own, d_own, q_pair, g_pair, d_pair, cums, mixed_in, gain,
    d_mixed, d_gate, ends, first, d_gain, memory,
):
    n = pl.program_id(0)

    @pl.when(n == 0)
    def _():
        memory[...] = jnp.zeros_like(memory)
        d_gain[...] = jnp.zeros_like(d_gain)

    for h, (q_ref, g_ref, d_ref) in enumerate(((q_own, g_own, d_own), (q_pair, g_pair, d_pair))):
        wide = slice(h * HEAD_V, (h + 1) * HEAD_V)
        cum = cums[:, h * HEAD_K : (h + 1) * HEAD_K]
        mixed = mixed_in[:, wide]
        scale = lax.rsqrt(jnp.mean(mixed * mixed, axis=-1, keepdims=True) + HEAD_EPS)
        normal = mixed * scale
        g, grad = g_ref[...], d_ref[...]
        sigmoid = jax.nn.sigmoid(g)
        silu = g * sigmoid
        d_gain[...] += jnp.sum(grad * normal * silu, axis=0, keepdims=True)
        scaled = grad * gain[...]
        d_gate[:, wide] = (scaled * normal * sigmoid * (1.0 + g * (1.0 - sigmoid))).astype(BF)
        scaled = scaled * silu
        back = scale * (scaled - normal * jnp.mean(scaled * normal, axis=-1, keepdims=True))
        back = (back * HEAD_K**-0.5).astype(BF)
        d_mixed[:, wide] = back
        ends[0, h] = memory[h]
        q = q_ref[...].astype(BF).astype(F32)
        faded = (q * jnp.exp(cum)).astype(BF)
        memory[h] = jnp.exp(cum[CHUNK - 1 :, :]) * memory[h] + contract_rows(back, faded)

    @pl.when(n == pl.num_programs(0) - 1)
    def _():
        first[...] = memory[...]


def mix_back_kernel(
    shift, q_own, k_own, v_own, low, q_pair, k_pair, v_pair, cums, logits, full, ends, arrived, up,
    d_mixed, d_gate, back_own, back_pair, d_up, d_bias, d_q, d_k, scores, grads, passed,
):
    n = pl.program_id(0)

    @pl.when(n == 0)
    def _():
        passed[...] = jnp.zeros_like(passed)
        d_up[...] = jnp.zeros_like(d_up)
        d_bias[...] = jnp.zeros_like(d_bias)

    row, col = positions()
    heads = ((q_own, k_own, v_own, back_own), (q_pair, k_pair, v_pair, back_pair))
    lowest = jnp.min(cums[CHUNK - 1 :, :])
    for h, (_, _, v_ref, _) in enumerate(heads):
        back = d_mixed[:, h * HEAD_V : (h + 1) * HEAD_V]
        grads[h] = contract_last(back, v_ref[...].astype(BF))

    @pl.when(lowest > -SAFE_RANGE)
    def _():
        for h, (q_ref, k_ref, _, _) in enumerate(heads):
            cum = cums[:, h * HEAD_K : (h + 1) * HEAD_K]
            middle = cum[CHUNK // 2 : CHUNK // 2 + 1, :]
            q = q_ref[...].astype(BF).astype(F32)
            k = k_ref[...].astype(BF).astype(F32)
            rise, fall = jnp.exp(cum - middle), jnp.exp(middle - cum)
            q_faded, k_faded = (q * rise).astype(BF), (k * fall).astype(BF)
            scores[h] = jnp.where(row >= col, contract_last(q_faded, k_faded), 0.0)
            strict = jnp.where(row > col, grads[h], 0.0).astype(BF)
            d_q[h] = project(strict, k_faded) * rise
            d_k[h] = contract_rows(strict, q_faded) * fall

    @pl.when(lowest <= -SAFE_RANGE)
    def _():
        for h, (q_ref, k_ref, _, _) in enumerate(heads):
            cum = cums[:, h * HEAD_K : (h + 1) * HEAD_K]
            q = q_ref[...].astype(BF).astype(F32)
            k = k_ref[...].astype(BF).astype(F32)
            scores[h] = jnp.where(row == col, jnp.sum(q * k, axis=1, keepdims=True), 0.0)
            d_q[h] = jnp.zeros((CHUNK, HEAD_K), F32)
            d_k[h] = jnp.zeros((CHUNK, HEAD_K), F32)

            def level(step, carry):
                fade, mask = level_terms(cum, jnp.int32(1) << step)
                q_faded, k_faded = (q * fade).astype(BF), (k * fade).astype(BF)
                scores[h] = scores[h] + jnp.where(mask, contract_last(q_faded, k_faded), 0.0)
                crossing = jnp.where(mask, grads[h], 0.0).astype(BF)
                d_q[h] = d_q[h] + project(crossing, k_faded) * fade
                d_k[h] = d_k[h] + contract_rows(crossing, q_faded) * fade
                return carry

            lax.fori_loop(0, CHUNK.bit_length() - 1, level, 0)

    later = (row <= col).astype(F32)
    d_low = jnp.zeros((CHUNK, LANES), F32)
    for h, (q_ref, k_ref, v_ref, out) in enumerate(heads):
        columns = slice(h * HEAD_K, (h + 1) * HEAD_K)
        wide = slice(h * HEAD_V, (h + 1) * HEAD_V)
        cum = cums[:, columns]
        closing = cum[CHUNK - 1 :, :]
        q = q_ref[...].astype(BF).astype(F32)
        k = k_ref[...].astype(BF).astype(F32)
        v, back, state = v_ref[...].astype(BF), d_mixed[:, wide], full[0, h]
        state_grad = ends[0, h] + jnp.exp(passed[h]) * arrived[h]
        passed[h] = passed[h] + closing
        low_grad = state_grad.astype(BF)
        fade = jnp.exp(closing - cum)
        q_strict = d_q[h] + project(back, state) * jnp.exp(cum)
        k_state = project(v, low_grad) * fade
        k_strict = d_k[h] + k_state
        diagonal = jnp.sum(jnp.where(row == col, grads[h], 0.0), axis=1, keepdims=True)
        d_v = contract_rows(scores[h].astype(BF), back) + contract_last((k * fade).astype(BF), low_grad)
        d_closing = jnp.sum(k * k_state, axis=0, keepdims=True) + jnp.exp(closing) * jnp.sum(
            state.astype(F32) * state_grad, axis=0, keepdims=True
        )
        d_decay = exact(later, q * q_strict - k * k_strict) + d_closing
        d_logit = d_decay * (jax.nn.sigmoid(-logits[:, columns]) / NORMALIZER)
        out[:, :HEAD_K] = (q_strict + diagonal * k).astype(BF)
        out[:, HEAD_K : 2 * HEAD_K] = (k_strict + diagonal * q).astype(BF)
        out[:, 2 * HEAD_K : 2 * HEAD_K + HEAD_V] = d_v.astype(BF)
        out[:, 2 * HEAD_K + HEAD_V : 2 * HEAD_K + 2 * HEAD_V] = d_gate[:, wide]
        low_logit = d_logit.astype(BF)
        d_low = d_low + contract_last(low_logit, up[h].astype(BF))
        d_up[h] = d_up[h] + contract_rows(low[...].astype(BF), low_logit)
        d_bias[h] = d_bias[h] + jnp.sum(d_logit, axis=0, keepdims=True)
    back_own[:, 2 * HEAD_K + 2 * HEAD_V :] = d_low.astype(BF)


def whole(shape):
    return pl.BlockSpec(shape, lambda n, shift: (0,) * len(shape))


def call(kernel, steps, ins, outs, scratch, flops, arrays, shift, backward=False):
    def at(n):
        return steps - 1 - n if backward else n

    def spec(entry):
        shape, kind, column = entry
        if kind == "r":
            return pl.BlockSpec(shape, lambda n, shift: ((at(n) + shift[0]) % steps, column))
        if kind == "t":
            return pl.BlockSpec(shape, lambda n, shift: (at(n),) + (0,) * (len(shape) - 1))
        return whole(shape)

    shapes = []
    for (shape, kind, _), dtype in outs:
        shapes.append(jax.ShapeDtypeStruct((shape[0] * (steps if kind != "w" else 1),) + shape[1:], dtype))
    return pl.pallas_call(
        kernel,
        grid_spec=pltpu.PrefetchScalarGridSpec(
            num_scalar_prefetch=1,
            grid=(steps,),
            in_specs=[spec(entry) for entry in ins],
            out_specs=[spec(entry) for entry, _ in outs],
            scratch_shapes=scratch,
        ),
        out_shape=shapes,
        compiler_params=pltpu.CompilerParams(vmem_limit_bytes=40 << 20),
        cost_estimate=pl.CostEstimate(flops=flops, bytes_accessed=12 << 20, transcendentals=0),
    )(shift, *arrays)


NARROW, WIDE = (CHUNK, HEAD_K), (CHUNK, HEAD_V)
STATES = (1, 2, HEAD_V, HEAD_K)
Q, K, V, G = (NARROW, "r", 0), (NARROW, "r", 1), (WIDE, "r", 1), (WIDE, "r", 2)
LOW = (NARROW, "r", (2 * HEAD_K + 2 * HEAD_V) // LANES)
CUMS = ((CHUNK, 2 * HEAD_K), "t", 0)
HEADS_WIDE = ((CHUNK, 2 * HEAD_V), "t", 0)
STATE = ((2, HEAD_V, HEAD_K), "w", 0)
SQUARES = pltpu.VMEM((2, CHUNK, CHUNK), F32)
MEMORY = pltpu.VMEM((2, HEAD_V, HEAD_K), F32)
PASSED = pltpu.VMEM((2, 1, HEAD_K), F32)
UP = ((2, LANES, HEAD_K), "w", 0)
BIAS = ((2, 1, HEAD_K), "w", 0)
GAIN = ((1, HEAD_V), "w", 0)
RISE = ((0, 2), (1, 3))
FALL = ((2, 0), (3, 1))


def mixer(own, pair, up, bias, gain, shift):
    steps = own.shape[0] // CHUNK
    logits, cums, starts, end = call(
        state_kernel,
        steps,
        [K, V, K, V, LOW, UP, BIAS],
        [(CUMS, F32), (CUMS, F32), ((STATES, "t", 0), F32), (STATE, F32)],
        [MEMORY],
        4 << 30,
        (own, own, pair, pair, own, up, bias),
        shift,
    )
    arrived = lax.ppermute(end[::-1], "tensor", RISE)
    gated_own, gated_pair, mixed, full = call(
        mix_kernel,
        steps,
        [Q, K, V, G, Q, K, V, G, CUMS, (STATES, "t", 0), STATE, GAIN],
        [((WIDE, "r", 0), BF), ((WIDE, "r", 0), BF), (HEADS_WIDE, F32), ((STATES, "t", 0), BF)],
        [SQUARES, PASSED],
        6 << 30,
        (own, own, own, own, pair, pair, pair, pair, cums, starts, arrived, gain),
        shift,
    )
    return gated_own, gated_pair, (logits, cums, mixed, full)


def mixer_back(own, pair, up, gain, shift, kept, d_own, d_pair):
    logits, cums, mixed, full = kept
    steps = own.shape[0] // CHUNK
    grad = (WIDE, "r", 0)
    d_mixed, d_gate, ends, first, d_gain = call(
        gate_back_kernel,
        steps,
        [Q, G, grad, Q, G, grad, CUMS, HEADS_WIDE, GAIN],
        [(HEADS_WIDE, BF), (HEADS_WIDE, BF), ((STATES, "t", 0), F32), (STATE, F32), (GAIN, F32)],
        [MEMORY],
        6 << 30,
        (own, own, d_own, pair, pair, d_pair, cums, mixed, gain),
        shift,
        backward=True,
    )
    arrived = lax.ppermute(first[::-1], "tensor", FALL)
    back_own, back_pair, d_up, d_bias = call(
        mix_back_kernel,
        steps,
        [Q, K, V, LOW, Q, K, V, CUMS, CUMS, (STATES, "t", 0), (STATES, "t", 0), STATE, UP, HEADS_WIDE, HEADS_WIDE],
        [
            (((CHUNK, own.shape[1]), "r", 0), BF),
            (((CHUNK, pair.shape[1]), "r", 0), BF),
            (UP, F32),
            (BIAS, F32),
        ],
        [pltpu.VMEM((2, CHUNK, HEAD_K), F32), pltpu.VMEM((2, CHUNK, HEAD_K), F32), SQUARES, SQUARES, PASSED],
        12 << 30,
        (own, own, own, own, pair, pair, pair, cums, logits, full, ends, arrived, up, d_mixed, d_gate),
        shift,
        backward=True,
    )
    return back_own, back_pair, d_up, d_bias, d_gain


def hidden_kernel(rows, cot, *refs):
    for h in range(2):
        gate_w, up_w, down_w = refs[3 * h : 3 * h + 3]
        hidden, d_gate, d_up = refs[6 + 3 * h : 9 + 3 * h]
        gate = project(rows[...], gate_w[...])
        up = project(rows[...], up_w[...])
        grad = project(cot[...], down_w[...])
        sigmoid = jax.nn.sigmoid(gate)
        silu = gate * sigmoid
        hidden[...] = (silu * up).astype(BF)
        d_up[...] = (grad * silu).astype(BF)
        d_gate[...] = (grad * up * sigmoid * (1.0 + gate * (1.0 - sigmoid))).astype(BF)


def hidden_products(rows, cot, weights):
    tokens, width = rows.shape
    units = weights[0].shape[1]
    tile = min(FF_ROWS, tokens)
    by_row = pl.BlockSpec((tile, width), lambda n: (n, 0))
    fixed = pl.BlockSpec((width, units), lambda n: (0, 0))
    return pl.pallas_call(
        hidden_kernel,
        grid=(tokens // tile,),
        in_specs=[by_row, by_row] + [fixed] * 6,
        out_specs=[pl.BlockSpec((tile, units), lambda n: (n, 0))] * 6,
        out_shape=[jax.ShapeDtypeStruct((tokens, units), BF)] * 6,
        compiler_params=pltpu.CompilerParams(vmem_limit_bytes=56 << 20),
        cost_estimate=pl.CostEstimate(
            flops=12 * tokens * width * units, bytes_accessed=24 << 20, transcendentals=0
        ),
    )(rows, cot, *weights)


def norm_back(grad_out, normal, scale, gain):
    scaled_grad = grad_out * gain
    return scale * (scaled_grad - normal * jnp.mean(scaled_grad * normal, axis=-1, keepdims=True))


def sum_cores(full):
    half = full.shape[0] // 2
    return full[:half].astype(F32) + swap(full[half:].astype(BF), "tensor", CORE).astype(F32)


def both_cores(mine):
    return jnp.concatenate([mine, swap(mine, "tensor", CORE)], axis=0)


def local(
    tokens,
    norm_gain,
    query_weight,
    key_weight,
    value_weight,
    gate_weight,
    low_down,
    low_up,
    rank_bias,
    head_gain,
    out_weight,
    mlp_gain,
    mlp_gate,
    mlp_up,
    mlp_down,
    cotangent,
):
    count = lax.axis_size("dp")
    rows, rank = low_down.shape
    width = rows * count
    member = lax.axis_index("tensor")
    shift = (member % 2 * (tokens.shape[0] // CHUNK)).astype(jnp.int32).reshape(1)

    def tall(array):
        return jnp.pad(array, ((0, rows - array.shape[0]), (0, 0)))

    small = [low_down, norm_gain[:, None], mlp_gain[:, None], tall(low_up[0].T), tall(rank_bias.T), tall(head_gain[:, None])]
    small = jnp.concatenate(small, axis=1)
    small = jnp.pad(small, ((0, 0), (0, LANES - small.shape[1])))
    in_own, in_pair = gather(jnp.concatenate([query_weight, key_weight, value_weight, gate_weight, small], axis=1))
    out_own, out_pair = gather(out_weight.T)
    gate_own, gate_pair = gather(mlp_gate)
    up_own, up_pair = gather(mlp_up)
    down_own, down_pair = gather(mlp_down.T)

    def joined(pieces, start=0, stop=None):
        return jnp.concatenate([p[:, start:stop] for p in pieces], axis=0)

    used = 2 * HEAD_K + 2 * HEAD_V
    w_in_own = joined(in_own)
    w_in_pair = joined(in_pair, 0, used)
    small_own = w_in_own[:, used:]
    small_pair = joined(in_pair, used)
    w_out_own, w_out_pair = joined(out_own), joined(out_pair)
    w_gate_own, w_gate_pair = joined(gate_own), joined(gate_pair)
    w_up_own, w_up_pair = joined(up_own), joined(up_pair)
    w_down_own, w_down_pair = joined(down_own), joined(down_pair)

    order = block_matrix()

    def to_actual(array, start, stop, depth):
        blocks = array[:, start:stop].reshape(count, rows, stop - start)[:, :depth].astype(F32)
        flat = exact(order, blocks.reshape(count, depth * (stop - start)))
        return flat.reshape(count * depth, stop - start)

    def to_places(array, depth):
        blocks = array.reshape(count, depth, array.shape[1])
        flat = lax.dot_general(
            order, blocks.reshape(count, -1), (((0,), (0,)), ((), ())), preferred_element_type=F32, precision=TOP_PRECISION
        )
        return flat.reshape(count, depth, array.shape[1])

    slots = rank + 2
    gain_one = small_own[:, rank].astype(F32)
    gain_two = small_own[:, rank + 1].astype(F32)
    deep = low_up.shape[2]
    up, bias = [], []
    for array in (small_own, small_pair):
        head = to_actual(array, slots, slots + rank + 1, deep)
        up.append(jnp.pad(head[:, :rank].T, ((0, LANES - rank), (0, 0))))
        bias.append(head[:, rank][None, :])
    up, bias = jnp.stack(up), jnp.stack(bias)
    gain_head = to_actual(small_own, slots + rank + 1, slots + rank + 2, head_gain.shape[0]).reshape(1, -1)

    places = place_matrix(width)
    tokens = project(tokens, places).astype(BF)
    cot_mine = project(cotangent, places).astype(BF)
    cot_rows = both_cores(cot_mine)

    inputs = tokens.astype(F32)
    scale_one = lax.rsqrt(jnp.mean(inputs * inputs, axis=-1, keepdims=True) + NORM_EPS)
    normal_one = inputs * scale_one
    normed_rows = both_cores((normal_one * gain_one).astype(BF))
    proj_own = project(normed_rows, w_in_own)
    proj_pair = project(normed_rows, w_in_pair)
    gated_own, gated_pair, kept = mixer(proj_own, proj_pair, up, bias, gain_head, shift)
    middle = inputs + sum_cores(contract_last(gated_own, w_out_own) + contract_last(gated_pair, w_out_pair))
    scale_two = lax.rsqrt(jnp.mean(middle * middle, axis=-1, keepdims=True) + NORM_EPS)
    normal_two = middle * scale_two
    mlp_rows = both_cores((normal_two * gain_two).astype(BF))

    hidden_own, d_gate_own, d_up_own, hidden_pair, d_gate_pair, d_up_pair = hidden_products(
        mlp_rows, cot_rows, (w_gate_own, w_up_own, w_down_own, w_gate_pair, w_up_pair, w_down_pair)
    )
    grad_second = sum_cores(
        contract_last(d_gate_own, w_gate_own)
        + contract_last(d_gate_pair, w_gate_pair)
        + contract_last(d_up_own, w_up_own)
        + contract_last(d_up_pair, w_up_pair)
    )
    outputs = middle + sum_cores(contract_last(hidden_own, w_down_own) + contract_last(hidden_pair, w_down_pair))
    block_out = contract_last(outputs.astype(BF), places).astype(BF)

    def weight_grad(left, own, pair):
        return scatter(contract_rows(left, own).astype(BF), contract_rows(left, pair).astype(BF))

    grad_mlp_down = weight_grad(cot_rows, hidden_own, hidden_pair).T
    grad_mlp_gate = weight_grad(mlp_rows, d_gate_own, d_gate_pair)
    grad_mlp_up = weight_grad(mlp_rows, d_up_own, d_up_pair)

    grad_mlp_gain = jnp.sum(grad_second * normal_two, axis=0)
    grad_middle = cot_mine.astype(F32) + norm_back(grad_second, normal_two, scale_two, gain_two)
    mixer_cot = both_cores(grad_middle.astype(BF))
    grad_out_weight = weight_grad(mixer_cot, gated_own, gated_pair).T
    back_own, back_pair, d_up, d_bias, d_gain = mixer_back(
        proj_own, proj_pair, up, gain_head, shift, kept, project(mixer_cot, w_out_own), project(mixer_cot, w_out_pair)
    )
    grad_normed = sum_cores(contract_last(back_own, w_in_own) + contract_last(back_pair, w_in_pair))
    grad_norm_gain = jnp.sum(grad_normed * normal_one, axis=0)
    grad_inputs = grad_middle + norm_back(grad_normed, normal_one, scale_one, gain_one)
    high = grad_inputs.astype(BF)
    rest = (grad_inputs - high.astype(F32)).astype(BF)
    grad_inputs = contract_last(high, places) + contract_last(rest, places)

    grad_own = contract_rows(normed_rows, back_own).astype(BF)
    grad_pair = contract_rows(normed_rows, back_pair).astype(BF)
    grad_in = scatter(grad_own[:, :used], grad_pair)

    quarter = rows // 4
    shared = jnp.concatenate(
        [
            grad_own[:, used : used + rank].astype(F32),
            grad_norm_gain[:, None],
            grad_mlp_gain[:, None],
            jnp.pad(
                to_places(d_gain.reshape(-1, 1), head_gain.shape[0]).reshape(count, 4, -1, 1),
                ((0, 0), (0, 0), (0, quarter - head_gain.shape[0] // 4), (0, 0)),
            ).reshape(width, 1),
        ],
        axis=1,
    )
    half_of = lax.broadcasted_iota(jnp.int32, (width, 1), 0) % rows // (2 * quarter)
    pieces = []
    for h, half in ((0, member // 2), (1, 1 - member // 2)):
        head = jnp.concatenate([d_up[h, :rank].T, d_bias[h].T], axis=1)
        head = jnp.pad(to_places(head, deep), ((0, 0), (0, rows - deep), (0, 0))).reshape(width, rank + 1)
        piece = jnp.concatenate([jnp.where(half_of == half, shared, 0.0), head], axis=1)
        pieces.append(jnp.pad(piece, ((0, 0), (0, LANES - piece.shape[1]))).astype(BF))
    small_grad = scatter(*pieces)
    grad_low_up = small_grad[:deep, rank + 3 : 2 * rank + 3].T[None]
    grad_rank_bias = small_grad[:deep, 2 * rank + 3][None]
    shared = small_grad + swap(small_grad.astype(BF), "tensor", CORE).astype(F32)
    shared = lax.dynamic_slice_in_dim(shared, member * quarter, quarter, 0)

    return (
        block_out,
        grad_inputs,
        shared[:, rank],
        grad_in[:, :HEAD_K],
        grad_in[:, HEAD_K : 2 * HEAD_K],
        grad_in[:, 2 * HEAD_K : 2 * HEAD_K + HEAD_V],
        grad_in[:, 2 * HEAD_K + HEAD_V :],
        shared[:, :rank],
        grad_low_up,
        grad_rank_bias,
        shared[: head_gain.shape[0] // 4, rank + 2],
        grad_out_weight,
        shared[:, rank + 1],
        grad_mlp_gate,
        grad_mlp_up,
        grad_mlp_down,
    )


def solution(mesh):
    return jax.shard_map(
        local,
        mesh=mesh,
        in_specs=(
            P(("dp", "tensor"), None),
            P("dp"),
            P("dp", "tensor"),
            P("dp", "tensor"),
            P("dp", "tensor"),
            P("dp", "tensor"),
            P("dp", None),
            P("tensor", None, "dp"),
            P("tensor", "dp"),
            P("dp"),
            P("tensor", "dp"),
            P("dp"),
            P("dp", "tensor"),
            P("dp", "tensor"),
            P("tensor", "dp"),
            P(("dp", "tensor"), None),
        ),
        out_specs=(
            P(("dp", "tensor"), None),
            P(("dp", "tensor"), None),
            P(("dp", "tensor")),
            P("dp", "tensor"),
            P("dp", "tensor"),
            P("dp", "tensor"),
            P("dp", "tensor"),
            P(("dp", "tensor"), None),
            P("tensor", None, "dp"),
            P("tensor", "dp"),
            P(("dp", "tensor")),
            P("tensor", "dp"),
            P(("dp", "tensor")),
            P("dp", "tensor"),
            P("dp", "tensor"),
            P("tensor", "dp"),
        ),
        check_vma=False,
    )
```

time: 1550 us -> 614 us (0.40)
  waiting for transfers between devices: 542 us -> 135 us
  blocking collectives: 307 us -> 0 us
  matrix products: 347 us -> 83.4 us
  starting transfers between devices: 20.2 us -> 129 us
  local copies, waits for them, and re-layouts: 214 us -> 134 us
  Pallas kernels: 0 us -> 61.9 us
  other arithmetic: 73.4 us -> 56.5 us
    reduce_scatter x7 -> x0, waiting for transfers between devices: 327 us -> none  [the longest x1 76 us: local(): lax.psum_scatter(grad_mlp_up, 'dp', scatter_dimension=0, tiled=True)]
    all_gather x9 -> x0, blocking collectives: 250 us -> none  [the longest x1 33.3 us: local(): lax.all_gather(gate_weight, 'dp', axis=0, tiled=True)]
    dot_general x524 -> x12, matrix products: 254 us -> 18.4 us  [the longest x6 16.7 us: project(): return jnp.dot(former, latter, preferred_element_type=F32)]
    all_gather x7 -> x0, waiting for transfers between devices: 170 us -> none  [the longest x1 37 us: local(): lax.all_gather(mlp_gate, 'dp', axis=0, tiled=True)]
    ppermute x0 -> x100, waiting for transfers between devices: none -> 135 us  [the longest x98 131 us: swap(): return lax.ppermute(array, axis, [(i, i ^ mask) for i in range(size)])]
    dynamic_slice x192 -> x0, local copies, waits for them, and re-layouts: 135 us -> none  [mixer(): lax.scan(jax.checkpoint(block_step), initial, (blocked(queries, HEAD_K),...]
    ppermute x0 -> x100, starting transfers between devices: none -> 129 us  [the longest x98 124 us: swap(): return lax.ppermute(array, axis, [(i, i ^ mask) for i in range(size)])]
    pallas_call x0 -> x5, Pallas kernels: none -> 61.9 us  [the longest x4 36.6 us: call(): pl.pallas_call(kernel, grid_spec=pltpu.PrefetchScalarGridSpec(num_scalar_...]
  transfers between devices with their start and end apart: 19 -> 100, of which waited for: 16 -> 32; matrix products, arithmetic and copies ran while one was open for 8% -> 37% of each run, Pallas kernels for 0% -> 6%
where the time goes in v1:
time: 614 us; the launch traced here: 603 us
  waiting for transfers between devices  135 us (22%)
  local copies, waits for them, and re-layouts  134 us (22%)
  starting transfers between devices  129 us (21%)
  matrix products  83.4 us (14%)
  Pallas kernels  61.9 us (10%)
  other arithmetic  56.5 us (9%)
    ppermute x98, waiting for transfers between devices, swap(): return lax.ppermute(array, axis, [(i, i ^ mask) for i in range(size)])  131 us
    ppermute x98, starting transfers between devices, swap(): return lax.ppermute(array, axis, [(i, i ^ mask) for i in range(size)])  124 us
    unnamed x279, local copies, waits for them, and re-layouts  62.7 us
    pallas_call x4, Pallas kernels, call(): pl.pallas_call(kernel, grid_spec=pltpu.PrefetchScalarGridSpec(num_scalar_...  36.6 us
    dot_general x13, matrix products, contract_last(): lax.dot_general(former, latter, (((1,), (1,)), ((), ())), preferred_eleme...  36.5 us
    dot_general x10, matrix products, contract_rows(): lax.dot_general(former, latter, (((0,), (0,)), ((), ())), preferred_eleme...  28.5 us
    pallas_call x1, Pallas kernels, hidden_products(): pl.pallas_call(hidden_kernel, grid=(tokens // tile,), in_specs=[by_row, b...  25.2 us
    dot_general x6, matrix products, project(): return jnp.dot(former, latter, preferred_element_type=F32)  16.7 us
  transfers between devices with their start and end apart: 100, of which 32 were waited for; matrix products, arithmetic and copies ran while one was open for 37% of the time, Pallas kernels for 6%

profile of v1, /device:TPU:0, one launch (start us, length us, event | category | flops | bytes accessed | tf_op | source)
XLA Modules:
  0.0 603.0 jit_solution(7357070466126145537)
XLA Ops:
  10.8 3.0 collective-permute-start
  23.5 4.1 fusion.24
  42.5 12.1 %collective-permute-done.20 = bf16[128,704]{1,0:T(8,128)(2,1)S(1)} collective-permute-done((bf16[128,704]{1,0:T(8,128)(2,1)S(1)}, bf16[128,704]{1,0:T(8,128)(2,1)S(1)}, u32[]{:S(2)}, u32[]{:S(2)}) %collective-permute-start.20) | collective-permute-done | bytes 180256 | tf_op jit(solution)/shard_map/ppermute | solution.py:27
  54.6 6.4 %collective-permute-start.24 = (bf16[128,704]{1,0:T(8,128)(2,1)S(1)}, bf16[128,704]{1,0:T(8,128)(2,1)}, u32[]{:S(2)}, u32[]{:S(2)}) collective-permute-start(bf16[128,704]{1,0:T(8,128)(2,1)S(1)} %copy.125), channel_id=1, source_target_pairs={{0,16},{4,20},{8,24},{12,28},{16,0},{20,4},{24,8},{28,12},{1,17},{... | collective-permute-start | bytes 540680 | tf_op jit(solution)/shard_map/ppermute | solution.py:27
  68.0 8.4 %collective-permute-done.24 = bf16[128,704]{1,0:T(8,128)(2,1)} collective-permute-done((bf16[128,704]{1,0:T(8,128)(2,1)S(1)}, bf16[128,704]{1,0:T(8,128)(2,1)}, u32[]{:S(2)}, u32[]{:S(2)}) %collective-permute-start.24) | collective-permute-done | bytes 180256 | tf_op jit(solution)/shard_map/ppermute | solution.py:27
  89.7 10.1 %collective-permute-done.14 = bf16[256,256]{0,1:T(8,128)(2,1)S(1)} collective-permute-done((bf16[256,256]{0,1:T(8,128)(2,1)S(1)}, bf16[256,256]{0,1:T(8,128)(2,1)S(1)}, u32[]{:S(2)}, u32[]{:S(2)}) %collective-permute-start.14) | collective-permute-done | bytes 131104 | tf_op jit(solution)/shard_map/ppermute | solution.py:27
  99.8 5.8 collective-permute-start.28
  117.4 3.0 collective-permute-start.29
  123.5 3.6 fusion.61.k_own.v_own.low.q_own.g_own
  127.2 4.7 fusion.28.k_pair.v_pair.q_pair.g_pair
  131.9 9.3 %shard_map.279 = (f32[1024,256]{1,0:T(8,128)S(1)}, f32[1024,256]{1,0:T(8,128)S(1)}, f32[8,2,256,128]{3,2,1,0:T(8,128)S(1)}, f32[2,256,128]{2,1,0:T(8,128)S(1)}) custom-call(s32[1]{0:T(128)} %bitcast.1.shift, f32[1024,896]{1,0:T(8,128)S(1)} %fusion.61.k_own.v_own.low.q_own.g_own, f32[1024,896]{1,0:T(8,128)S(1)} %fusion.61.k_own.v_own.low.q_own.g_own, ...), custom_call_target="tpu_custom_call" | custom-call | flops 4294967296 | bytes 12582912 | tf_op jit(solution)/shard_map/pallas_call | solution.py:353
  145.2 3.8 collective-permute-start.8
  150.5 4.8 collective-permute-done.8.arrived
  160.1 7.0 %shard_map.280 = (bf16[1024,256]{1,0:T(8,128)(2,1)S(1)}, bf16[1024,256]{1,0:T(8,128)(2,1)S(1)}, f32[1024,512]{1,0:T(8,128)S(1)}, bf16[8,2,256,128]{3,2,1,0:T(8,128)(2,1)S(1)}) custom-call(s32[1]{0:T(128)} %bitcast.1.shift, f32[1024,896]{1,0:T(8,128)S(1)} %copy-done.3, f32[1024,896]{1,0:T(8,128)S(1)} %copy-done.3, f32[1024,896]{1,0:T(8,128)S(1)} %copy-done.3, ...), custom_call_target="tpu_custom_call" | custom-call | flops 6442450944 | bytes 12582912 | tf_op jit(solution)/shard_map/pallas_call | solution.py:353
  203.1 7.7 %collective-permute-done.34 = bf16[512,704]{0,1:T(8,128)(2,1)} collective-permute-done((bf16[512,704]{0,1:T(8,128)(2,1)}, bf16[512,704]{0,1:T(8,128)(2,1)}, u32[]{:S(2)}, u32[]{:S(2)}) %collective-permute-start.34) | collective-permute-done | bytes 720928 | tf_op jit(solution)/shard_map/ppermute | solution.py:27
  245.8 3.0 pad_maximum_fusion.2.cot
  262.1 25.2 %shard_map.281 = (bf16[1024,704]{1,0:T(8,128)(2,1)}, bf16[1024,704]{1,0:T(8,128)(2,1)}, bf16[1024,704]{1,0:T(8,128)(2,1)}, bf16[1024,704]{1,0:T(8,128)(2,1)}, bf...) custom-call(bf16[1024,1024]{1,0:T(8,128)(2,1)} %pad_maximum_fusion.1.rows, bf16[1024,1024]{1,0:T(8,128)(2,1)} %pad_maximum_fusion.2.cot, ...), custom_call_target="tpu_custom_call" | custom-call | flops 8858370048 | bytes 25165824 | tf_op jit(solution)/shard_map/pallas_call | solution.py:466
  287.3 3.8 convolution_convert_fusion.2
  295.6 3.4 convolution_convert_fusion.3
  302.3 3.4 convolution_convert_fusion.5
  307.0 3.2 convolution_convert_fusion.4
  313.0 3.2 convolution_convert_fusion.6
  318.1 3.8 fusion.96
  323.7 5.2 convolution_add_fusion.2
  331.9 3.2 add_add_fusion
  335.1 3.4 convolution_convert_fusion.7
  346.4 4.4 collective-permute-done.85
  360.2 6.0 %collective-permute-done.93 = bf16[256,704]{0,1:T(8,128)(2,1)S(1)} collective-permute-done((bf16[256,704]{0,1:T(8,128)(2,1)S(1)}, bf16[256,704]{0,1:T(8,128)(2,1)S(1)}, u32[]{:S(2)}, u32[]{:S(2)}) %collective-permute-start.93) | collective-permute-done | bytes 360480 | tf_op jit(solution)/shard_map/ppermute | solution.py:27
  370.5 3.5 collective-permute-done.82
  376.8 4.9 collective-permute-done.84
  383.7 5.8 collective-permute-done.73
  389.6 4.7 collective-permute-done.75
  398.6 13.9 %collective-permute-done.98 = bf16[128,704]{0,1:T(8,128)(2,1)S(1)} collective-permute-done((bf16[128,704]{0,1:T(8,128)(2,1)S(1)}, bf16[128,704]{0,1:T(8,128)(2,1)S(1)}, u32[]{:S(2)}, u32[]{:S(2)}) %collective-permute-start.98) | collective-permute-done | bytes 180256 | tf_op jit(solution)/shard_map/ppermute | solution.py:27
  414.9 5.3 collective-permute-start.79
  420.1 6.4 %collective-permute-done.89 = bf16[128,704]{0,1:T(8,128)(2,1)S(1)} collective-permute-done((bf16[128,704]{0,1:T(8,128)(2,1)S(1)}, bf16[128,704]{0,1:T(8,128)(2,1)S(1)}, u32[]{:S(2)}, u32[]{:S(2)}) %collective-permute-start.89) | collective-permute-done | bytes 180256 | tf_op jit(solution)/shard_map/ppermute | solution.py:27
  426.5 3.1 collective-permute-start.81
  430.5 9.1 %collective-permute-done.80 = bf16[128,704]{0,1:T(8,128)(2,1)S(1)} collective-permute-done((bf16[128,704]{0,1:T(8,128)(2,1)S(1)}, bf16[128,704]{0,1:T(8,128)(2,1)S(1)}, u32[]{:S(2)}, u32[]{:S(2)}) %collective-permute-start.80) | collective-permute-done | bytes 180256 | tf_op jit(solution)/shard_map/ppermute | solution.py:27
  441.7 3.3 fusion.77
  458.7 6.6 %shard_map.282 = (bf16[1024,512]{1,0:T(8,128)(2,1)S(1)}, bf16[1024,512]{1,0:T(8,128)(2,1)S(1)}, f32[8,2,256,128]{3,2,1,0:T(8,128)S(1)}, f32[2,256,128]{2,1,0:T(8,128)S(1)}, f32[1,256]{1,0:T(1,128)S(1)}) custom-call(s32[1]{0:T(128)} %bitcast.1.shift, f32[1024,896]{1,0:T(8,128)} %copy-done.2, f32[1024,896]{1,0:T(8,128)} %copy-done.2, ...), custom_call_target="tpu_custom_call" | custom-call | flops 6442450944 | bytes 12582912 | tf_op jit(solution)/shard_map/pallas_call | solution.py:353
  488.0 13.7 %shard_map.283 = (bf16[1024,896]{1,0:T(8,128)(2,1)S(1)}, bf16[1024,768]{1,0:T(8,128)(2,1)S(1)}, f32[2,128,128]{2,1,0:T(8,128)S(1)}, f32[2,1,128]{2,1,0:T(1,128)S(1)}) custom-call(s32[1]{0:T(128)} %bitcast.1.shift, f32[1024,896]{1,0:T(8,128)} %copy-done.2, f32[1024,896]{1,0:T(8,128)} %copy-done.2, f32[1024,896]{1,0:T(8,128)} %copy-done.2, ...), custom_call_target="tpu_custom_call" | custom-call | flops 12884901888 | bytes 12582912 | tf_op jit(solution)/shard_map/pallas_call | solution.py:353
  501.7 3.4 convolution_convert_fusion
  513.3 3.1 convolution_convert_fusion.1
  521.5 4.3 convolution_add_fusion.1
  526.5 3.3 collective-permute-done.56
  540.6 3.1 collective-permute-done.57
  553.5 5.2 collective-permute-done.61
  558.7 6.4 %collective-permute-done.62 = bf16[128,768]{0,1:T(8,128)(2,1)} collective-permute-done((bf16[128,768]{0,1:T(8,128)(2,1)}, bf16[128,768]{0,1:T(8,128)(2,1)}, u32[]{:S(2)}, u32[]{:S(2)}) %collective-permute-start.62) | collective-permute-done | bytes 196640 | tf_op jit(solution)/shard_map/ppermute | solution.py:27
  588.8 4.2 collective-permute-start.51
  (630 shorter events, 321.4 us)
Async XLA Ops:
  10.8 50.1 %collective-permute-start = (bf16[128,896]{1,0:T(8,128)(2,1)}, bf16[128,896]{1,0:T(8,128)(2,1)S(1)}, u32[]{:S(2)}, u32[]{:S(2)}) collective-permute-start(bf16[128,896]{1,0:T(8,128)(2,1)} %get-tuple-element.200), channel_id=1, source_target_pairs={{0,8},{4,12},{8,0},{12,4},{16,24},{20,28},{24,16},{28,20},{1,9},{5... | collective-permute-start | bytes 688136 | tf_op jit(solution)/shard_map/ppermute | solution.py:27
  13.9 49.0 %collective-permute-start.1 = (bf16[128,896]{1,0:T(8,128)(2,1)}, bf16[128,896]{1,0:T(8,128)(2,1)S(1)}, u32[]{:S(2)}, u32[]{:S(2)}) collective-permute-start(bf16[128,896]{1,0:T(8,128)(2,1)} %get-tuple-element.200), channel_id=1, source_target_pairs={{0,16},{4,20},{8,24},{12,28},{16,0},{20,4},{24,8},{28,12},{1,17},{... | collective-permute-start | bytes 688136 | tf_op jit(solution)/shard_map/ppermute | solution.py:27
  33.7 20.8 %collective-permute-start.20 = (bf16[128,704]{1,0:T(8,128)(2,1)S(1)}, bf16[128,704]{1,0:T(8,128)(2,1)S(1)}, u32[]{:S(2)}, u32[]{:S(2)}) collective-permute-start(bf16[128,704]{1,0:T(8,128)(2,1)S(1)} %copy.118), channel_id=1, source_target_pairs={{0,16},{4,20},{8,24},{12,28},{16,0},{20,4},{24,8},{28,12},{1,17},{... | collective-permute-start | bytes 540680 | tf_op jit(solution)/shard_map/ppermute | solution.py:27
  35.0 19.6 %collective-permute-start.21 = (bf16[128,704]{1,0:T(8,128)(2,1)S(1)}, bf16[128,704]{1,0:T(8,128)(2,1)S(1)}, u32[]{:S(2)}, u32[]{:S(2)}) collective-permute-start(bf16[128,704]{1,0:T(8,128)(2,1)S(1)} %copy.118), channel_id=1, source_target_pairs={{0,24},{4,28},{8,16},{12,20},{16,8},{20,12},{24,0},{28,4},{1,25},{... | collective-permute-start | bytes 540680 | tf_op jit(solution)/shard_map/ppermute | solution.py:27
  40.7 22.2 %collective-permute-start.2 = (bf16[128,896]{1,0:T(8,128)(2,1)}, bf16[128,896]{1,0:T(8,128)(2,1)S(1)}, u32[]{:S(2)}, u32[]{:S(2)}) collective-permute-start(bf16[128,896]{1,0:T(8,128)(2,1)} %get-tuple-element.200), channel_id=1, source_target_pairs={{0,24},{4,28},{8,16},{12,20},{16,8},{20,12},{24,0},{28,4},{1,25},{... | collective-permute-start | bytes 688136 | tf_op jit(solution)/shard_map/ppermute | solution.py:27
  54.6 21.9 %collective-permute-start.24 = (bf16[128,704]{1,0:T(8,128)(2,1)S(1)}, bf16[128,704]{1,0:T(8,128)(2,1)}, u32[]{:S(2)}, u32[]{:S(2)}) collective-permute-start(bf16[128,704]{1,0:T(8,128)(2,1)S(1)} %copy.125), channel_id=1, source_target_pairs={{0,16},{4,20},{8,24},{12,28},{16,0},{20,4},{24,8},{28,12},{1,17},{... | collective-permute-start | bytes 540680 | tf_op jit(solution)/shard_map/ppermute | solution.py:27
  62.9 112.8 %collective-permute-start.27 = (bf16[128,704]{1,0:T(8,128)(2,1)}, bf16[128,704]{1,0:T(8,128)(2,1)}, u32[]{:S(2)}, u32[]{:S(2)}) collective-permute-start(bf16[128,704]{1,0:T(8,128)(2,1)} %bitcast.17), channel_id=1, source_target_pairs={{0,8},{4,12},{8,0},{12,4},{16,24},{20,28},{24,16},{28,20},{1,9},{5... | collective-permute-start | bytes 540680 | tf_op jit(solution)/shard_map/ppermute | solution.py:27
  62.9 21.0 %collective-permute-start.13 = (bf16[512,256]{0,1:T(8,128)(2,1)}, bf16[512,256]{0,1:T(8,128)(2,1)}, u32[]{:S(2)}, u32[]{:S(2)}) collective-permute-start(bf16[512,256]{0,1:T(8,128)(2,1)} %pad_maximum_fusion.16), channel_id=1, source_target_pairs={{0,2},{1,3},{2,0},{3,1},{4,6},{5,7},{6,4},{7,5},{8,10},{9,11},{10,... | collective-permute-start | bytes 786440 | tf_op jit(solution)/shard_map/ppermute | solution.py:27
  66.5 19.1 %collective-permute-start.12 = (bf16[512,256]{0,1:T(8,128)(2,1)}, bf16[512,256]{0,1:T(8,128)(2,1)}, u32[]{:S(2)}, u32[]{:S(2)}) collective-permute-start(bf16[512,256]{0,1:T(8,128)(2,1)} %pad_maximum_fusion.16), channel_id=1, source_target_pairs={{0,4},{4,0},{8,12},{12,8},{16,20},{20,16},{24,28},{28,24},{1,5},{5... | collective-permute-start | bytes 786440 | tf_op jit(solution)/shard_map/ppermute | solution.py:27
  76.4 30.6 %collective-permute-start.5 = (bf16[512,896]{1,0:T(8,128)(2,1)}, bf16[512,896]{1,0:T(8,128)(2,1)S(1)}, u32[]{:S(2)}, u32[]{:S(2)}) collective-permute-start(bf16[512,896]{1,0:T(8,128)(2,1)} %pad_maximum_fusion.8), channel_id=1, source_target_pairs={{0,2},{1,3},{2,0},{3,1},{4,6},{5,7},{6,4},{7,5},{8,10},{9,11},{10,... | collective-permute-start | bytes 2752520 | tf_op jit(solution)/shard_map/ppermute | solution.py:27
  78.0 31.4 %collective-permute-start.3 = (bf16[512,896]{1,0:T(8,128)(2,1)}, bf16[512,896]{1,0:T(8,128)(2,1)}, u32[]{:S(2)}, u32[]{:S(2)}) collective-permute-start(bf16[512,896]{1,0:T(8,128)(2,1)} %pad_maximum_fusion.8), channel_id=1, source_target_pairs={{0,4},{4,0},{8,12},{12,8},{16,20},{20,16},{24,28},{28,24},{1,5},{5... | collective-permute-start | bytes 2752520 | tf_op jit(solution)/shard_map/ppermute | solution.py:27
  86.5 19.8 %collective-permute-start.15 = (bf16[256,256]{0,1:T(8,128)(2,1)S(1)}, bf16[256,256]{0,1:T(8,128)(2,1)S(1)}, u32[]{:S(2)}, u32[]{:S(2)}) collective-permute-start(bf16[256,256]{0,1:T(8,128)(2,1)S(1)} %slice.499), channel_id=1, source_target_pairs={{0,2},{1,3},{2,0},{3,1},{4,6},{5,7},{6,4},{7,5},{8,10},{9,11},{10,... | collective-permute-start | bytes 393224 | tf_op jit(solution)/shard_map/ppermute | solution.py:27
  99.8 78.3 %collective-permute-start.28 = (bf16[128,704]{1,0:T(8,128)(2,1)}, bf16[128,704]{1,0:T(8,128)(2,1)}, u32[]{:S(2)}, u32[]{:S(2)}) collective-permute-start(bf16[128,704]{1,0:T(8,128)(2,1)} %bitcast.17), channel_id=1, source_target_pairs={{0,16},{4,20},{8,24},{12,28},{16,0},{20,4},{24,8},{28,12},{1,17},{... | collective-permute-start | bytes 540680 | tf_op jit(solution)/shard_map/ppermute | solution.py:27
  117.4 61.3 %collective-permute-start.29 = (bf16[128,704]{1,0:T(8,128)(2,1)}, bf16[128,704]{1,0:T(8,128)(2,1)}, u32[]{:S(2)}, u32[]{:S(2)}) collective-permute-start(bf16[128,704]{1,0:T(8,128)(2,1)} %bitcast.17), channel_id=1, source_target_pairs={{0,24},{4,28},{8,16},{12,20},{16,8},{20,12},{24,0},{28,4},{1,25},{... | collective-permute-start | bytes 540680 | tf_op jit(solution)/shard_map/ppermute | solution.py:27
  120.6 117.4 %collective-permute-start.18 = (bf16[512,1024]{1,0:T(8,128)(2,1)}, bf16[512,1024]{1,0:T(8,128)(2,1)}, u32[]{:S(2)}, u32[]{:S(2)}) collective-permute-start(bf16[512,1024]{1,0:T(8,128)(2,1)} %fusion.24), channel_id=1, source_target_pairs={{0,1},{1,0},{2,3},{3,2},{4,5},{5,4},{6,7},{7,6},{8,9},{9,8},{10,11... | collective-permute-start | bytes 3145736 | tf_op jit(solution)/shard_map/ppermute | solution.py:27
  175.0 21.0 %collective-permute-start.16 = (bf16[512,1024]{1,0:T(8,128)(2,1)}, bf16[512,1024]{1,0:T(8,128)(2,1)}, u32[]{:S(2)}, u32[]{:S(2)}) collective-permute-start(bf16[512,1024]{1,0:T(8,128)(2,1)} %slice.669), channel_id=1, source_target_pairs={{0,1},{1,0},{2,3},{3,2},{4,5},{5,4},{6,7},{7,6},{8,9},{9,8},{10,11... | collective-permute-start | bytes 3145736 | tf_op jit(solution)/shard_map/ppermute | solution.py:27
  175.7 19.7 %collective-permute-start.31 = (bf16[512,704]{0,1:T(8,128)(2,1)}, bf16[512,704]{0,1:T(8,128)(2,1)}, u32[]{:S(2)}, u32[]{:S(2)}) collective-permute-start(bf16[512,704]{0,1:T(8,128)(2,1)} %copy.117), channel_id=1, source_target_pairs={{0,2},{1,3},{2,0},{3,1},{4,6},{5,7},{6,4},{7,5},{8,10},{9,11},{10,... | collective-permute-start | bytes 2162696 | tf_op jit(solution)/shard_map/ppermute | solution.py:27
  178.1 21.8 %collective-permute-start.22 = (bf16[512,704]{0,1:T(8,128)(2,1)}, bf16[512,704]{0,1:T(8,128)(2,1)}, u32[]{:S(2)}, u32[]{:S(2)}) collective-permute-start(bf16[512,704]{0,1:T(8,128)(2,1)} %copy.117), channel_id=1, source_target_pairs={{0,4},{4,0},{8,12},{12,8},{16,20},{20,16},{24,28},{28,24},{1,5},{5... | collective-permute-start | bytes 2162696 | tf_op jit(solution)/shard_map/ppermute | solution.py:27
  178.7 32.1 %collective-permute-start.34 = (bf16[512,704]{0,1:T(8,128)(2,1)}, bf16[512,704]{0,1:T(8,128)(2,1)}, u32[]{:S(2)}, u32[]{:S(2)}) collective-permute-start(bf16[512,704]{0,1:T(8,128)(2,1)} %copy.124), channel_id=1, source_target_pairs={{0,2},{1,3},{2,0},{3,1},{4,6},{5,7},{6,4},{7,5},{8,10},{9,11},{10,... | collective-permute-start | bytes 2162696 | tf_op jit(solution)/shard_map/ppermute | solution.py:27
  195.4 29.2 %collective-permute-start.26 = (bf16[512,704]{0,1:T(8,128)(2,1)}, bf16[512,704]{0,1:T(8,128)(2,1)}, u32[]{:S(2)}, u32[]{:S(2)}) collective-permute-start(bf16[512,704]{0,1:T(8,128)(2,1)} %copy.124), channel_id=1, source_target_pairs={{0,4},{4,0},{8,12},{12,8},{16,20},{20,16},{24,28},{28,24},{1,5},{5... | collective-permute-start | bytes 2162696 | tf_op jit(solution)/shard_map/ppermute | solution.py:27
  196.0 33.8 %collective-permute-start.30 = (bf16[512,704]{0,1:T(8,128)(2,1)}, bf16[512,704]{0,1:T(8,128)(2,1)}, u32[]{:S(2)}, u32[]{:S(2)}) collective-permute-start(bf16[512,704]{0,1:T(8,128)(2,1)} %copy.128), channel_id=1, source_target_pairs={{0,4},{4,0},{8,12},{12,8},{16,20},{20,16},{24,28},{28,24},{1,5},{5... | collective-permute-start | bytes 2162696 | tf_op jit(solution)/shard_map/ppermute | solution.py:27
  199.9 36.7 %collective-permute-start.37 = (bf16[512,704]{0,1:T(8,128)(2,1)}, bf16[512,704]{0,1:T(8,128)(2,1)}, u32[]{:S(2)}, u32[]{:S(2)}) collective-permute-start(bf16[512,704]{0,1:T(8,128)(2,1)} %copy.128), channel_id=1, source_target_pairs={{0,2},{1,3},{2,0},{3,1},{4,6},{5,7},{6,4},{7,5},{8,10},{9,11},{10,... | collective-permute-start | bytes 2162696 | tf_op jit(solution)/shard_map/ppermute | solution.py:27
  210.8 48.2 %collective-permute-start.17 = (bf16[512,1024]{1,0:T(8,128)(2,1)}, bf16[512,1024]{1,0:T(8,128)(2,1)}, u32[]{:S(2)}, u32[]{:S(2)}) collective-permute-start(bf16[512,1024]{1,0:T(8,128)(2,1)} %multiply_convert_fusion), channel_id=1, source_target_pairs={{0,1},{1,0},{2,3},{3,2},{4,5},{5,4},{6,7},{7,6},{8,9},{9,8},{10,11... | collective-permute-start | bytes 3145736 | tf_op jit(solution)/shard_map/ppermute | solution.py:27
  224.6 18.5 %collective-permute-start.32 = (bf16[256,704]{1,0:T(8,128)(2,1)}, bf16[256,704]{1,0:T(8,128)(2,1)}, u32[]{:S(2)}, u32[]{:S(2)}) collective-permute-start(bf16[256,704]{1,0:T(8,128)(2,1)} %slice.503), channel_id=1, source_target_pairs={{0,4},{4,0},{8,12},{12,8},{16,20},{20,16},{24,28},{28,24},{1,5},{5... | collective-permute-start | bytes 1081352 | tf_op jit(solution)/shard_map/ppermute | solution.py:27
  292.1 46.9 %collective-permute-start.92 = (bf16[256,704]{0,1:T(8,128)(2,1)}, bf16[256,704]{0,1:T(8,128)(2,1)}, u32[]{:S(2)}, u32[]{:S(2)}) collective-permute-start(bf16[256,704]{0,1:T(8,128)(2,1)} %get-tuple-element.153), channel_id=1, source_target_pairs={{0,2},{1,3},{2,0},{3,1},{4,6},{5,7},{6,4},{7,5},{8,10},{9,11},{10,... | collective-permute-start | bytes 1081352 | tf_op jit(solution)/shard_map/ppermute | solution.py:27
  293.9 48.2 %collective-permute-start.94 = (bf16[256,704]{0,1:T(8,128)(2,1)}, bf16[256,704]{0,1:T(8,128)(2,1)}, u32[]{:S(2)}, u32[]{:S(2)}) collective-permute-start(bf16[256,704]{0,1:T(8,128)(2,1)} %get-tuple-element.155), channel_id=1, source_target_pairs={{0,4},{4,0},{8,12},{12,8},{16,20},{20,16},{24,28},{28,24},{1,5},{5... | collective-permute-start | bytes 1081352 | tf_op jit(solution)/shard_map/ppermute | solution.py:27
  295.3 59.6 %collective-permute-start.96 = (bf16[256,704]{0,1:T(8,128)(2,1)}, bf16[256,704]{0,1:T(8,128)(2,1)}, u32[]{:S(2)}, u32[]{:S(2)}) collective-permute-start(bf16[256,704]{0,1:T(8,128)(2,1)} %get-tuple-element.154), channel_id=1, source_target_pairs={{0,2},{1,3},{2,0},{3,1},{4,6},{5,7},{6,4},{7,5},{8,10},{9,11},{10,... | collective-permute-start | bytes 1081352 | tf_op jit(solution)/shard_map/ppermute | solution.py:27
  299.9 55.7 %collective-permute-start.91 = (bf16[256,704]{0,1:T(8,128)(2,1)}, bf16[256,704]{0,1:T(8,128)(2,1)}, u32[]{:S(2)}, u32[]{:S(2)}) collective-permute-start(bf16[256,704]{0,1:T(8,128)(2,1)} %slice.582), channel_id=1, source_target_pairs={{0,4},{4,0},{8,12},{12,8},{16,20},{20,16},{24,28},{28,24},{1,5},{5... | collective-permute-start | bytes 1081352 | tf_op jit(solution)/shard_map/ppermute | solution.py:27
  311.3 33.3 %collective-permute-start.83 = (bf16[256,704]{0,1:T(8,128)(2,1)}, bf16[256,704]{0,1:T(8,128)(2,1)}, u32[]{:S(2)}, u32[]{:S(2)}) collective-permute-start(bf16[256,704]{0,1:T(8,128)(2,1)} %get-tuple-element.156), channel_id=1, source_target_pairs={{0,2},{1,3},{2,0},{3,1},{4,6},{5,7},{6,4},{7,5},{8,10},{9,11},{10,... | collective-permute-start | bytes 1081352 | tf_op jit(solution)/shard_map/ppermute | solution.py:27
  354.9 19.1 %collective-permute-start.82 = (bf16[256,704]{0,1:T(8,128)(2,1)S(1)}, bf16[256,704]{0,1:T(8,128)(2,1)S(1)}, u32[]{:S(2)}, u32[]{:S(2)}) collective-permute-start(bf16[256,704]{0,1:T(8,128)(2,1)S(1)} %copy-done.70), channel_id=1, source_target_pairs={{0,4},{4,0},{8,12},{12,8},{16,20},{20,16},{24,28},{28,24},{1,5},{5... | collective-permute-start | bytes 1081352 | tf_op jit(solution)/shard_map/ppermute | solution.py:27
  355.6 19.8 %collective-permute-start.87 = (bf16[256,704]{0,1:T(8,128)(2,1)S(1)}, bf16[256,704]{0,1:T(8,128)(2,1)S(1)}, u32[]{:S(2)}, u32[]{:S(2)}) collective-permute-start(bf16[256,704]{0,1:T(8,128)(2,1)S(1)} %copy-done.72), channel_id=1, source_target_pairs={{0,2},{1,3},{2,0},{3,1},{4,6},{5,7},{6,4},{7,5},{8,10},{9,11},{10,... | collective-permute-start | bytes 1081352 | tf_op jit(solution)/shard_map/ppermute | solution.py:27
  358.5 23.2 %collective-permute-start.84 = (bf16[256,704]{0,1:T(8,128)(2,1)S(1)}, bf16[256,704]{0,1:T(8,128)(2,1)S(1)}, u32[]{:S(2)}, u32[]{:S(2)}) collective-permute-start(bf16[256,704]{0,1:T(8,128)(2,1)S(1)} %add_convert_fusion.5), channel_id=1, source_target_pairs={{0,4},{4,0},{8,12},{12,8},{16,20},{20,16},{24,28},{28,24},{1,5},{5... | collective-permute-start | bytes 1081352 | tf_op jit(solution)/shard_map/ppermute | solution.py:27
  366.3 23.2 %collective-permute-start.73 = (bf16[256,704]{0,1:T(8,128)(2,1)S(1)}, bf16[256,704]{0,1:T(8,128)(2,1)S(1)}, u32[]{:S(2)}, u32[]{:S(2)}) collective-permute-start(bf16[256,704]{0,1:T(8,128)(2,1)S(1)} %slice.560), channel_id=1, source_target_pairs={{0,4},{4,0},{8,12},{12,8},{16,20},{20,16},{24,28},{28,24},{1,5},{5... | collective-permute-start | bytes 1081352 | tf_op jit(solution)/shard_map/ppermute | solution.py:27
  375.4 18.9 %collective-permute-start.75 = (bf16[256,704]{0,1:T(8,128)(2,1)S(1)}, bf16[256,704]{0,1:T(8,128)(2,1)S(1)}, u32[]{:S(2)}, u32[]{:S(2)}) collective-permute-start(bf16[256,704]{0,1:T(8,128)(2,1)S(1)} %add_convert_fusion.7), channel_id=1, source_target_pairs={{0,4},{4,0},{8,12},{12,8},{16,20},{20,16},{24,28},{28,24},{1,5},{5... | collective-permute-start | bytes 1081352 | tf_op jit(solution)/shard_map/ppermute | solution.py:27
  383.2 57.2 %collective-permute-start.41 = (bf16[512,1024]{1,0:T(8,128)(2,1)S(1)}, bf16[512,1024]{1,0:T(8,128)(2,1)S(1)}, u32[]{:S(2)}, u32[]{:S(2)}) collective-permute-start(bf16[512,1024]{1,0:T(8,128)(2,1)S(1)} %slice.667), channel_id=1, source_target_pairs={{0,1},{1,0},{2,3},{3,2},{4,5},{5,4},{6,7},{7,6},{8,9},{9,8},{10,11... | collective-permute-start | bytes 3145736 | tf_op jit(solution)/shard_map/ppermute | solution.py:27
  389.4 55.6 %collective-permute-start.40 = (bf16[512,1024]{1,0:T(8,128)(2,1)S(1)}, bf16[512,1024]{1,0:T(8,128)(2,1)S(1)}, u32[]{:S(2)}, u32[]{:S(2)}) collective-permute-start(bf16[512,1024]{1,0:T(8,128)(2,1)S(1)} %slice.668), channel_id=1, source_target_pairs={{0,1},{1,0},{2,3},{3,2},{4,5},{5,4},{6,7},{7,6},{8,9},{9,8},{10,11... | collective-permute-start | bytes 3145736 | tf_op jit(solution)/shard_map/ppermute | solution.py:27
  394.3 18.2 %collective-permute-start.98 = (bf16[128,704]{0,1:T(8,128)(2,1)S(1)}, bf16[128,704]{0,1:T(8,128)(2,1)S(1)}, u32[]{:S(2)}, u32[]{:S(2)}) collective-permute-start(bf16[128,704]{0,1:T(8,128)(2,1)S(1)} %get-tuple-element.167), channel_id=1, source_target_pairs={{0,16},{4,20},{8,24},{12,28},{16,0},{20,4},{24,8},{28,12},{1,17},{... | collective-permute-start | bytes 540680 | tf_op jit(solution)/shard_map/ppermute | solution.py:27
  394.6 17.9 %collective-permute-start.99 = (bf16[128,704]{0,1:T(8,128)(2,1)S(1)}, bf16[128,704]{0,1:T(8,128)(2,1)S(1)}, u32[]{:S(2)}, u32[]{:S(2)}) collective-permute-start(bf16[128,704]{0,1:T(8,128)(2,1)S(1)} %get-tuple-element.166), channel_id=1, source_target_pairs={{0,24},{4,28},{8,16},{12,20},{16,8},{20,12},{24,0},{28,4},{1,25},{... | collective-permute-start | bytes 540680 | tf_op jit(solution)/shard_map/ppermute | solution.py:27
  449.3 56.7 %collective-permute-start.64 = (bf16[256,256]{1,0:T(8,128)(2,1)}, bf16[256,256]{1,0:T(8,128)(2,1)}, u32[]{:S(2)}, u32[]{:S(2)}) collective-permute-start(bf16[256,256]{1,0:T(8,128)(2,1)} %slice.548), channel_id=1, source_target_pairs={{0,4},{4,0},{8,12},{12,8},{16,20},{20,16},{24,28},{28,24},{1,5},{5... | collective-permute-start | bytes 393224 | tf_op jit(solution)/shard_map/ppermute | solution.py:27
  452.1 22.0 %collective-permute-start.65 = (bf16[256,256]{1,0:T(8,128)(2,1)}, bf16[256,256]{1,0:T(8,128)(2,1)}, u32[]{:S(2)}, u32[]{:S(2)}) collective-permute-start(bf16[256,256]{1,0:T(8,128)(2,1)} %get-tuple-element.174), channel_id=1, source_target_pairs={{0,2},{1,3},{2,0},{3,1},{4,6},{5,7},{6,4},{7,5},{8,10},{9,11},{10,... | collective-permute-start | bytes 393224 | tf_op jit(solution)/shard_map/ppermute | solution.py:27
  453.7 22.8 %collective-permute-start.67 = (bf16[256,256]{1,0:T(8,128)(2,1)}, bf16[256,256]{1,0:T(8,128)(2,1)}, u32[]{:S(2)}, u32[]{:S(2)}) collective-permute-start(bf16[256,256]{1,0:T(8,128)(2,1)} %get-tuple-element.176), channel_id=1, source_target_pairs={{0,4},{4,0},{8,12},{12,8},{16,20},{20,16},{24,28},{28,24},{1,5},{5... | collective-permute-start | bytes 393224 | tf_op jit(solution)/shard_map/ppermute | solution.py:27
  454.2 51.8 %collective-permute-start.69 = (bf16[256,256]{1,0:T(8,128)(2,1)}, bf16[256,256]{1,0:T(8,128)(2,1)}, u32[]{:S(2)}, u32[]{:S(2)}) collective-permute-start(bf16[256,256]{1,0:T(8,128)(2,1)} %get-tuple-element.175), channel_id=1, source_target_pairs={{0,2},{1,3},{2,0},{3,1},{4,6},{5,7},{6,4},{7,5},{8,10},{9,11},{10,... | collective-permute-start | bytes 393224 | tf_op jit(solution)/shard_map/ppermute | solution.py:27
  475.2 30.8 %collective-permute-start.66 = (bf16[256,256]{1,0:T(8,128)(2,1)S(1)}, bf16[256,256]{1,0:T(8,128)(2,1)S(1)}, u32[]{:S(2)}, u32[]{:S(2)}) collective-permute-start(bf16[256,256]{1,0:T(8,128)(2,1)S(1)} %add_convert_fusion.9), channel_id=1, source_target_pairs={{0,4},{4,0},{8,12},{12,8},{16,20},{20,16},{24,28},{28,24},{1,5},{5... | collective-permute-start | bytes 393224 | tf_op jit(solution)/shard_map/ppermute | solution.py:27
  477.5 28.5 %collective-permute-start.68 = (bf16[256,256]{1,0:T(8,128)(2,1)S(1)}, bf16[256,256]{1,0:T(8,128)(2,1)S(1)}, u32[]{:S(2)}, u32[]{:S(2)}) collective-permute-start(bf16[256,256]{1,0:T(8,128)(2,1)S(1)} %add_convert_fusion.8), channel_id=1, source_target_pairs={{0,2},{1,3},{2,0},{3,1},{4,6},{5,7},{6,4},{7,5},{8,10},{9,11},{10,... | collective-permute-start | bytes 393224 | tf_op jit(solution)/shard_map/ppermute | solution.py:27
  509.0 38.8 %collective-permute-start.70 = (bf16[128,256]{1,0:T(8,128)(2,1)}, bf16[128,256]{1,0:T(8,128)(2,1)}, u32[]{:S(2)}, u32[]{:S(2)}) collective-permute-start(bf16[128,256]{1,0:T(8,128)(2,1)} %get-tuple-element.181), channel_id=1, source_target_pairs={{0,8},{4,12},{8,0},{12,4},{16,24},{20,28},{24,16},{28,20},{1,9},{5... | collective-permute-start | bytes 196616 | tf_op jit(solution)/shard_map/ppermute | solution.py:27
  518.2 20.0 %collective-permute-start.60 = (bf16[256,768]{0,1:T(8,128)(2,1)}, bf16[256,768]{0,1:T(8,128)(2,1)}, u32[]{:S(2)}, u32[]{:S(2)}) collective-permute-start(bf16[256,768]{0,1:T(8,128)(2,1)} %get-tuple-element.151), channel_id=1, source_target_pairs={{0,2},{1,3},{2,0},{3,1},{4,6},{5,7},{6,4},{7,5},{8,10},{9,11},{10,... | collective-permute-start | bytes 1179656 | tf_op jit(solution)/shard_map/ppermute | solution.py:27
  520.2 18.8 %collective-permute-start.55 = (bf16[256,768]{0,1:T(8,128)(2,1)}, bf16[256,768]{0,1:T(8,128)(2,1)}, u32[]{:S(2)}, u32[]{:S(2)}) collective-permute-start(bf16[256,768]{0,1:T(8,128)(2,1)} %slice.529), channel_id=1, source_target_pairs={{0,4},{4,0},{8,12},{12,8},{16,20},{20,16},{24,28},{28,24},{1,5},{5... | collective-permute-start | bytes 1179656 | tf_op jit(solution)/shard_map/ppermute | solution.py:27
  543.7 30.6 %collective-permute-start.44 = (bf16[512,1024]{1,0:T(8,128)(2,1)S(1)}, bf16[512,1024]{1,0:T(8,128)(2,1)S(1)}, u32[]{:S(2)}, u32[]{:S(2)}) collective-permute-start(bf16[512,1024]{1,0:T(8,128)(2,1)S(1)} %slice.666), channel_id=1, source_target_pairs={{0,1},{1,0},{2,3},{3,2},{4,5},{5,4},{6,7},{7,6},{8,9},{9,8},{10,11... | collective-permute-start | bytes 3145736 | tf_op jit(solution)/shard_map/ppermute | solution.py:27
  (170 other events, 1575.7 us)

commit v2 on v1

--- a/solution.py
+++ b/solution.py
@@ -8,7 +8,7 @@
 HEAD_K = 128
 HEAD_V = 256
 CHUNK = 128
-FF_ROWS = 256
+TILE = 256
 LANES = 128
 SAFE_RANGE = 60.0
 
@@ -27,69 +27,92 @@
     return lax.ppermute(array, axis, [(i, i ^ mask) for i in range(size)])
 
 
-def radices(count):
-    result = []
-    while count > 1:
-        radix = 4 if count % 4 == 0 else 2
-        result.append(radix)
-        count //= radix
+def after(array, *others):
+    return lax.optimization_barrier((array, *others))[0]
+
+
+def slow_masks():
+    mask, result = lax.axis_size("dp") // 2, []
+    while mask > 1:
+        result.append(mask)
+        mask //= 2
     return result
 
 
-def gather(part):
-    span, held = 2, part
-    for radix in radices(lax.axis_size("dp") // 2):
-        held = jnp.concatenate([held] + [swap(held, "dp", d * span) for d in range(1, radix)], axis=0)
-        span *= radix
+def gather_slow(part):
+    for mask in slow_masks():
+        part = jnp.concatenate([part, swap(part, "dp", mask)], axis=0)
+    return part
+
+
+def gather_fast(held):
     half = held.shape[0] // 2
     beside = swap(held, "dp", 1)
     pair = swap(held, "tensor", PAIR)
     pair_low = swap(pair[:half], "dp", 1)
     pair_high = swap(beside[half:], "tensor", PAIR)
-    return (held, beside), (pair, pair_low, pair_high)
-
-
-def scatter(own, pair):
-    count = own.shape[0] // 2
-    half = count // 2
-    pair_low = swap(pair[count : count + half], "dp", 1)
-    own_high = swap(pair[count + half :], "tensor", PAIR)
-    total = own[:count].astype(F32)
-    beside_low = swap(own[count : count + half], "dp", 1)
-    pair_rest = swap(pair[half:count], "tensor", PAIR)
-    beside_high = swap(
-        (own[count + half :].astype(F32) + own_high.astype(F32)).astype(BF), "dp", 1
-    )
-    pair_sum = swap((pair[:half].astype(F32) + pair_low.astype(F32)).astype(BF), "tensor", PAIR)
-    total = total + jnp.concatenate([beside_low, beside_high], axis=0).astype(F32)
-    total = total + jnp.concatenate([pair_sum, pair_rest], axis=0).astype(F32)
-    spans, span = [], 2
-    for radix in radices(lax.axis_size("dp") // 2):
-        spans.append((radix, span))
-        span *= radix
-    for radix, span in reversed(spans):
-        rows = total.shape[0] // radix
-        low = total.astype(BF)
-        arrived = [swap(low[d * rows : (d + 1) * rows], "dp", d * span) for d in range(1, radix)]
-        total = total[:rows] + sum(a.astype(F32) for a in arrived)
+    return held, beside, pair, pair_low, pair_high
+
+
+def send_first(own, pair):
+    low = swap(pair[2], "dp", 1)
+    high = swap(pair[3], "tensor", PAIR)
+    beside_low = swap(own[2], "dp", 1)
+    pair_rest = swap(pair[1], "tensor", PAIR)
+    return low, high, beside_low, pair_rest
+
+
+def send_second(own, pair, first, *others):
+    low, high, beside_low, pair_rest = first
+    if others:
+        low, high = after(low, *others), after(high, *others)
+    beside_high = swap((own[3].astype(F32) + high.astype(F32)).astype(BF), "dp", 1)
+    pair_sum = swap((pair[0].astype(F32) + low.astype(F32)).astype(BF), "tensor", PAIR)
+    return [
+        own[0].astype(F32) + beside_low.astype(F32) + pair_sum.astype(F32),
+        own[1].astype(F32) + beside_high.astype(F32) + pair_rest.astype(F32),
+    ]
+
+
+def send_slow(kept, given, mask):
+    return kept + swap(given.astype(BF), "dp", mask).astype(F32)
+
+
+def scatter_slow(halves, *others):
+    total, given = halves
+    if others:
+        given = after(given, *others)
+    masks = slow_masks()[::-1]
+    total = send_slow(total, given, masks[0])
+    for mask in masks[1:]:
+        rows = total.shape[0] // 2
+        total = send_slow(total[:rows], total[rows:], mask)
     return total
 
 
+def slot_owner(slot):
+    count = lax.axis_size("dp")
+    bits = count.bit_length() - 1
+    delta = sum(((slot >> i) & 1) << (bits - 1 - i) for i in range(bits))
+    return delta ^ lax.axis_index("dp")
+
+
 def place_matrix(width):
-    count = lax.axis_size("dp")
-    block = width // count
+    block = width // lax.axis_size("dp")
     feature = lax.broadcasted_iota(jnp.int32, (width, width), 0)
     place = lax.broadcasted_iota(jnp.int32, (width, width), 1)
-    slot = place // block
-    owner = (slot % (count // 2) * 2 + slot // (count // 2)) ^ lax.axis_index("dp")
-    return (feature == owner * block + place % block).astype(BF)
-
-
-def block_matrix():
+    return (feature == slot_owner(place // block) * block + place % block).astype(BF)
+
+
+def small_places(width, length, groups):
     count = lax.axis_size("dp")
-    owner = lax.broadcasted_iota(jnp.int32, (count, count), 0)
-    slot = lax.broadcasted_iota(jnp.int32, (count, count), 1)
-    return (owner == ((slot % (count // 2) * 2 + slot // (count // 2)) ^ lax.axis_index("dp"))).astype(F32)
+    block, deep = width // count, length // count
+    place = lax.broadcasted_iota(jnp.int32, (width, length), 0)
+    entry = lax.broadcasted_iota(jnp.int32, (width, length), 1)
+    inside, room = place % block, block // groups
+    held = inside % room < deep // groups
+    stands = slot_owner(place // block) * deep + inside // room * (deep // groups) + inside % room
+    return (held & (entry == stands)).astype(BF)
 
 
 def contract_rows(former, latter):
@@ -192,7 +215,7 @@
 
     for h, (q_ref, _, v_ref, g_ref, out) in enumerate(heads):
         cum = cums[:, h * HEAD_K : (h + 1) * HEAD_K]
-        state = (starts[0, h] + jnp.exp(passed[h]) * arrived[h]).astype(BF)
+        state = (starts[0, h] + jnp.exp(passed[h]) * arrived[h].astype(F32)).astype(BF)
         full[0, h] = state
         passed[h] = passed[h] + cum[CHUNK - 1 :, :]
         q = q_ref[...].astype(BF).astype(F32)
@@ -244,7 +267,7 @@
 
 def mix_back_kernel(
     shift, q_own, k_own, v_own, low, q_pair, k_pair, v_pair, cums, logits, full, ends, arrived, up,
-    d_mixed, d_gate, back_own, back_pair, d_up, d_bias, d_q, d_k, scores, grads, passed,
+    d_mixed, d_gate, back_own, back_pair, d_up, d_bias, d_q, d_k, d_cum, scores, grads, passed,
 ):
     n = pl.program_id(0)
 
@@ -272,8 +295,9 @@
             q_faded, k_faded = (q * rise).astype(BF), (k * fall).astype(BF)
             scores[h] = jnp.where(row >= col, contract_last(q_faded, k_faded), 0.0)
             strict = jnp.where(row > col, grads[h], 0.0).astype(BF)
-            d_q[h] = project(strict, k_faded) * rise
-            d_k[h] = contract_rows(strict, q_faded) * fall
+            q_part, k_part = project(strict, k_faded), contract_rows(strict, q_faded)
+            d_q[h], d_k[h] = q_part * rise, k_part * fall
+            d_cum[h] = q_faded.astype(F32) * q_part - k_faded.astype(F32) * k_part
 
     @pl.when(lowest <= -SAFE_RANGE)
     def _():
@@ -284,14 +308,17 @@
             scores[h] = jnp.where(row == col, jnp.sum(q * k, axis=1, keepdims=True), 0.0)
             d_q[h] = jnp.zeros((CHUNK, HEAD_K), F32)
             d_k[h] = jnp.zeros((CHUNK, HEAD_K), F32)
+            d_cum[h] = jnp.zeros((CHUNK, HEAD_K), F32)
 
             def level(step, carry):
                 fade, mask = level_terms(cum, jnp.int32(1) << step)
                 q_faded, k_faded = (q * fade).astype(BF), (k * fade).astype(BF)
                 scores[h] = scores[h] + jnp.where(mask, contract_last(q_faded, k_faded), 0.0)
                 crossing = jnp.where(mask, grads[h], 0.0).astype(BF)
-                d_q[h] = d_q[h] + project(crossing, k_faded) * fade
-                d_k[h] = d_k[h] + contract_rows(crossing, q_faded) * fade
+                q_part, k_part = project(crossing, k_faded), contract_rows(crossing, q_faded)
+                d_q[h] = d_q[h] + q_part * fade
+                d_k[h] = d_k[h] + k_part * fade
+                d_cum[h] = d_cum[h] + q_faded.astype(F32) * q_part - k_faded.astype(F32) * k_part
                 return carry
 
             lax.fori_loop(0, CHUNK.bit_length() - 1, level, 0)
@@ -306,22 +333,21 @@
         q = q_ref[...].astype(BF).astype(F32)
         k = k_ref[...].astype(BF).astype(F32)
         v, back, state = v_ref[...].astype(BF), d_mixed[:, wide], full[0, h]
-        state_grad = ends[0, h] + jnp.exp(passed[h]) * arrived[h]
+        state_grad = ends[0, h] + jnp.exp(passed[h]) * arrived[h].astype(F32)
         passed[h] = passed[h] + closing
         low_grad = state_grad.astype(BF)
         fade = jnp.exp(closing - cum)
-        q_strict = d_q[h] + project(back, state) * jnp.exp(cum)
+        q_state = project(back, state) * jnp.exp(cum)
         k_state = project(v, low_grad) * fade
-        k_strict = d_k[h] + k_state
         diagonal = jnp.sum(jnp.where(row == col, grads[h], 0.0), axis=1, keepdims=True)
         d_v = contract_rows(scores[h].astype(BF), back) + contract_last((k * fade).astype(BF), low_grad)
         d_closing = jnp.sum(k * k_state, axis=0, keepdims=True) + jnp.exp(closing) * jnp.sum(
             state.astype(F32) * state_grad, axis=0, keepdims=True
         )
-        d_decay = exact(later, q * q_strict - k * k_strict) + d_closing
+        d_decay = exact(later, d_cum[h] + q * q_state - k * k_state) + d_closing
         d_logit = d_decay * (jax.nn.sigmoid(-logits[:, columns]) / NORMALIZER)
-        out[:, :HEAD_K] = (q_strict + diagonal * k).astype(BF)
-        out[:, HEAD_K : 2 * HEAD_K] = (k_strict + diagonal * q).astype(BF)
+        out[:, :HEAD_K] = (d_q[h] + q_state + diagonal * k).astype(BF)
+        out[:, HEAD_K : 2 * HEAD_K] = (d_k[h] + k_state + diagonal * q).astype(BF)
         out[:, 2 * HEAD_K : 2 * HEAD_K + HEAD_V] = d_v.astype(BF)
         out[:, 2 * HEAD_K + HEAD_V : 2 * HEAD_K + 2 * HEAD_V] = d_gate[:, wide]
         low_logit = d_logit.astype(BF)
@@ -373,6 +399,7 @@
 HEADS_WIDE = ((CHUNK, 2 * HEAD_V), "t", 0)
 STATE = ((2, HEAD_V, HEAD_K), "w", 0)
 SQUARES = pltpu.VMEM((2, CHUNK, CHUNK), F32)
+NARROWS = pltpu.VMEM((2, CHUNK, HEAD_K), F32)
 MEMORY = pltpu.VMEM((2, HEAD_V, HEAD_K), F32)
 PASSED = pltpu.VMEM((2, 1, HEAD_K), F32)
 UP = ((2, LANES, HEAD_K), "w", 0)
@@ -394,7 +421,7 @@
         (own, own, pair, pair, own, up, bias),
         shift,
     )
-    arrived = lax.ppermute(end[::-1], "tensor", RISE)
+    arrived = lax.ppermute(end[::-1].astype(BF), "tensor", RISE)
     gated_own, gated_pair, mixed, full = call(
         mix_kernel,
         steps,
@@ -423,7 +450,7 @@
         shift,
         backward=True,
     )
-    arrived = lax.ppermute(first[::-1], "tensor", FALL)
+    arrived = lax.ppermute(first[::-1].astype(BF), "tensor", FALL)
     back_own, back_pair, d_up, d_bias = call(
         mix_back_kernel,
         steps,
@@ -434,46 +461,276 @@
             (UP, F32),
             (BIAS, F32),
         ],
-        [pltpu.VMEM((2, CHUNK, HEAD_K), F32), pltpu.VMEM((2, CHUNK, HEAD_K), F32), SQUARES, SQUARES, PASSED],
+        [NARROWS, NARROWS, NARROWS, SQUARES, SQUARES, PASSED],
         12 << 30,
         (own, own, own, own, pair, pair, pair, cums, logits, full, ends, arrived, up, d_mixed, d_gate),
         shift,
         backward=True,
     )
-    return back_own, back_pair, d_up, d_bias, d_gain
-
-
-def hidden_kernel(rows, cot, *refs):
-    for h in range(2):
-        gate_w, up_w, down_w = refs[3 * h : 3 * h + 3]
-        hidden, d_gate, d_up = refs[6 + 3 * h : 9 + 3 * h]
-        gate = project(rows[...], gate_w[...])
-        up = project(rows[...], up_w[...])
-        grad = project(cot[...], down_w[...])
-        sigmoid = jax.nn.sigmoid(gate)
-        silu = gate * sigmoid
-        hidden[...] = (silu * up).astype(BF)
-        d_up[...] = (grad * silu).astype(BF)
-        d_gate[...] = (grad * up * sigmoid * (1.0 + gate * (1.0 - sigmoid))).astype(BF)
-
-
-def hidden_products(rows, cot, weights):
+    return back_own, back_pair, d_up, d_bias, d_gain, (d_gain, d_bias)
+
+
+def matmul_call(kernel, steps, ins, outs, arrays, flops):
+    return pl.pallas_call(
+        kernel,
+        grid=(steps,),
+        in_specs=[pl.BlockSpec(shape, index) for shape, index in ins],
+        out_specs=[pl.BlockSpec(shape, index) for (shape, index), _ in outs],
+        out_shape=[shape for _, shape in outs],
+        compiler_params=pltpu.CompilerParams(vmem_limit_bytes=56 << 20),
+        cost_estimate=pl.CostEstimate(flops=flops, bytes_accessed=16 << 20, transcendentals=0),
+    )(*arrays)
+
+
+def fixed(array):
+    return array.shape, lambda n: (0,) * array.ndim
+
+
+def by_rows(rows, array, start=0):
+    return (rows,) + array.shape[1:], lambda n: (n + start, 0)
+
+
+def struct(rows, columns, kind):
+    return jax.ShapeDtypeStruct((rows, columns), kind)
+
+
+def split_rows(x):
+    half, quarter = x.shape[1] // 2, x.shape[1] // 4
+    return x[:, :half], x[:, half : half + quarter], x[:, half + quarter :]
+
+
+def own_product(x, pieces, start, stop):
+    half = x.shape[1] // 2
+    return project(x[:, :half], pieces[0][:, start:stop]) + project(x[:, half:], pieces[1][:, start:stop])
+
+
+def pair_product(x, pieces, start, stop):
+    first, second, third = split_rows(x)
+    return (
+        project(first, pieces[2][:, start:stop])
+        + project(second, pieces[3][:, start:stop])
+        + project(third, pieces[4][:, start:stop])
+    )
+
+
+def project_in(rows, pieces, used):
+    tokens = rows.shape[0]
+    columns = pieces[0].shape[1]
+    tile = min(TILE, tokens)
+
+    def kernel(x_ref, *refs):
+        own, pair = refs[5:]
+        x = x_ref[...]
+        own[...] = own_product(x, refs, 0, columns)
+        pair[...] = pair_product(x, refs, 0, used)
+
+    outs = [struct(tokens, columns, F32), struct(tokens, used, F32)]
+    return matmul_call(
+        kernel,
+        tokens // tile,
+        [by_rows(tile, rows)] + [fixed(p) for p in pieces],
+        [(by_rows(tile, o), o) for o in outs],
+        (rows, *pieces),
+        4 * tokens * rows.shape[1] * columns,
+    )
+
+
+def project_out(own, pair, pieces, start, kind, part):
+    tokens, width = own.shape[0] // 2, 2 * pieces[0].shape[0]
+    tile = min(TILE, tokens)
+    half, quarter = width // 2, width // 4
+    own_stop, pair_stop = start + own.shape[1], start + pair.shape[1]
+
+    def kernel(own_ref, pair_ref, a, b, c, d, e, out):
+        mine, other = own_ref[...], pair_ref[...]
+        out[:, :half] = (
+            contract_last(mine, a[:, start:own_stop]) + contract_last(other, c[:, start:pair_stop])
+        ).astype(kind)
+        out[:, half : half + quarter] = (
+            contract_last(mine, b[:quarter, start:own_stop]) + contract_last(other, d[:, start:pair_stop])
+        ).astype(kind)
+        out[:, half + quarter :] = (
+            contract_last(mine, b[quarter:, start:own_stop]) + contract_last(other, e[:, start:pair_stop])
+        ).astype(kind)
+
+    steps = tokens // tile
+    out = struct(tokens, width, kind)
+    return matmul_call(
+        kernel,
+        steps,
+        [by_rows(tile, own, part * steps), by_rows(tile, pair, part * steps)] + [fixed(p) for p in pieces],
+        [(by_rows(tile, out), out)],
+        (own, pair, *pieces),
+        4 * tokens * width * own.shape[1],
+    )[0]
+
+
+def hidden_products(rows, cot, pieces, down, start):
     tokens, width = rows.shape
-    units = weights[0].shape[1]
-    tile = min(FF_ROWS, tokens)
-    by_row = pl.BlockSpec((tile, width), lambda n: (n, 0))
-    fixed = pl.BlockSpec((width, units), lambda n: (0, 0))
-    return pl.pallas_call(
-        hidden_kernel,
-        grid=(tokens // tile,),
-        in_specs=[by_row, by_row] + [fixed] * 6,
-        out_specs=[pl.BlockSpec((tile, units), lambda n: (n, 0))] * 6,
-        out_shape=[jax.ShapeDtypeStruct((tokens, units), BF)] * 6,
-        compiler_params=pltpu.CompilerParams(vmem_limit_bytes=56 << 20),
-        cost_estimate=pl.CostEstimate(
-            flops=12 * tokens * width * units, bytes_accessed=24 << 20, transcendentals=0
-        ),
-    )(rows, cot, *weights)
+    units = pieces[0].shape[1] // 2
+    tile = min(TILE, tokens)
+
+    def kernel(x_ref, c_ref, *refs):
+        both, downs, outs = refs[:5], refs[5:10], refs[10:]
+        x, c = x_ref[...], c_ref[...]
+        for h, product in enumerate((own_product, pair_product)):
+            hidden, back = outs[2 * h : 2 * h + 2]
+            gate_up = product(x, both, 0, 2 * units)
+            grad = product(c, downs, start, start + units)
+            gate, up = gate_up[:, :units], gate_up[:, units:]
+            sigmoid = jax.nn.sigmoid(gate)
+            silu = gate * sigmoid
+            hidden[...] = (silu * up).astype(BF)
+            back[:, :units] = (grad * up * sigmoid * (1.0 + gate * (1.0 - sigmoid))).astype(BF)
+            back[:, units:] = (grad * silu).astype(BF)
+
+    outs = [struct(tokens, units, BF), struct(tokens, 2 * units, BF)] * 2
+    return matmul_call(
+        kernel,
+        tokens // tile,
+        [by_rows(tile, rows), by_rows(tile, cot)] + [fixed(p) for p in (*pieces, *down)],
+        [(by_rows(tile, o), o) for o in outs],
+        (rows, cot, *pieces, *down),
+        12 * tokens * width * units,
+    )
+
+
+def weight_grads(rows, own, pair, pieces=None):
+    tokens, width = rows.shape
+    quarter = width // 4
+    columns = own.shape[1]
+    weights = () if pieces is None else tuple(pieces)
+
+    def kernel(x_ref, own_ref, pair_ref, *refs):
+        n = pl.program_id(0)
+        outs = refs[len(weights) :]
+        x = x_ref[...]
+        own_grad, pair_grad = contract_rows(x, own_ref[...]), contract_rows(x, pair_ref[...])
+        for j in range(4):
+
+            @pl.when(n == j)
+            def _():
+                outs[j][...] = own_grad.astype(BF)
+                outs[4 + j][...] = pair_grad.astype(BF)
+                if weights:
+                    own_weight, pair_weight = block_of(refs, j, quarter, columns)
+                    total = own_grad * own_weight.astype(F32) + pair_grad * pair_weight.astype(F32)
+                    total = jnp.sum(total, axis=1, keepdims=True)
+                    outs[8][...] = jnp.broadcast_to(total, (quarter, LANES))
+
+    shapes = [struct(quarter, columns, BF)] * 8
+    outs = [(fixed(o), o) for o in shapes]
+    if weights:
+        total = struct(width, LANES, F32)
+        outs.append((by_rows(quarter, total), total))
+    result = matmul_call(
+        kernel,
+        4,
+        [((tokens, quarter), lambda n: (0, n)), fixed(own), fixed(pair)] + [fixed(p) for p in weights],
+        outs,
+        (rows, own, pair, *weights),
+        4 * tokens * width * columns,
+    )
+    return result[:4], result[4:8], result[8:]
+
+
+def block_of(pieces, j, quarter, columns):
+    a, b, c, d, e = pieces[:5]
+    own = (a, b)[j // 2][j % 2 * quarter : (j % 2 + 1) * quarter, :columns]
+    pair = (c[:quarter, :columns], c[quarter:, :columns], d[:, :columns], e[:, :columns])[j]
+    return own, pair
+
+
+NORM_COLUMN, MLP_COLUMN, HEAD_COLUMN, UP_COLUMN = 16, 17, 18, 32
+
+
+def mixer_weight_grads(rows, own, pair, cot, gated_own, gated_pair, pieces, gain, mlp_total, up, bias, head, places):
+    tokens, width = rows.shape
+    quarter = width // 4
+    used = pair.shape[1]
+    out_end = used + gated_own.shape[1]
+    columns = out_end + LANES
+    rank = UP_COLUMN // 2
+
+    def kernel(
+        x_ref, own_ref, pair_ref, c_ref, gated_o, gated_p, a, b, c, d, e, gain_ref, mlp_ref, up_ref, bias_ref,
+        head_ref, deep_ref, wide_ref, mine_ref, *outs,
+    ):
+        n = pl.program_id(0)
+        x, cots = x_ref[...], c_ref[...]
+        own_grad, pair_grad = contract_rows(x, own_ref[...]), contract_rows(x, pair_ref[...])
+        own_out, pair_out = contract_rows(cots, gated_o[...]), contract_rows(cots, gated_p[...])
+        column = lax.broadcasted_iota(jnp.int32, (quarter, LANES), 1)
+        line = lax.broadcasted_iota(jnp.int32, (LANES, HEAD_K), 0)
+        head_total = jnp.sum(wide_ref[...].astype(F32) * head_ref[...], axis=1, keepdims=True)
+        heads = []
+        for h in range(2):
+            entries = jnp.where(line < rank, up_ref[h], jnp.where(line == rank, bias_ref[h], 0.0))
+            entries = jnp.concatenate(
+                [jnp.zeros((UP_COLUMN, HEAD_K), F32), entries[: LANES - UP_COLUMN]], axis=0
+            ).astype(BF)
+            heads.append(contract_last(deep_ref[...], entries))
+        for j in range(4):
+
+            @pl.when(n == j)
+            def _():
+                own_weight, pair_weight = block_of((a, b, c, d, e), j, quarter, own_ref.shape[1])
+                low = own_weight[:, used:].astype(F32) * own_grad[:, used:]
+                total = (
+                    jnp.sum(own_grad[:, :used] * own_weight[:, :used].astype(F32), axis=1, keepdims=True)
+                    + jnp.sum(pair_grad * pair_weight[:, :used].astype(F32), axis=1, keepdims=True)
+                    + jnp.sum(low, axis=1, keepdims=True)
+                )
+                shared = own_grad[:, used:]
+                shared = jnp.where(column == NORM_COLUMN, total / gain_ref[...], shared)
+                shared = jnp.where(column == MLP_COLUMN, mlp_ref[...], shared)
+                shared = jnp.where(column == HEAD_COLUMN, head_total, shared)
+                mine = mine_ref[...] > 0.0
+                for h, (grad, out) in enumerate(((own_grad, own_out), (pair_grad, pair_out))):
+                    target = outs[4 * h + j]
+                    target[:, :used] = grad[:, :used].astype(BF)
+                    target[:, used:out_end] = out.astype(BF)
+                    here = mine if h == 0 else jnp.logical_not(mine)
+                    target[:, out_end:] = (jnp.where(here, shared, 0.0) + heads[h]).astype(BF)
+
+    by_columns = ((tokens, quarter), lambda n: (0, n))
+
+    def blocks(array):
+        return by_rows(quarter, array)
+
+    shapes = [struct(quarter, columns, BF)] * 8
+    deep, wide, mine = places
+    result = matmul_call(
+        kernel,
+        4,
+        [by_columns, fixed(own), fixed(pair), by_columns, fixed(gated_own), fixed(gated_pair)]
+        + [fixed(p) for p in pieces]
+        + [blocks(gain), blocks(mlp_total), fixed(up), fixed(bias), fixed(head), blocks(deep), blocks(wide), blocks(mine)],
+        [(fixed(o), o) for o in shapes],
+        (rows, own, pair, cot, gated_own, gated_pair, *pieces, gain, mlp_total, up, bias, head, deep, wide, mine),
+        4 * tokens * width * columns,
+    )
+    return result[:4], result[4:]
+
+
+def gated_grads(rows, pieces, stop):
+    tokens = rows.shape[0]
+    tile = min(TILE, tokens)
+
+    def kernel(x_ref, *refs):
+        x = x_ref[...]
+        refs[5][...] = own_product(x, refs, 0, stop)
+        refs[6][...] = pair_product(x, refs, 0, stop)
+
+    outs = [struct(tokens, stop, F32)] * 2
+    return matmul_call(
+        kernel,
+        tokens // tile,
+        [by_rows(tile, rows)] + [fixed(p) for p in pieces],
+        [(by_rows(tile, o), o) for o in outs],
+        (rows, *pieces),
+        4 * tokens * rows.shape[1] * stop,
+    )
 
 
 def norm_back(grad_out, normal, scale, gain):
@@ -481,9 +738,8 @@
     return scale * (scaled_grad - normal * jnp.mean(scaled_grad * normal, axis=-1, keepdims=True))
 
 
-def sum_cores(full):
-    half = full.shape[0] // 2
-    return full[:half].astype(F32) + swap(full[half:].astype(BF), "tensor", CORE).astype(F32)
+def add_theirs(mine, theirs):
+    return mine + swap(theirs, "tensor", CORE).astype(F32)
 
 
 def both_cores(mine):
@@ -513,154 +769,125 @@
     width = rows * count
     member = lax.axis_index("tensor")
     shift = (member % 2 * (tokens.shape[0] // CHUNK)).astype(jnp.int32).reshape(1)
-
-    def tall(array):
-        return jnp.pad(array, ((0, rows - array.shape[0]), (0, 0)))
-
-    small = [low_down, norm_gain[:, None], mlp_gain[:, None], tall(low_up[0].T), tall(rank_bias.T), tall(head_gain[:, None])]
-    small = jnp.concatenate(small, axis=1)
-    small = jnp.pad(small, ((0, 0), (0, LANES - small.shape[1])))
-    in_own, in_pair = gather(jnp.concatenate([query_weight, key_weight, value_weight, gate_weight, small], axis=1))
-    out_own, out_pair = gather(out_weight.T)
-    gate_own, gate_pair = gather(mlp_gate)
-    up_own, up_pair = gather(mlp_up)
-    down_own, down_pair = gather(mlp_down.T)
-
-    def joined(pieces, start=0, stop=None):
-        return jnp.concatenate([p[:, start:stop] for p in pieces], axis=0)
-
     used = 2 * HEAD_K + 2 * HEAD_V
-    w_in_own = joined(in_own)
-    w_in_pair = joined(in_pair, 0, used)
-    small_own = w_in_own[:, used:]
-    small_pair = joined(in_pair, used)
-    w_out_own, w_out_pair = joined(out_own), joined(out_pair)
-    w_gate_own, w_gate_pair = joined(gate_own), joined(gate_pair)
-    w_up_own, w_up_pair = joined(up_own), joined(up_pair)
-    w_down_own, w_down_pair = joined(down_own), joined(down_pair)
-
-    order = block_matrix()
-
-    def to_actual(array, start, stop, depth):
-        blocks = array[:, start:stop].reshape(count, rows, stop - start)[:, :depth].astype(F32)
-        flat = exact(order, blocks.reshape(count, depth * (stop - start)))
-        return flat.reshape(count * depth, stop - start)
-
-    def to_places(array, depth):
-        blocks = array.reshape(count, depth, array.shape[1])
-        flat = lax.dot_general(
-            order, blocks.reshape(count, -1), (((0,), (0,)), ((), ())), preferred_element_type=F32, precision=TOP_PRECISION
-        )
-        return flat.reshape(count, depth, array.shape[1])
-
-    slots = rank + 2
-    gain_one = small_own[:, rank].astype(F32)
-    gain_two = small_own[:, rank + 1].astype(F32)
-    deep = low_up.shape[2]
-    up, bias = [], []
-    for array in (small_own, small_pair):
-        head = to_actual(array, slots, slots + rank + 1, deep)
-        up.append(jnp.pad(head[:, :rank].T, ((0, LANES - rank), (0, 0))))
-        bias.append(head[:, rank][None, :])
-    up, bias = jnp.stack(up), jnp.stack(bias)
-    gain_head = to_actual(small_own, slots + rank + 1, slots + rank + 2, head_gain.shape[0]).reshape(1, -1)
+
+    def column_at(array, start, total):
+        array = array if array.ndim == 2 else array[:, None]
+        return jnp.pad(array, ((0, rows - array.shape[0]), (start, total - start - array.shape[1])))
+
+    spaced = jnp.pad(head_gain.reshape(4, -1), ((0, 0), (0, (rows - head_gain.shape[0]) // 4))).reshape(-1)
+    total = used + LANES
+    mixer_part = column_at(query_weight, 0, total)
+    for array, start in (
+        (key_weight, HEAD_K),
+        (value_weight, 2 * HEAD_K),
+        (gate_weight, 2 * HEAD_K + HEAD_V),
+        (low_down, used),
+        (norm_gain, used + NORM_COLUMN),
+        (mlp_gain, used + MLP_COLUMN),
+        (spaced, used + HEAD_COLUMN),
+        (low_up[0].T, used + UP_COLUMN),
+        (rank_bias.T, used + UP_COLUMN + rank),
+    ):
+        mixer_part = mixer_part + column_at(array, start, total)
+    mixer_held = gather_slow(mixer_part)
+    mixer_in = gather_fast(mixer_held)
+    down_held = gather_slow(after(jnp.concatenate([out_weight.T, mlp_down.T], axis=1), mixer_held))
+    down = gather_fast(after(down_held, *mixer_in[3:]))
+    up_held = gather_slow(after(jnp.concatenate([mlp_gate, mlp_up], axis=1), down_held))
+    gate_up = gather_fast(after(up_held, *down[3:]))
+    down_start = out_weight.shape[0]
 
     places = place_matrix(width)
+    deep_places = small_places(width, HEAD_K, 1)
+    wide_places = small_places(width, HEAD_V, 4)
+    place = lax.broadcasted_iota(jnp.int32, (width, LANES), 0)
+    mine_places = (place % rows // (rows // 2) == member // 2).astype(F32)
     tokens = project(tokens, places).astype(BF)
     cot_mine = project(cotangent, places).astype(BF)
     cot_rows = both_cores(cot_mine)
+
+    small_own = jnp.concatenate([p[:, used:] for p in mixer_in[:2]], axis=0)
+    small_pair = jnp.concatenate([p[:, used:] for p in mixer_in[2:]], axis=0)
+    gain_one = small_own[:, NORM_COLUMN].astype(F32)
+    gain_two = small_own[:, MLP_COLUMN].astype(F32)
+    heads = jnp.stack([contract_rows(s, deep_places) for s in (small_own, small_pair)])
+    up = jnp.pad(heads[:, UP_COLUMN : UP_COLUMN + rank], ((0, 0), (0, LANES - rank), (0, 0)))
+    bias = heads[:, UP_COLUMN + rank : UP_COLUMN + rank + 1]
+    gain_head = contract_rows(small_own[:, HEAD_COLUMN : HEAD_COLUMN + 1], wide_places)
 
     inputs = tokens.astype(F32)
     scale_one = lax.rsqrt(jnp.mean(inputs * inputs, axis=-1, keepdims=True) + NORM_EPS)
     normal_one = inputs * scale_one
     normed_rows = both_cores((normal_one * gain_one).astype(BF))
-    proj_own = project(normed_rows, w_in_own)
-    proj_pair = project(normed_rows, w_in_pair)
+    proj_own, proj_pair = project_in(normed_rows, mixer_in, used)
     gated_own, gated_pair, kept = mixer(proj_own, proj_pair, up, bias, gain_head, shift)
-    middle = inputs + sum_cores(contract_last(gated_own, w_out_own) + contract_last(gated_pair, w_out_pair))
+    theirs = project_out(gated_own, gated_pair, down, 0, BF, 1)
+    middle = inputs + add_theirs(project_out(gated_own, gated_pair, down, 0, F32, 0), theirs)
     scale_two = lax.rsqrt(jnp.mean(middle * middle, axis=-1, keepdims=True) + NORM_EPS)
     normal_two = middle * scale_two
     mlp_rows = both_cores((normal_two * gain_two).astype(BF))
 
-    hidden_own, d_gate_own, d_up_own, hidden_pair, d_gate_pair, d_up_pair = hidden_products(
-        mlp_rows, cot_rows, (w_gate_own, w_up_own, w_down_own, w_gate_pair, w_up_pair, w_down_pair)
-    )
-    grad_second = sum_cores(
-        contract_last(d_gate_own, w_gate_own)
-        + contract_last(d_gate_pair, w_gate_pair)
-        + contract_last(d_up_own, w_up_own)
-        + contract_last(d_up_pair, w_up_pair)
-    )
-    outputs = middle + sum_cores(contract_last(hidden_own, w_down_own) + contract_last(hidden_pair, w_down_pair))
-    block_out = contract_last(outputs.astype(BF), places).astype(BF)
-
-    def weight_grad(left, own, pair):
-        return scatter(contract_rows(left, own).astype(BF), contract_rows(left, pair).astype(BF))
-
-    grad_mlp_down = weight_grad(cot_rows, hidden_own, hidden_pair).T
-    grad_mlp_gate = weight_grad(mlp_rows, d_gate_own, d_gate_pair)
-    grad_mlp_up = weight_grad(mlp_rows, d_up_own, d_up_pair)
-
-    grad_mlp_gain = jnp.sum(grad_second * normal_two, axis=0)
+    hidden_own, back_gu_own, hidden_pair, back_gu_pair = hidden_products(mlp_rows, cot_rows, gate_up, down, down_start)
+    grad_down_own, grad_down_pair, _ = weight_grads(cot_rows, hidden_own, hidden_pair)
+    down_first = send_first(grad_down_own, grad_down_pair)
+    theirs = project_out(back_gu_own, back_gu_pair, gate_up, 0, BF, 1)
+    grad_second = add_theirs(project_out(back_gu_own, back_gu_pair, gate_up, 0, F32, 0), theirs)
+    grad_gu_own, grad_gu_pair, (mlp_total,) = weight_grads(mlp_rows, back_gu_own, back_gu_pair, gate_up)
+    down_second = send_second(grad_down_own, grad_down_pair, down_first, mlp_total)
+    gu_first = send_first(grad_gu_own, grad_gu_pair)
     grad_middle = cot_mine.astype(F32) + norm_back(grad_second, normal_two, scale_two, gain_two)
     mixer_cot = both_cores(grad_middle.astype(BF))
-    grad_out_weight = weight_grad(mixer_cot, gated_own, gated_pair).T
-    back_own, back_pair, d_up, d_bias, d_gain = mixer_back(
-        proj_own, proj_pair, up, gain_head, shift, kept, project(mixer_cot, w_out_own), project(mixer_cot, w_out_pair)
-    )
-    grad_normed = sum_cores(contract_last(back_own, w_in_own) + contract_last(back_pair, w_in_pair))
-    grad_norm_gain = jnp.sum(grad_normed * normal_one, axis=0)
+
+    d_own, d_pair = gated_grads(mixer_cot, down, down_start)
+    back_own, back_pair, d_up, d_bias, d_gain, marks = mixer_back(
+        proj_own, proj_pair, up, gain_head, shift, kept, d_own, d_pair
+    )
+    gu_second = send_second(grad_gu_own, grad_gu_pair, gu_first, marks[0])
+    grad_mlp_down = scatter_slow(down_second, marks[0]).T
+    grad_gu = scatter_slow(gu_second, marks[1])
+
+    own_blocks, pair_blocks = mixer_weight_grads(
+        normed_rows, back_own, back_pair, mixer_cot, gated_own, gated_pair, mixer_in,
+        jnp.broadcast_to(gain_one[:, None], (width, LANES)), mlp_total / gain_two[:, None],
+        d_up, d_bias, d_gain, (deep_places, wide_places, mine_places),
+    )
+    mixer_first = send_first(own_blocks, pair_blocks)
+    theirs = project_out(back_own, back_pair, mixer_in, 0, BF, 1)
+    grad_normed = add_theirs(project_out(back_own, back_pair, mixer_in, 0, F32, 0), theirs)
+    grad_in = scatter_slow(send_second(own_blocks, pair_blocks, mixer_first))
+
+    hidden_own = after(hidden_own, back_own)
+    theirs = project_out(hidden_own, hidden_pair, down, down_start, BF, 1)
+    outputs = middle + add_theirs(project_out(hidden_own, hidden_pair, down, down_start, F32, 0), theirs)
+    block_out = contract_last(outputs.astype(BF), places).astype(BF)
     grad_inputs = grad_middle + norm_back(grad_normed, normal_one, scale_one, gain_one)
     high = grad_inputs.astype(BF)
     rest = (grad_inputs - high.astype(F32)).astype(BF)
     grad_inputs = contract_last(high, places) + contract_last(rest, places)
 
-    grad_own = contract_rows(normed_rows, back_own).astype(BF)
-    grad_pair = contract_rows(normed_rows, back_pair).astype(BF)
-    grad_in = scatter(grad_own[:, :used], grad_pair)
-
-    quarter = rows // 4
-    shared = jnp.concatenate(
-        [
-            grad_own[:, used : used + rank].astype(F32),
-            grad_norm_gain[:, None],
-            grad_mlp_gain[:, None],
-            jnp.pad(
-                to_places(d_gain.reshape(-1, 1), head_gain.shape[0]).reshape(count, 4, -1, 1),
-                ((0, 0), (0, 0), (0, quarter - head_gain.shape[0] // 4), (0, 0)),
-            ).reshape(width, 1),
-        ],
-        axis=1,
-    )
-    half_of = lax.broadcasted_iota(jnp.int32, (width, 1), 0) % rows // (2 * quarter)
-    pieces = []
-    for h, half in ((0, member // 2), (1, 1 - member // 2)):
-        head = jnp.concatenate([d_up[h, :rank].T, d_bias[h].T], axis=1)
-        head = jnp.pad(to_places(head, deep), ((0, 0), (0, rows - deep), (0, 0))).reshape(width, rank + 1)
-        piece = jnp.concatenate([jnp.where(half_of == half, shared, 0.0), head], axis=1)
-        pieces.append(jnp.pad(piece, ((0, 0), (0, LANES - piece.shape[1]))).astype(BF))
-    small_grad = scatter(*pieces)
-    grad_low_up = small_grad[:deep, rank + 3 : 2 * rank + 3].T[None]
-    grad_rank_bias = small_grad[:deep, 2 * rank + 3][None]
+    out_end = used + down_start
+    small_grad = grad_in[:, out_end:]
+    deep, quarter = low_up.shape[2], rows // 4
     shared = small_grad + swap(small_grad.astype(BF), "tensor", CORE).astype(F32)
     shared = lax.dynamic_slice_in_dim(shared, member * quarter, quarter, 0)
 
     return (
         block_out,
         grad_inputs,
-        shared[:, rank],
+        shared[:, NORM_COLUMN],
         grad_in[:, :HEAD_K],
         grad_in[:, HEAD_K : 2 * HEAD_K],
         grad_in[:, 2 * HEAD_K : 2 * HEAD_K + HEAD_V],
-        grad_in[:, 2 * HEAD_K + HEAD_V :],
+        grad_in[:, 2 * HEAD_K + HEAD_V : used],
         shared[:, :rank],
-        grad_low_up,
-        grad_rank_bias,
-        shared[: head_gain.shape[0] // 4, rank + 2],
-        grad_out_weight,
-        shared[:, rank + 1],
-        grad_mlp_gate,
-        grad_mlp_up,
+        small_grad[:deep, UP_COLUMN : UP_COLUMN + rank].T[None],
+        small_grad[:deep, UP_COLUMN + rank][None],
+        shared[: head_gain.shape[0] // 4, HEAD_COLUMN],
+        grad_in[:, used:out_end].T,
+        shared[:, MLP_COLUMN],
+        grad_gu[:, : mlp_gate.shape[1]],
+        grad_gu[:, mlp_gate.shape[1] :],
         grad_mlp_down,
     )
 

time: 614 us -> 489 us (0.80)
  Pallas kernels: 61.9 us -> 151 us
  starting transfers between devices: 129 us -> 60.7 us
  matrix products: 83.4 us -> 15.6 us
  local copies, waits for them, and re-layouts: 134 us -> 67.9 us
    pallas_call x1 -> x14, Pallas kernels: 25.2 us -> 115 us  [matmul_call(): pl.pallas_call(kernel, grid=(steps,), in_specs=[pl.BlockSpec(shape, index...]
    ppermute x98 -> x51, starting transfers between devices: 124 us -> 56.3 us  [swap(): return lax.ppermute(array, axis, [(i, i ^ mask) for i in range(size)])]
    dot_general x13 -> x3, matrix products: 36.5 us -> 6.52 us  [contract_last(): lax.dot_general(former, latter, (((1,), (1,)), ((), ())), preferred_eleme...]
    dot_general x10 -> x3, matrix products: 28.5 us -> 4.9 us  [contract_rows(): lax.dot_general(former, latter, (((0,), (0,)), ((), ())), preferred_eleme...]
    unnamed x279 -> x180, local copies, waits for them, and re-layouts: 62.7 us -> 40.4 us
    slice x48 -> x19, local copies, waits for them, and re-layouts: 34.4 us -> 14.1 us  [the longest x3 4.15 us: gather_fast(): pair_high = swap(beside[half:], 'tensor', PAIR)]
    concatenate x13 -> x1, local copies, waits for them, and re-layouts: 14 us -> 1.08 us  [gather_slow(): part = jnp.concatenate([part, swap(part, 'dp', mask)], axis=0)]
    dot_general x6 -> x2, matrix products: 16.7 us -> 4.18 us  [project(): return jnp.dot(former, latter, preferred_element_type=F32)]
  transfers between devices with their start and end apart: 100 -> 53, of which waited for: 32 -> 19; matrix products, arithmetic and copies ran while one was open for 37% -> 20% of each run, Pallas kernels for 6% -> 26%
where the time goes in v2:
time: 489 us; the launch traced here: 481 us
  Pallas kernels  151 us (31%)
  waiting for transfers between devices  129 us (26%)
  local copies, waits for them, and re-layouts  67.9 us (14%)
  starting transfers between devices  60.7 us (12%)
  other arithmetic  53.5 us (11%)
  matrix products  15.6 us (3%)
    ppermute x51, waiting for transfers between devices, swap(): return lax.ppermute(array, axis, [(i, i ^ mask) for i in range(size)])  123 us
    pallas_call x14, Pallas kernels, matmul_call(): pl.pallas_call(kernel, grid=(steps,), in_specs=[pl.BlockSpec(shape, index...  115 us
    ppermute x51, starting transfers between devices, swap(): return lax.ppermute(array, axis, [(i, i ^ mask) for i in range(size)])  56.3 us
    unnamed x180, local copies, waits for them, and re-layouts  40.4 us
    pallas_call x4, Pallas kernels, call(): pl.pallas_call(kernel, grid_spec=pltpu.PrefetchScalarGridSpec(num_scalar_...  35.9 us
    concatenate x4, other arithmetic, both_cores(): return jnp.concatenate([mine, swap(mine, 'tensor', CORE)], axis=0)  10.2 us
  transfers between devices with their start and end apart: 53, of which 19 were waited for; matrix products, arithmetic and copies ran while one was open for 20% of the time, Pallas kernels for 26%

profile of v2, /device:TPU:0, one launch (start us, length us, event | category | flops | bytes accessed | tf_op | source)
XLA Modules:
  0.0 480.5 jit_solution(15246958935999327585)
XLA Ops:
  6.5 4.1 collective-permute-start
  10.6 10.5 %collective-permute-done = bf16[128,896]{1,0:T(8,128)(2,1)S(1)} collective-permute-done((bf16[128,896]{1,0:T(8,128)(2,1)S(1)}, bf16[128,896]{1,0:T(8,128)(2,1)S(1)}, u32[]{:S(2)}, u32[]{:S(2)}) %collective-permute-start) | collective-permute-done | bytes 229408 | tf_op jit(solution)/shard_map/ppermute | solution.py:27
  24.1 8.9 %collective-permute-done.1 = bf16[256,896]{1,0:T(8,128)(2,1)} collective-permute-done((bf16[256,896]{1,0:T(8,128)(2,1)S(1)}, bf16[256,896]{1,0:T(8,128)(2,1)}, u32[]{:S(2)}, u32[]{:S(2)}) %collective-permute-start.1) | collective-permute-done | bytes 458784 | tf_op jit(solution)/shard_map/ppermute | solution.py:27
  34.1 3.2 collective-permute-start.8
  42.2 6.7 %collective-permute-done.8 = bf16[128,960]{1,0:T(8,128)(2,1)S(1)} collective-permute-done((bf16[128,960]{1,0:T(8,128)(2,1)S(1)}, bf16[128,960]{1,0:T(8,128)(2,1)S(1)}, u32[]{:S(2)}, u32[]{:S(2)}) %collective-permute-start.8) | collective-permute-done | bytes 245792 | tf_op jit(solution)/shard_map/ppermute | solution.py:27
  54.1 8.9 %collective-permute-done.9 = bf16[256,960]{1,0:T(8,128)(2,1)} collective-permute-done((bf16[256,960]{1,0:T(8,128)(2,1)}, bf16[256,960]{1,0:T(8,128)(2,1)}, u32[]{:S(2)}, u32[]{:S(2)}) %collective-permute-start.9) | collective-permute-done | bytes 491552 | tf_op jit(solution)/shard_map/ppermute | solution.py:27
  64.1 3.2 collective-permute-start.17
  91.0 7.9 %shard_map.279 = (f32[1024,896]{1,0:T(8,128)}, f32[1024,768]{1,0:T(8,128)}) custom-call(bf16[1024,1024]{1,0:T(8,128)(2,1)} %pad_maximum_fusion.x_ref, bf16[512,896]{1,0:T(8,128)(2,1)} %copy-done.44, bf16[512,896]{1,0:T(8,128)(2,1)} %collective-permute-done.2.refs_1_.b, bf16[512,896]{1,0:T(8,128)(2,1)} %collective-permute-done.4.refs_2_.c, ...), custom_call_target="tpu_custom_call" | custom-call | flops 3758096384 | bytes 16777216 | tf_op jit(solution)/shard_map/pallas_call | solution.py:474
  102.9 9.2 %shard_map.280 = (f32[1024,256]{1,0:T(8,128)S(1)}, f32[1024,256]{1,0:T(8,128)S(1)}, f32[8,2,256,128]{3,2,1,0:T(8,128)S(1)}, f32[2,256,128]{2,1,0:T(8,128)S(1)}) custom-call(s32[1]{0:T(128)} %bitcast.1.shift, f32[1024,896]{1,0:T(8,128)S(1)} %copy-done.2, f32[1024,896]{1,0:T(8,128)S(1)} %copy-done.2, f32[1024,768]{1,0:T(8,128)S(1)} %copy-done.4, ...), custom_call_target="tpu_custom_call" | custom-call | flops 4294967296 | bytes 12582912 | tf_op jit(solution)/shard_map/pallas_call | solution.py:379
  115.5 2.9 collective-permute-start.7
  136.0 7.0 %shard_map.281 = (bf16[1024,256]{1,0:T(8,128)(2,1)S(1)}, bf16[1024,256]{1,0:T(8,128)(2,1)S(1)}, f32[1024,512]{1,0:T(8,128)S(1)}, bf16[8,2,256,128]{3,2,1,0:T(8,128)(2,1)S(1)}) custom-call(s32[1]{0:T(128)} %bitcast.1.shift, f32[1024,896]{1,0:T(8,128)S(1)} %copy-done.3, f32[1024,896]{1,0:T(8,128)S(1)} %copy-done.3, f32[1024,896]{1,0:T(8,128)S(1)} %copy-done.3, ...), custom_call_target="tpu_custom_call" | custom-call | flops 6442450944 | bytes 12582912 | tf_op jit(solution)/shard_map/pallas_call | solution.py:379
  147.8 4.2 shard_map.283
  152.1 2.4 fusion.21
  159.0 4.3 shard_map.282
  167.1 23.1 %collective-permute-done.20.refs_2_.c = bf16[512,1408]{1,0:T(8,128)(2,1)S(1)} collective-permute-done((bf16[512,1408]{1,0:T(8,128)(2,1)S(1)}, bf16[512,1408]{1,0:T(8,128)(2,1)S(1)}, u32[]{:S(2)}, u32[]{:S(2)}) %collective-permute-start.20) | collective-permute-done | bytes 1441824 | tf_op jit(solution)/shard_map/ppermute | solution.py:27
  195.5 3.0 pad_maximum_fusion.2.c_ref.x_ref
  198.6 3.0 pad_maximum_fusion.1.x_ref
  201.6 7.6 %collective-permute-done.21.refs_3_.d = bf16[256,1408]{1,0:T(8,128)(2,1)} collective-permute-done((bf16[256,1408]{1,0:T(8,128)(2,1)}, bf16[256,1408]{1,0:T(8,128)(2,1)}, u32[]{:S(2)}, u32[]{:S(2)}) %collective-permute-start.21) | collective-permute-done | bytes 720928 | tf_op jit(solution)/shard_map/ppermute | solution.py:27
  209.2 2.4 collective-permute-done.22.refs_4_.e
  211.6 17.3 %shard_map.284 = (bf16[1024,704]{1,0:T(8,128)(2,1)}, bf16[1024,1408]{1,0:T(8,128)(2,1)}, bf16[1024,704]{1,0:T(8,128)(2,1)}, bf16[1024,1408]{1,0:T(8,128)(2,1)}) custom-call(bf16[1024,1024]{1,0:T(8,128)(2,1)} %pad_maximum_fusion.1.x_ref, bf16[1024,1024]{1,0:T(8,128)(2,1)} %pad_maximum_fusion.2.c_ref.x_ref, bf16[512,1408]{1,0:T(8,128)(2,1)} %copy-done.43, ...), custom_call_target="tpu_custom_call" | custom-call | flops 8858370048 | bytes 16777216 | tf_op jit(solution)/shard_map/pallas_call | solution.py:474
  228.9 7.7 %shard_map.286 = bf16[512,1024]{1,0:T(8,128)(2,1)} custom-call(bf16[1024,1408]{1,0:T(8,128)(2,1)} %get-tuple-element.91.own_ref, bf16[1024,1408]{1,0:T(8,128)(2,1)} %get-tuple-element.92.pair_ref, bf16[512,1408]{1,0:T(8,128)(2,1)} %copy-done.43, bf16[512,1408]{1,0:T(8,128)(2,1)} %collective-permute-done.19.refs_1_.b, bf16[512,1408]{1,0:T(8,128)(2,1)} %copy-done.45, ...), custom_call_target="tpu_custom_call" | custom-call | flops 2952790016 | bytes 16777216 | tf_op jit(solution)/shard_map/pallas_call | solution.py:474
  236.6 2.4 fusion.63
  241.3 8.2 %shard_map.296 = (bf16[256,704]{1,0:T(8,128)(2,1)}, bf16[256,704]{1,0:T(8,128)(2,1)}, bf16[256,704]{1,0:T(8,128)(2,1)}, bf16[256,704]{1,0:T(8,128)(2,1)}, bf16[2...) custom-call(bf16[1024,1024]{1,0:T(8,128)(2,1)} %pad_maximum_fusion.2.c_ref.x, ...), custom_call_target="tpu_custom_call" | custom-call | flops 2952790016 | bytes 16777216 | tf_op jit(solution)/shard_map/pallas_call | solution.py:474
  252.9 7.7 %shard_map.285 = f32[512,1024]{1,0:T(8,128)} custom-call(bf16[1024,1408]{1,0:T(8,128)(2,1)} %get-tuple-element.91.own_ref, bf16[1024,1408]{1,0:T(8,128)(2,1)} %get-tuple-element.92.pair_ref, bf16[512,1408]{1,0:T(8,128)(2,1)} %copy-done.43, bf16[512,1408]{1,0:T(8,128)(2,1)} %collective-permute-done.19.refs_1_.b, bf16[512,1408]{1,0:T(8,128)(2,1)} %copy-done.45, ...), custom_call_target="tpu_custom_call" | custom-call | flops 2952790016 | bytes 16777216 | tf_op jit(solution)/shard_map/pallas_call | solution.py:474
  260.7 2.5 multiply_reduce_fusion
  263.2 3.9 fusion.91
  267.1 16.2 %shard_map.294 = (bf16[256,1408]{1,0:T(8,128)(2,1)}, bf16[256,1408]{1,0:T(8,128)(2,1)}, bf16[256,1408]{1,0:T(8,128)(2,1)}, bf16[256,1408]{1,0:T(8,128)(2,1)}, bf...) custom-call(bf16[1024,1024]{1,0:T(8,128)(2,1)} %pad_maximum_fusion.1, ...), custom_call_target="tpu_custom_call" | custom-call | flops 5905580032 | bytes 16777216 | tf_op jit(solution)/shard_map/pallas_call | solution.py:474
  292.5 3.9 collective-permute-done.49
  299.4 2.7 pad_maximum_fusion.3.x_ref.c_ref
  302.1 6.1 %shard_map.287 = (f32[1024,256]{1,0:T(8,128)}, f32[1024,256]{1,0:T(8,128)}) custom-call(bf16[1024,1024]{1,0:T(8,128)(2,1)} %pad_maximum_fusion.3.x_ref.c_ref, bf16[512,960]{1,0:T(8,128)(2,1)} %copy-done.33, bf16[512,960]{1,0:T(8,128)(2,1)} %copy.79.b.refs_6_.refs_1_, bf16[512,960]{1,0:T(8,128)(2,1)} %copy.80.c.refs_7_.refs_2_, ...), custom_call_target="tpu_custom_call" | custom-call | flops 1073741824 | bytes 16777216 | tf_op jit(solution)/shard_map/pallas_call | solution.py:474
  310.6 6.5 %shard_map.288 = (bf16[1024,512]{1,0:T(8,128)(2,1)S(1)}, bf16[1024,512]{1,0:T(8,128)(2,1)S(1)}, f32[8,2,256,128]{3,2,1,0:T(8,128)S(1)}, f32[2,256,128]{2,1,0:T(8,128)S(1)}, f32[1,256]{1,0:T(1,128)S(1)}) custom-call(s32[1]{0:T(128)} %bitcast.1.shift, f32[1024,896]{1,0:T(8,128)} %get-tuple-element.77.k_own.v_own.low.q_own.g_own, ...), custom_call_target="tpu_custom_call" | custom-call | flops 6442450944 | bytes 12582912 | tf_op jit(solution)/shard_map/pallas_call | solution.py:379
  324.1 2.5 add_convert_fusion.2
  326.6 2.4 add_convert_fusion.1
  329.0 6.7 %collective-permute-done.25.arrived = bf16[2,256,128]{2,1,0:T(8,128)(2,1)S(1)} collective-permute-done((bf16[2,256,128]{2,1,0:T(8,128)(2,1)}, bf16[2,256,128]{2,1,0:T(8,128)(2,1)S(1)}, u32[]{:S(2)}, u32[]{:S(2)}) %collective-permute-start.25) | collective-permute-done | bytes 131104 | tf_op jit(solution)/shard_map/ppermute | solution.py:453
  339.1 13.2 %shard_map.289 = (bf16[1024,896]{1,0:T(8,128)(2,1)S(1)}, bf16[1024,768]{1,0:T(8,128)(2,1)S(1)}, f32[2,128,128]{2,1,0:T(8,128)S(1)}, f32[2,1,128]{2,1,0:T(1,128)S(1)}) custom-call(s32[1]{0:T(128)} %bitcast.1.shift, f32[1024,896]{1,0:T(8,128)} %get-tuple-element.77.k_own.v_own.low.q_own.g_own, f32[1024,896]{1,0:T(8,128)} %get-tuple-element.77.k_own.v_own.low.q_own.g_own, ...), custom_call_target="tpu_custom_call" | custom-call | flops 12884901888 | bytes 12582912 | tf_op jit(solution)/shard_map/pallas_call | solution.py:379
  356.0 5.4 %shard_map.293 = bf16[512,1024]{1,0:T(8,128)(2,1)} custom-call(bf16[1024,896]{1,0:T(8,128)(2,1)} %copy-done.6, bf16[1024,768]{1,0:T(8,128)(2,1)} %copy-done.7, bf16[512,896]{1,0:T(8,128)(2,1)} %copy-done.44, bf16[512,896]{1,0:T(8,128)(2,1)} %collective-permute-done.2.refs_1_.b, bf16[512,896]{1,0:T(8,128)(2,1)} %collective-permute-done.4.refs_2_.c, ...), custom_call_target="tpu_custom_call" | custom-call | flops 1879048192 | bytes 16777216 | tf_op jit(solution)/shard_map/pallas_call | solution.py:474
  361.4 5.3 %shard_map.291 = bf16[512,1024]{1,0:T(8,128)(2,1)} custom-call(bf16[1024,704]{1,0:T(8,128)(2,1)} %get-tuple-element.101.own_ref, bf16[1024,704]{1,0:T(8,128)(2,1)} %get-tuple-element.102.pair_ref, bf16[512,960]{1,0:T(8,128)(2,1)} %copy-done.33, bf16[512,960]{1,0:T(8,128)(2,1)} %copy.79.b.refs_6_.refs_1_, bf16[512,960]{1,0:T(8,128)(2,1)} %copy.80.c.refs_7_.refs_2_, ...), custom_call_target="tpu_custom_call" | custom-call | flops 1476395008 | bytes 16777216 | tf_op jit(solution)/shard_map/pallas_call | solution.py:474
  367.7 13.9 %shard_map.295 = (bf16[256,1152]{1,0:T(8,128)(2,1)}, bf16[256,1152]{1,0:T(8,128)(2,1)}, bf16[256,1152]{1,0:T(8,128)(2,1)}, bf16[256,1152]{1,0:T(8,128)(2,1)}, bf...) custom-call(bf16[1024,1024]{1,0:T(8,128)(2,1)} %pad_maximum_fusion.x, ...), custom_call_target="tpu_custom_call" | custom-call | flops 4831838208 | bytes 16777216 | tf_op jit(solution)/shard_map/pallas_call | solution.py:474
  385.2 5.4 %shard_map.290 = f32[512,1024]{1,0:T(8,128)} custom-call(bf16[1024,704]{1,0:T(8,128)(2,1)} %get-tuple-element.101.own_ref, bf16[1024,704]{1,0:T(8,128)(2,1)} %get-tuple-element.102.pair_ref, bf16[512,960]{1,0:T(8,128)(2,1)} %copy-done.33, bf16[512,960]{1,0:T(8,128)(2,1)} %copy.79.b.refs_6_.refs_1_, bf16[512,960]{1,0:T(8,128)(2,1)} %copy.80.c.refs_7_.refs_2_, ...), custom_call_target="tpu_custom_call" | custom-call | flops 1476395008 | bytes 16777216 | tf_op jit(solution)/shard_map/pallas_call | solution.py:474
  390.6 5.8 %shard_map.292 = f32[512,1024]{1,0:T(8,128)} custom-call(bf16[1024,896]{1,0:T(8,128)(2,1)} %copy-done.6, bf16[1024,768]{1,0:T(8,128)(2,1)} %copy-done.7, bf16[512,896]{1,0:T(8,128)(2,1)} %copy-done.44, bf16[512,896]{1,0:T(8,128)(2,1)} %collective-permute-done.2.refs_1_.b, bf16[512,896]{1,0:T(8,128)(2,1)} %collective-permute-done.4.refs_2_.c, ...), custom_call_target="tpu_custom_call" | custom-call | flops 1879048192 | bytes 16777216 | tf_op jit(solution)/shard_map/pallas_call | solution.py:474
  403.3 8.0 %collective-permute-done.29 = bf16[256,1152]{1,0:T(8,128)(2,1)} collective-permute-done((bf16[256,1152]{1,0:T(8,128)(2,1)}, bf16[256,1152]{1,0:T(8,128)(2,1)}, u32[]{:S(2)}, u32[]{:S(2)}) %collective-permute-start.29) | collective-permute-done | bytes 589856 | tf_op jit(solution)/shard_map/ppermute | solution.py:27
  420.5 2.6 convolution_convert_fusion
  423.1 2.6 convolution_add_fusion
  426.5 8.8 %collective-permute-done.32 = bf16[256,1152]{1,0:T(8,128)(2,1)S(1)} collective-permute-done((bf16[256,1152]{1,0:T(8,128)(2,1)S(1)}, bf16[256,1152]{1,0:T(8,128)(2,1)S(1)}, u32[]{:S(2)}, u32[]{:S(2)}) %collective-permute-start.32) | collective-permute-done | bytes 589856 | tf_op jit(solution)/shard_map/ppermute | solution.py:27
  439.9 2.4 collective-permute-start.44
  442.3 4.9 %collective-permute-done.28 = bf16[256,1152]{1,0:T(8,128)(2,1)S(1)} collective-permute-done((bf16[256,1152]{1,0:T(8,128)(2,1)S(1)}, bf16[256,1152]{1,0:T(8,128)(2,1)S(1)}, u32[]{:S(2)}, u32[]{:S(2)}) %collective-permute-start.28) | collective-permute-done | bytes 589856 | tf_op jit(solution)/shard_map/ppermute | solution.py:27
  449.4 9.5 %collective-permute-done.34 = bf16[256,1152]{1,0:T(8,128)(2,1)S(1)} collective-permute-done((bf16[256,1152]{1,0:T(8,128)(2,1)S(1)}, bf16[256,1152]{1,0:T(8,128)(2,1)S(1)}, u32[]{:S(2)}, u32[]{:S(2)}) %collective-permute-start.34) | collective-permute-done | bytes 589856 | tf_op jit(solution)/shard_map/ppermute | solution.py:27
  462.6 10.8 %collective-permute-done.35 = bf16[128,1152]{1,0:T(8,128)(2,1)} collective-permute-done((bf16[128,1152]{1,0:T(8,128)(2,1)S(1)}, bf16[128,1152]{1,0:T(8,128)(2,1)}, u32[]{:S(2)}, u32[]{:S(2)}) %collective-permute-start.35) | collective-permute-done | bytes 294944 | tf_op jit(solution)/shard_map/ppermute | solution.py:27
  (349 shorter events, 160.3 us)
Async XLA Ops:
  6.5 14.6 %collective-permute-start = (bf16[128,896]{1,0:T(8,128)(2,1)S(1)}, bf16[128,896]{1,0:T(8,128)(2,1)S(1)}, u32[]{:S(2)}, u32[]{:S(2)}) collective-permute-start(bf16[128,896]{1,0:T(8,128)(2,1)S(1)} %pad_add_fusion), channel_id=1, source_target_pairs={{0,16},{4,20},{8,24},{12,28},{16,0},{20,4},{24,8},{28,12},{1,17},{... | collective-permute-start | bytes 688136 | tf_op jit(solution)/shard_map/ppermute | solution.py:27
  21.2 11.9 %collective-permute-start.1 = (bf16[256,896]{1,0:T(8,128)(2,1)S(1)}, bf16[256,896]{1,0:T(8,128)(2,1)}, u32[]{:S(2)}, u32[]{:S(2)}) collective-permute-start(bf16[256,896]{1,0:T(8,128)(2,1)S(1)} %pad_maximum_fusion.8), channel_id=1, source_target_pairs={{0,8},{4,12},{8,0},{12,4},{16,24},{20,28},{24,16},{28,20},{1,9},{5... | collective-permute-start | bytes 1376264 | tf_op jit(solution)/shard_map/ppermute | solution.py:27
  34.1 14.7 %collective-permute-start.8 = (bf16[128,960]{1,0:T(8,128)(2,1)S(1)}, bf16[128,960]{1,0:T(8,128)(2,1)S(1)}, u32[]{:S(2)}, u32[]{:S(2)}) collective-permute-start(bf16[128,960]{1,0:T(8,128)(2,1)S(1)} %pad_maximum_fusion.12), channel_id=1, source_target_pairs={{0,16},{4,20},{8,24},{12,28},{16,0},{20,4},{24,8},{28,12},{1,17},{... | collective-permute-start | bytes 737288 | tf_op jit(solution)/shard_map/ppermute | solution.py:27
  39.1 28.2 %collective-permute-start.4 = (bf16[512,896]{1,0:T(8,128)(2,1)S(1)}, bf16[512,896]{1,0:T(8,128)(2,1)}, u32[]{:S(2)}, u32[]{:S(2)}) collective-permute-start(bf16[512,896]{1,0:T(8,128)(2,1)S(1)} %pad_maximum_fusion.5.refs_0_.a), channel_id=1, source_target_pairs={{0,2},{1,3},{2,0},{3,1},{4,6},{5,7},{6,4},{7,5},{8,10},{9,11},{10,... | collective-permute-start | bytes 2752520 | tf_op jit(solution)/shard_map/ppermute | solution.py:27
  40.7 29.3 %collective-permute-start.2 = (bf16[512,896]{1,0:T(8,128)(2,1)S(1)}, bf16[512,896]{1,0:T(8,128)(2,1)}, u32[]{:S(2)}, u32[]{:S(2)}) collective-permute-start(bf16[512,896]{1,0:T(8,128)(2,1)S(1)} %pad_maximum_fusion.5.refs_0_.a), channel_id=1, source_target_pairs={{0,4},{4,0},{8,12},{12,8},{16,20},{20,16},{24,28},{28,24},{1,5},{5... | collective-permute-start | bytes 2752520 | tf_op jit(solution)/shard_map/ppermute | solution.py:27
  49.7 13.3 %collective-permute-start.9 = (bf16[256,960]{1,0:T(8,128)(2,1)}, bf16[256,960]{1,0:T(8,128)(2,1)}, u32[]{:S(2)}, u32[]{:S(2)}) collective-permute-start(bf16[256,960]{1,0:T(8,128)(2,1)} %pad_maximum_fusion.7), channel_id=1, source_target_pairs={{0,8},{4,12},{8,0},{12,4},{16,24},{20,28},{24,16},{28,20},{1,9},{5... | collective-permute-start | bytes 1474568 | tf_op jit(solution)/shard_map/ppermute | solution.py:27
  64.1 54.3 %collective-permute-start.17 = (bf16[128,1408]{1,0:T(8,128)(2,1)}, bf16[128,1408]{1,0:T(8,128)(2,1)}, u32[]{:S(2)}, u32[]{:S(2)}) collective-permute-start(bf16[128,1408]{1,0:T(8,128)(2,1)} %pad_maximum_fusion.10), channel_id=1, source_target_pairs={{0,16},{4,20},{8,24},{12,28},{16,0},{20,4},{24,8},{28,12},{1,17},{... | collective-permute-start | bytes 1081352 | tf_op jit(solution)/shard_map/ppermute | solution.py:27
  68.4 11.8 %collective-permute-start.5 = (bf16[256,896]{1,0:T(8,128)(2,1)S(1)}, bf16[256,896]{1,0:T(8,128)(2,1)}, u32[]{:S(2)}, u32[]{:S(2)}) collective-permute-start(bf16[256,896]{1,0:T(8,128)(2,1)S(1)} %slice.153), channel_id=1, source_target_pairs={{0,4},{4,0},{8,12},{12,8},{16,20},{20,16},{24,28},{28,24},{1,5},{5... | collective-permute-start | bytes 1376264 | tf_op jit(solution)/shard_map/ppermute | solution.py:27
  74.2 15.3 %collective-permute-start.3 = (bf16[512,1024]{1,0:T(8,128)(2,1)S(1)}, bf16[512,1024]{1,0:T(8,128)(2,1)S(1)}, u32[]{:S(2)}, u32[]{:S(2)}) collective-permute-start(bf16[512,1024]{1,0:T(8,128)(2,1)S(1)} %fusion.15), channel_id=1, source_target_pairs={{0,1},{1,0},{2,3},{3,2},{4,5},{5,4},{6,7},{7,6},{8,9},{9,8},{10,11... | collective-permute-start | bytes 3145736 | tf_op jit(solution)/shard_map/ppermute | solution.py:27
  83.8 38.1 %collective-permute-start.11 = (bf16[512,960]{0,1:T(8,128)(2,1)}, bf16[512,960]{0,1:T(8,128)(2,1)}, u32[]{:S(2)}, u32[]{:S(2)}) collective-permute-start(bf16[512,960]{0,1:T(8,128)(2,1)} %copy.75), channel_id=1, source_target_pairs={{0,2},{1,3},{2,0},{3,1},{4,6},{5,7},{6,4},{7,5},{8,10},{9,11},{10,... | collective-permute-start | bytes 2949128 | tf_op jit(solution)/shard_map/ppermute | solution.py:27
  85.3 42.4 %collective-permute-start.10 = (bf16[512,960]{0,1:T(8,128)(2,1)}, bf16[512,960]{0,1:T(8,128)(2,1)}, u32[]{:S(2)}, u32[]{:S(2)}) collective-permute-start(bf16[512,960]{0,1:T(8,128)(2,1)} %copy.75), channel_id=1, source_target_pairs={{0,4},{4,0},{8,12},{12,8},{16,20},{20,16},{24,28},{28,24},{1,5},{5... | collective-permute-start | bytes 2949128 | tf_op jit(solution)/shard_map/ppermute | solution.py:27
  115.5 15.6 %collective-permute-start.7 = (bf16[2,256,128]{2,1,0:T(8,128)(2,1)S(1)}, bf16[2,256,128]{2,1,0:T(8,128)(2,1)S(1)}, u32[]{:S(2)}, u32[]{:S(2)}) collective-permute-start(bf16[2,256,128]{2,1,0:T(8,128)(2,1)S(1)} %rev.11), channel_id=1, source_target_pairs={{0,2},{1,3},{4,6},{5,7},{8,10},{9,11},{12,14},{13,15},{16,18},{17,... | collective-permute-start | bytes 393224 | tf_op jit(solution)/shard_map/ppermute | solution.py:424
  120.5 34.5 %collective-permute-start.18 = (bf16[256,1408]{1,0:T(8,128)(2,1)}, bf16[256,1408]{1,0:T(8,128)(2,1)}, u32[]{:S(2)}, u32[]{:S(2)}) collective-permute-start(bf16[256,1408]{1,0:T(8,128)(2,1)} %pad_maximum_fusion.6), channel_id=1, source_target_pairs={{0,8},{4,12},{8,0},{12,4},{16,24},{20,28},{24,16},{28,20},{1,9},{5... | collective-permute-start | bytes 2162696 | tf_op jit(solution)/shard_map/ppermute | solution.py:27
  126.2 20.7 %collective-permute-start.12 = (bf16[256,960]{1,0:T(8,128)(2,1)}, bf16[256,960]{1,0:T(8,128)(2,1)}, u32[]{:S(2)}, u32[]{:S(2)}) collective-permute-start(bf16[256,960]{1,0:T(8,128)(2,1)} %slice.160), channel_id=1, source_target_pairs={{0,4},{4,0},{8,12},{12,8},{16,20},{20,16},{24,28},{28,24},{1,5},{5... | collective-permute-start | bytes 1474568 | tf_op jit(solution)/shard_map/ppermute | solution.py:27
  131.1 15.9 %collective-permute-start.13 = (bf16[256,960]{1,0:T(8,128)(2,1)S(1)}, bf16[256,960]{1,0:T(8,128)(2,1)S(1)}, u32[]{:S(2)}, u32[]{:S(2)}) collective-permute-start(bf16[256,960]{1,0:T(8,128)(2,1)S(1)} %slice.161), channel_id=1, source_target_pairs={{0,2},{1,3},{2,0},{3,1},{4,6},{5,7},{6,4},{7,5},{8,10},{9,11},{10,... | collective-permute-start | bytes 1474568 | tf_op jit(solution)/shard_map/ppermute | solution.py:27
  154.5 41.0 %collective-permute-start.16 = (bf16[512,1024]{1,0:T(8,128)(2,1)}, bf16[512,1024]{1,0:T(8,128)(2,1)}, u32[]{:S(2)}, u32[]{:S(2)}) collective-permute-start(bf16[512,1024]{1,0:T(8,128)(2,1)} %fusion.21), channel_id=1, source_target_pairs={{0,1},{1,0},{2,3},{3,2},{4,5},{5,4},{6,7},{7,6},{8,9},{9,8},{10,11... | collective-permute-start | bytes 3145736 | tf_op jit(solution)/shard_map/ppermute | solution.py:27
  156.4 33.8 %collective-permute-start.20 = (bf16[512,1408]{1,0:T(8,128)(2,1)S(1)}, bf16[512,1408]{1,0:T(8,128)(2,1)S(1)}, u32[]{:S(2)}, u32[]{:S(2)}) collective-permute-start(bf16[512,1408]{1,0:T(8,128)(2,1)S(1)} %pad_maximum_fusion.4.refs_0_.a), channel_id=1, source_target_pairs={{0,2},{1,3},{2,0},{3,1},{4,6},{5,7},{6,4},{7,5},{8,10},{9,11},{10,... | collective-permute-start | bytes 4325384 | tf_op jit(solution)/shard_map/ppermute | solution.py:27
  158.5 33.3 %collective-permute-start.19 = (bf16[512,1408]{1,0:T(8,128)(2,1)S(1)}, bf16[512,1408]{1,0:T(8,128)(2,1)}, u32[]{:S(2)}, u32[]{:S(2)}) collective-permute-start(bf16[512,1408]{1,0:T(8,128)(2,1)S(1)} %pad_maximum_fusion.4.refs_0_.a), channel_id=1, source_target_pairs={{0,4},{4,0},{8,12},{12,8},{16,20},{20,16},{24,28},{28,24},{1,5},{5... | collective-permute-start | bytes 4325384 | tf_op jit(solution)/shard_map/ppermute | solution.py:27
  167.1 31.4 %collective-permute-start.15 = (bf16[512,1024]{1,0:T(8,128)(2,1)}, bf16[512,1024]{1,0:T(8,128)(2,1)}, u32[]{:S(2)}, u32[]{:S(2)}) collective-permute-start(bf16[512,1024]{1,0:T(8,128)(2,1)} %multiply_convert_fusion), channel_id=1, source_target_pairs={{0,1},{1,0},{2,3},{3,2},{4,5},{5,4},{6,7},{7,6},{8,9},{9,8},{10,11... | collective-permute-start | bytes 3145736 | tf_op jit(solution)/shard_map/ppermute | solution.py:27
  191.2 17.9 %collective-permute-start.21 = (bf16[256,1408]{1,0:T(8,128)(2,1)}, bf16[256,1408]{1,0:T(8,128)(2,1)}, u32[]{:S(2)}, u32[]{:S(2)}) collective-permute-start(bf16[256,1408]{1,0:T(8,128)(2,1)} %slice.164), channel_id=1, source_target_pairs={{0,4},{4,0},{8,12},{12,8},{16,20},{20,16},{24,28},{28,24},{1,5},{5... | collective-permute-start | bytes 2162696 | tf_op jit(solution)/shard_map/ppermute | solution.py:27
  193.8 17.7 %collective-permute-start.22 = (bf16[256,1408]{1,0:T(8,128)(2,1)}, bf16[256,1408]{1,0:T(8,128)(2,1)}, u32[]{:S(2)}, u32[]{:S(2)}) collective-permute-start(bf16[256,1408]{1,0:T(8,128)(2,1)} %slice.165), channel_id=1, source_target_pairs={{0,2},{1,3},{2,0},{3,1},{4,6},{5,7},{6,4},{7,5},{8,10},{9,11},{10,... | collective-permute-start | bytes 2162696 | tf_op jit(solution)/shard_map/ppermute | solution.py:27
  236.6 24.1 %collective-permute-start.23 = (bf16[512,1024]{1,0:T(8,128)(2,1)}, bf16[512,1024]{1,0:T(8,128)(2,1)}, u32[]{:S(2)}, u32[]{:S(2)}) collective-permute-start(bf16[512,1024]{1,0:T(8,128)(2,1)} %shard_map.286), channel_id=1, source_target_pairs={{0,1},{1,0},{2,3},{3,2},{4,5},{5,4},{6,7},{7,6},{8,9},{9,8},{10,11... | collective-permute-start | bytes 3145736 | tf_op jit(solution)/shard_map/ppermute | solution.py:27
  249.5 39.1 %collective-permute-start.46 = (bf16[256,704]{1,0:T(8,128)(2,1)}, bf16[256,704]{1,0:T(8,128)(2,1)}, u32[]{:S(2)}, u32[]{:S(2)}) collective-permute-start(bf16[256,704]{1,0:T(8,128)(2,1)} %get-tuple-element.130), channel_id=1, source_target_pairs={{0,4},{4,0},{8,12},{12,8},{16,20},{20,16},{24,28},{28,24},{1,5},{5... | collective-permute-start | bytes 1081352 | tf_op jit(solution)/shard_map/ppermute | solution.py:27
  250.9 32.4 %collective-permute-start.48 = (bf16[256,704]{1,0:T(8,128)(2,1)}, bf16[256,704]{1,0:T(8,128)(2,1)}, u32[]{:S(2)}, u32[]{:S(2)}) collective-permute-start(bf16[256,704]{1,0:T(8,128)(2,1)} %get-tuple-element.134), channel_id=1, source_target_pairs={{0,2},{1,3},{2,0},{3,1},{4,6},{5,7},{6,4},{7,5},{8,10},{9,11},{10,... | collective-permute-start | bytes 1081352 | tf_op jit(solution)/shard_map/ppermute | solution.py:27
  252.4 38.8 %collective-permute-start.50 = (bf16[256,704]{1,0:T(8,128)(2,1)}, bf16[256,704]{1,0:T(8,128)(2,1)S(1)}, u32[]{:S(2)}, u32[]{:S(2)}) collective-permute-start(bf16[256,704]{1,0:T(8,128)(2,1)} %get-tuple-element.136), channel_id=1, source_target_pairs={{0,2},{1,3},{2,0},{3,1},{4,6},{5,7},{6,4},{7,5},{8,10},{9,11},{10,... | collective-permute-start | bytes 1081352 | tf_op jit(solution)/shard_map/ppermute | solution.py:27
  267.1 31.7 %collective-permute-start.24 = (bf16[512,1024]{1,0:T(8,128)(2,1)}, bf16[512,1024]{1,0:T(8,128)(2,1)S(1)}, u32[]{:S(2)}, u32[]{:S(2)}) collective-permute-start(bf16[512,1024]{1,0:T(8,128)(2,1)} %get-tuple-element.190), channel_id=1, source_target_pairs={{0,1},{1,0},{2,3},{3,2},{4,5},{5,4},{6,7},{7,6},{8,9},{9,8},{10,11... | collective-permute-start | bytes 3145736 | tf_op jit(solution)/shard_map/ppermute | solution.py:27
  284.5 12.0 %collective-permute-start.49 = (bf16[256,704]{1,0:T(8,128)(2,1)S(1)}, bf16[256,704]{1,0:T(8,128)(2,1)S(1)}, u32[]{:S(2)}, u32[]{:S(2)}) collective-permute-start(bf16[256,704]{1,0:T(8,128)(2,1)S(1)} %add_convert_fusion.7), channel_id=1, source_target_pairs={{0,4},{4,0},{8,12},{12,8},{16,20},{20,16},{24,28},{28,24},{1,5},{5... | collective-permute-start | bytes 1081352 | tf_op jit(solution)/shard_map/ppermute | solution.py:27
  287.3 94.3 %collective-permute-start.45 = (bf16[256,704]{1,0:T(8,128)(2,1)}, bf16[256,704]{1,0:T(8,128)(2,1)}, u32[]{:S(2)}, u32[]{:S(2)}) collective-permute-start(bf16[256,704]{1,0:T(8,128)(2,1)} %get-tuple-element.128), channel_id=1, source_target_pairs={{0,4},{4,0},{8,12},{12,8},{16,20},{20,16},{24,28},{28,24},{1,5},{5... | collective-permute-start | bytes 1081352 | tf_op jit(solution)/shard_map/ppermute | solution.py:27
  288.7 32.3 %collective-permute-start.38 = (bf16[256,1408]{1,0:T(8,128)(2,1)}, bf16[256,1408]{1,0:T(8,128)(2,1)}, u32[]{:S(2)}, u32[]{:S(2)}) collective-permute-start(bf16[256,1408]{1,0:T(8,128)(2,1)} %get-tuple-element.119), channel_id=1, source_target_pairs={{0,4},{4,0},{8,12},{12,8},{16,20},{20,16},{24,28},{28,24},{1,5},{5... | collective-permute-start | bytes 2162696 | tf_op jit(solution)/shard_map/ppermute | solution.py:27
  291.1 30.7 %collective-permute-start.40 = (bf16[256,1408]{1,0:T(8,128)(2,1)}, bf16[256,1408]{1,0:T(8,128)(2,1)}, u32[]{:S(2)}, u32[]{:S(2)}) collective-permute-start(bf16[256,1408]{1,0:T(8,128)(2,1)} %get-tuple-element.123), channel_id=1, source_target_pairs={{0,2},{1,3},{2,0},{3,1},{4,6},{5,7},{6,4},{7,5},{8,10},{9,11},{10,... | collective-permute-start | bytes 2162696 | tf_op jit(solution)/shard_map/ppermute | solution.py:27
  296.5 101.6 %collective-permute-start.42 = (bf16[256,1408]{1,0:T(8,128)(2,1)}, bf16[256,1408]{1,0:T(8,128)(2,1)}, u32[]{:S(2)}, u32[]{:S(2)}) collective-permute-start(bf16[256,1408]{1,0:T(8,128)(2,1)} %get-tuple-element.125), channel_id=1, source_target_pairs={{0,2},{1,3},{2,0},{3,1},{4,6},{5,7},{6,4},{7,5},{8,10},{9,11},{10,... | collective-permute-start | bytes 2162696 | tf_op jit(solution)/shard_map/ppermute | solution.py:27
  298.8 138.6 %collective-permute-start.37 = (bf16[256,1408]{1,0:T(8,128)(2,1)}, bf16[256,1408]{1,0:T(8,128)(2,1)}, u32[]{:S(2)}, u32[]{:S(2)}) collective-permute-start(bf16[256,1408]{1,0:T(8,128)(2,1)} %get-tuple-element.117), channel_id=1, source_target_pairs={{0,4},{4,0},{8,12},{12,8},{16,20},{20,16},{24,28},{28,24},{1,5},{5... | collective-permute-start | bytes 2162696 | tf_op jit(solution)/shard_map/ppermute | solution.py:27
  320.9 60.8 %collective-permute-start.47 = (bf16[256,704]{1,0:T(8,128)(2,1)}, bf16[256,704]{1,0:T(8,128)(2,1)}, u32[]{:S(2)}, u32[]{:S(2)}) collective-permute-start(bf16[256,704]{1,0:T(8,128)(2,1)} %add_convert_fusion.8), channel_id=1, source_target_pairs={{0,2},{1,3},{2,0},{3,1},{4,6},{5,7},{6,4},{7,5},{8,10},{9,11},{10,... | collective-permute-start | bytes 1081352 | tf_op jit(solution)/shard_map/ppermute | solution.py:27
  322.6 13.1 %collective-permute-start.25 = (bf16[2,256,128]{2,1,0:T(8,128)(2,1)}, bf16[2,256,128]{2,1,0:T(8,128)(2,1)S(1)}, u32[]{:S(2)}, u32[]{:S(2)}) collective-permute-start(bf16[2,256,128]{2,1,0:T(8,128)(2,1)} %rev.10), channel_id=1, source_target_pairs={{2,0},{3,1},{6,4},{7,5},{10,8},{11,9},{14,12},{15,13},{18,16},{19,... | collective-permute-start | bytes 393224 | tf_op jit(solution)/shard_map/ppermute | solution.py:453
  335.7 47.5 %collective-permute-start.51 = (bf16[256,704]{1,0:T(8,128)(2,1)}, bf16[256,704]{1,0:T(8,128)(2,1)S(1)}, u32[]{:S(2)}, u32[]{:S(2)}) collective-permute-start(bf16[256,704]{1,0:T(8,128)(2,1)} %convert_add_fusion.4), channel_id=1, source_target_pairs={{0,8},{4,12},{8,0},{12,4},{16,24},{20,28},{24,16},{28,20},{1,9},{5... | collective-permute-start | bytes 1081352 | tf_op jit(solution)/shard_map/ppermute | solution.py:27
  381.6 56.7 %collective-permute-start.39 = (bf16[256,1408]{1,0:T(8,128)(2,1)}, bf16[256,1408]{1,0:T(8,128)(2,1)S(1)}, u32[]{:S(2)}, u32[]{:S(2)}) collective-permute-start(bf16[256,1408]{1,0:T(8,128)(2,1)} %add_convert_fusion.2), channel_id=1, source_target_pairs={{0,2},{1,3},{2,0},{3,1},{4,6},{5,7},{6,4},{7,5},{8,10},{9,11},{10,... | collective-permute-start | bytes 2162696 | tf_op jit(solution)/shard_map/ppermute | solution.py:27
  381.7 18.3 %collective-permute-start.41 = (bf16[256,1408]{1,0:T(8,128)(2,1)}, bf16[256,1408]{1,0:T(8,128)(2,1)}, u32[]{:S(2)}, u32[]{:S(2)}) collective-permute-start(bf16[256,1408]{1,0:T(8,128)(2,1)} %add_convert_fusion.1), channel_id=1, source_target_pairs={{0,4},{4,0},{8,12},{12,8},{16,20},{20,16},{24,28},{28,24},{1,5},{5... | collective-permute-start | bytes 2162696 | tf_op jit(solution)/shard_map/ppermute | solution.py:27
  384.5 11.9 %collective-permute-start.52 = (bf16[128,704]{1,0:T(8,128)(2,1)S(1)}, bf16[128,704]{1,0:T(8,128)(2,1)S(1)}, u32[]{:S(2)}, u32[]{:S(2)}) collective-permute-start(bf16[128,704]{1,0:T(8,128)(2,1)S(1)} %slice.227), channel_id=1, source_target_pairs={{0,16},{4,20},{8,24},{12,28},{16,0},{20,4},{24,8},{28,12},{1,17},{... | collective-permute-start | bytes 540680 | tf_op jit(solution)/shard_map/ppermute | solution.py:27
  396.4 14.9 %collective-permute-start.29 = (bf16[256,1152]{1,0:T(8,128)(2,1)}, bf16[256,1152]{1,0:T(8,128)(2,1)}, u32[]{:S(2)}, u32[]{:S(2)}) collective-permute-start(bf16[256,1152]{1,0:T(8,128)(2,1)} %get-tuple-element.111), channel_id=1, source_target_pairs={{0,4},{4,0},{8,12},{12,8},{16,20},{20,16},{24,28},{28,24},{1,5},{5... | collective-permute-start | bytes 1769480 | tf_op jit(solution)/shard_map/ppermute | solution.py:27
  398.1 16.5 %collective-permute-start.31 = (bf16[256,1152]{1,0:T(8,128)(2,1)}, bf16[256,1152]{1,0:T(8,128)(2,1)S(1)}, u32[]{:S(2)}, u32[]{:S(2)}) collective-permute-start(bf16[256,1152]{1,0:T(8,128)(2,1)} %get-tuple-element.114), channel_id=1, source_target_pairs={{0,2},{1,3},{2,0},{3,1},{4,6},{5,7},{6,4},{7,5},{8,10},{9,11},{10,... | collective-permute-start | bytes 1769480 | tf_op jit(solution)/shard_map/ppermute | solution.py:27
  400.0 25.6 %collective-permute-start.33 = (bf16[256,1152]{1,0:T(8,128)(2,1)}, bf16[256,1152]{1,0:T(8,128)(2,1)S(1)}, u32[]{:S(2)}, u32[]{:S(2)}) collective-permute-start(bf16[256,1152]{1,0:T(8,128)(2,1)} %get-tuple-element.115), channel_id=1, source_target_pairs={{0,2},{1,3},{2,0},{3,1},{4,6},{5,7},{6,4},{7,5},{8,10},{9,11},{10,... | collective-permute-start | bytes 1769480 | tf_op jit(solution)/shard_map/ppermute | solution.py:27
  414.7 23.6 %collective-permute-start.43 = (bf16[256,1408]{1,0:T(8,128)(2,1)S(1)}, bf16[256,1408]{1,0:T(8,128)(2,1)S(1)}, u32[]{:S(2)}, u32[]{:S(2)}) collective-permute-start(bf16[256,1408]{1,0:T(8,128)(2,1)S(1)} %convert_add_fusion.1), channel_id=1, source_target_pairs={{0,8},{4,12},{8,0},{12,4},{16,24},{20,28},{24,16},{28,20},{1,9},{5... | collective-permute-start | bytes 2162696 | tf_op jit(solution)/shard_map/ppermute | solution.py:27
  419.0 16.2 %collective-permute-start.32 = (bf16[256,1152]{1,0:T(8,128)(2,1)S(1)}, bf16[256,1152]{1,0:T(8,128)(2,1)S(1)}, u32[]{:S(2)}, u32[]{:S(2)}) collective-permute-start(bf16[256,1152]{1,0:T(8,128)(2,1)S(1)} %add_convert_fusion.4), channel_id=1, source_target_pairs={{0,4},{4,0},{8,12},{12,8},{16,20},{20,16},{24,28},{28,24},{1,5},{5... | collective-permute-start | bytes 1769480 | tf_op jit(solution)/shard_map/ppermute | solution.py:27
  425.7 21.5 %collective-permute-start.28 = (bf16[256,1152]{1,0:T(8,128)(2,1)S(1)}, bf16[256,1152]{1,0:T(8,128)(2,1)S(1)}, u32[]{:S(2)}, u32[]{:S(2)}) collective-permute-start(bf16[256,1152]{1,0:T(8,128)(2,1)S(1)} %copy-done.82), channel_id=1, source_target_pairs={{0,4},{4,0},{8,12},{12,8},{16,20},{20,16},{24,28},{28,24},{1,5},{5... | collective-permute-start | bytes 1769480 | tf_op jit(solution)/shard_map/ppermute | solution.py:27
  435.3 14.1 %collective-permute-start.30 = (bf16[256,1152]{1,0:T(8,128)(2,1)S(1)}, bf16[256,1152]{1,0:T(8,128)(2,1)S(1)}, u32[]{:S(2)}, u32[]{:S(2)}) collective-permute-start(bf16[256,1152]{1,0:T(8,128)(2,1)S(1)} %add_convert_fusion.5), channel_id=1, source_target_pairs={{0,2},{1,3},{2,0},{3,1},{4,6},{5,7},{6,4},{7,5},{8,10},{9,11},{10,... | collective-permute-start | bytes 1769480 | tf_op jit(solution)/shard_map/ppermute | solution.py:27
  437.5 21.4 %collective-permute-start.34 = (bf16[256,1152]{1,0:T(8,128)(2,1)S(1)}, bf16[256,1152]{1,0:T(8,128)(2,1)S(1)}, u32[]{:S(2)}, u32[]{:S(2)}) collective-permute-start(bf16[256,1152]{1,0:T(8,128)(2,1)S(1)} %add_convert_fusion.3), channel_id=1, source_target_pairs={{0,8},{4,12},{8,0},{12,4},{16,24},{20,28},{24,16},{28,20},{1,9},{5... | collective-permute-start | bytes 1769480 | tf_op jit(solution)/shard_map/ppermute | solution.py:27
  439.9 20.6 %collective-permute-start.44 = (bf16[128,1408]{1,0:T(8,128)(2,1)S(1)}, bf16[128,1408]{1,0:T(8,128)(2,1)S(1)}, u32[]{:S(2)}, u32[]{:S(2)}) collective-permute-start(bf16[128,1408]{1,0:T(8,128)(2,1)S(1)} %slice.225), channel_id=1, source_target_pairs={{0,16},{4,20},{8,24},{12,28},{16,0},{20,4},{24,8},{28,12},{1,17},{... | collective-permute-start | bytes 1081352 | tf_op jit(solution)/shard_map/ppermute | solution.py:27
  459.2 14.2 %collective-permute-start.35 = (bf16[128,1152]{1,0:T(8,128)(2,1)S(1)}, bf16[128,1152]{1,0:T(8,128)(2,1)}, u32[]{:S(2)}, u32[]{:S(2)}) collective-permute-start(bf16[128,1152]{1,0:T(8,128)(2,1)S(1)} %slice.226), channel_id=1, source_target_pairs={{0,16},{4,20},{8,24},{12,28},{16,0},{20,4},{24,8},{28,12},{1,17},{... | collective-permute-start | bytes 884744 | tf_op jit(solution)/shard_map/ppermute | solution.py:27
  (88 other events, 722.0 us)
